TPU v7x, 128 devices: a whole 4x4x4 slice. The times are simulated.
128 devices in a mesh: pipe: 4 (over x), ctx: 32 (over z, y, core).
Axes of the slice: x: 4, y: 4, z: 4, core: 2. Of those that a mesh axis runs over, the one named last changes fastest.
Arguments:
- incoming: bfloat16 [4, 8192, 8192], P('pipe', 'ctx'), may hold values from -6 to 6
- norm_gain: float32 [4, 8192], P('pipe'), may hold values from 0.5 to 1.5
- proj_state: bfloat16 [4, 8192, 256], P('pipe'), may hold values from -0.015625 to 0.015625
- proj_step: bfloat16 [4, 8192, 128], P('pipe'), may hold values from -0.0625 to 0.0625
- conv_weight: float32 [4, 4, 8192], P('pipe'), may hold values from -3 to 3
- decay_rate: float32 [4, 128], P('pipe'), may hold values from 2.4414063e-05 to 0.05
- step_bias: float32 [4, 128], P('pipe'), may hold values from -2 to 1
- skip_gain: float32 [4, 128], P('pipe'), may hold values from 0.5 to 2
- out_gain: float32 [4, 8192], P('pipe'), may hold values from 0.5 to 1.5
Outputs:
- passed: bfloat16 [4, 8192, 8192], P('pipe', 'ctx')
All inputs are finite; a program needn't handle non-finite values.
Results may differ from a plain program's by a relative error of at most 0.0071.
Values may be sent and summed in bfloat16 or wider, within the bound.
A program may use at most 320 MiB of HBM per device.

v0:
```python
import jax
import jax.numpy as jnp
from jax import lax
from jax.sharding import PartitionSpec as P

GROUP = 256
CONV = 4


epsilon = 1e-05
highest = lax.Precision.HIGHEST


def from_behind(array, axis, by):
    peers = lax.axis_size(axis)
    pairs = [(i, i + by) for i in range(peers) if 0 <= i + by < peers]
    return lax.ppermute(array, axis, pairs)


def entering(part, axis, combine, identity):
    place = lax.axis_index(axis)
    gathered = jax.tree.map(lambda a: lax.all_gather(a, axis), part)
    state = jax.tree.map(lambda a, e: jnp.zeros_like(a) + jnp.asarray(e, a.dtype), part, identity)

    def one(step, state):
        return combine(
            state, jax.tree.map(lambda a: lax.dynamic_index_in_dim(a, step, 0, False), gathered)
        )

    return lax.fori_loop(0, place, one, state)


def from_behind_2(array, axis, by):
    peers = lax.axis_size(axis)
    return lax.ppermute(array, axis, [(i, (i + by) % peers) for i in range(peers)])


def normalize(values_in, gain_row):
    values = values_in.astype(jnp.float32)
    meansq = jnp.mean(values * values, axis=-1, keepdims=True)
    return (values * lax.rsqrt(meansq + epsilon) * gain_row).astype(jnp.bfloat16)


def combine_states(earlier, later):
    return (earlier[0] * later[0], later[0][:, None, None] * earlier[1] + later[1])


def state_read(read_k, cumulative, state_now):
    product = jnp.einsum("tn,hpn->thp", read_k.astype(jnp.float32), state_now, precision=highest)
    return jnp.exp(cumulative)[:, :, None] * product


def shards(
    incoming,
    norm_gain,
    proj_state,
    proj_step,
    conv_weight,
    decay_rate,
    step_bias,
    skip_gain,
    out_gain,
):
    stream = incoming[0]
    tokens_here, features = stream.shape
    head_count = proj_step.shape[2]
    state_size = proj_state.shape[2] // 2
    head_size = features // head_count
    normed = normalize(stream, norm_gain[0])
    projected = jnp.dot(normed, proj_state[0], preferred_element_type=jnp.float32)
    write_proj = projected[:, :state_size].astype(jnp.bfloat16)
    read_proj = projected[:, state_size:].astype(jnp.bfloat16)
    step_size = jax.nn.softplus(
        jnp.dot(normed, proj_step[0], preferred_element_type=jnp.float32) + step_bias[0]
    )
    edge_rows = from_behind(normed[tokens_here - (CONV - 1) :], "ctx", 1)
    padded = jnp.concatenate([edge_rows, normed], axis=0).astype(jnp.float32)
    conv_taps = conv_weight[0]
    conv_sum = conv_taps[0] * padded[0:tokens_here]
    for tap_id in range(1, CONV):
        conv_sum = conv_sum + conv_taps[tap_id] * padded[tap_id : tap_id + tokens_here]
    inner_act = (
        jax.nn.silu(conv_sum).astype(jnp.bfloat16).reshape(tokens_here, head_count, head_size)
    )
    log_decay = -step_size * decay_rate[0]
    skip_row = skip_gain[0]
    out_row = out_gain[0]
    lower_mask = (jnp.arange(GROUP)[:, None] >= jnp.arange(GROUP)[None, :]).astype(jnp.float32)
    state_now = jnp.zeros((head_count, head_size, state_size), jnp.float32)
    prior_sum = jnp.zeros((head_count,), jnp.float32)
    cumulative = jnp.dot(lower_mask, log_decay, precision=highest)
    scores = jnp.dot(read_proj, write_proj.T, preferred_element_type=jnp.float32)
    cumul_heads = cumulative.T
    spread = cumul_heads[:, :, None] - cumul_heads[:, None, :]
    damping = jnp.exp(jnp.where(lower_mask[None] > 0, spread, -1e30))
    mixing = (scores[None] * damping * step_size.T[:, None, :]).astype(jnp.bfloat16)
    within = jnp.einsum("hts,shp->thp", mixing, inner_act, preferred_element_type=jnp.float32)
    within = within + skip_row[None, :, None] * inner_act.astype(jnp.float32)
    closing = cumulative[GROUP - 1]
    weights = jnp.exp(closing[None, :] - cumulative) * step_size
    weighted = (inner_act.astype(jnp.float32) * weights[:, :, None]).astype(jnp.bfloat16)
    fresh_state = jnp.einsum(
        "shp,sn->hpn", weighted, write_proj, preferred_element_type=jnp.float32
    )
    start_list = state_now
    state_now = jnp.exp(closing)[:, None, None] * state_now + fresh_state
    identity = (
        jnp.ones((head_count,), jnp.float32),
        jnp.zeros((head_count, head_size, state_size), jnp.float32),
    )
    carried_decay, carried = entering(
        (jnp.exp(closing), state_now), "ctx", combine_states, identity
    )
    block_start = jnp.exp(prior_sum)[:, None, None] * carried + start_list
    output = within + state_read(read_proj, cumulative, block_start)
    meansq = jnp.mean(output * output, axis=-1, keepdims=True)
    normed_out = (output * lax.rsqrt(meansq + epsilon)).reshape(GROUP, features)
    stream_k = stream.astype(jnp.float32)
    rows_out = (stream_k + normed_out * out_row).astype(jnp.bfloat16)
    passed = from_behind_2(rows_out, "pipe", 1)
    return passed[None]


def solution(mesh):
    return jax.shard_map(
        shards,
        mesh=mesh,
        in_specs=(
            P("pipe", "ctx", None),
            P("pipe", None),
            P("pipe", None, None),
            P("pipe", None, None),
            P("pipe", None, None),
            P("pipe", None),
            P("pipe", None),
            P("pipe", None),
            P("pipe", None),
        ),
        out_specs=P("pipe", "ctx", None),
        check_vma=False,
    )
```

profile of v0, /device:TPU:121, one launch (start us, length us, event | category | flops | bytes accessed | tf_op | source)
XLA Modules:
  0.0 860.3 jit_solution(17276851504912533203)
XLA Ops:
  46.0 20.9 %all-gather.1 = f32[32,1,128]{2,1,0:T(1,128)S(1)} all-gather(f32[1,1,128]{2,1,0:T(1,128)S(1)} %get-tuple-element.73), channel_id=1, replica_groups=mesh['pipe'=4,'ctx'=32] {'ctx'}, dimensions={0}, use_global_device_ids=true | all-gather | bytes 16896 | tf_op jit(solution)/shard_map/all_gather | solution.py:22
  67.1 355.4 %all-gather.4.cloned.1.call-done = f32[4096,64,128]{2,0,1:T(8,128)} async-done(((f32[128,64,128]{2,0,1:T(8,128)}), f32[4096,64,128]{2,0,1:T(8,128)}) %all-gather.4.cloned.1.call-update) | async-done | bytes 134217744 | tf_op jit(solution)/shard_map/all_gather | solution.py:22
  425.1 305.7 %while.12 = (s32[]{:T(128)}, f32[128,64,128]{2,1,0:T(8,128)}, s32[]{:T(128)}, f32[32,128]{1,0:T(8,128)S(1)}, f32[32,128,64,128]{3,1,0,2:T(8,128)}, /*index=5*/s32[]{:T(128)}, s32[]{:T(128)}, s32[]{:T(128)}) while((s32[]{:T(128)}, f32[128,64,128]{2,1,0:T(8,128)}, s32[]{:T(128)}, f32[32,128]{1,0:T(8,128)S(1)}, f32[32,128,64,128]{3,1,0,2:T(8,128)}, ...), condition=%wide.region_2.3_spmd, body=%wide.region_1.2_spmd.sunk | while | flops 2097157 | bytes 20973184 | solution.py:30
  427.9 7.1 fusion.69
  437.8 7.1 fusion.69
  447.6 7.1 fusion.69
  457.5 7.1 fusion.69
  467.3 7.1 fusion.69
  477.2 7.1 fusion.69
  487.0 7.1 fusion.69
  496.9 7.1 fusion.69
  506.7 7.1 fusion.69
  516.5 7.1 fusion.69
  526.4 7.1 fusion.69
  536.4 7.1 fusion.69
  546.2 7.1 fusion.69
  556.1 7.1 fusion.69
  565.9 7.1 fusion.69
  575.8 7.1 fusion.69
  585.6 7.1 fusion.69
  595.4 7.1 fusion.69
  605.3 7.1 fusion.69
  615.1 7.1 fusion.69
  625.0 7.1 fusion.69
  634.8 7.1 fusion.69
  644.8 7.1 fusion.69
  654.7 7.1 fusion.69
  664.5 7.1 fusion.69
  674.3 7.1 fusion.69
  737.0 10.4 %multiply_reduce_fusion = (f32[256,128]{0,1:T(8,128)S(1)}, f32[256,128,64]{0,2,1:T(8,128)S(1)}) fusion(f32[256,128,64]{0,2,1:T(8,128)S(1)} %fusion.53, f32[256,128]{0,1:T(8,128)S(1)} %copy.25, bf16[256,128,64]{0,2,1:T(8,128)(2,1)S(1)} %bitcast.97, f32[128]{0:T(128)S(1)} %bitcast.111, f32[128,256]{1,0:T(8,128)S(1)} %copy.24, f32[128,256]{1,0:T(8,128)S(1)} %copy.22, ...), kind=kOutput, calls=%fused_computation.35 | convolution fusion | flops 1130332160 | bytes 21824000 | tf_op jit(solution)/shard_map/hts,shp->thp/dot_general | solution.py:97
  752.0 9.0 %copy.31 = f32[256,8192]{1,0:T(8,128)} copy(f32[256,8192]{0,1:T(8,128)} %bitcast.96) | data formatting | bytes 16777216 | tf_op jit(solution)/shard_map/reshape | solution.py:117
  768.3 83.2 %collective-permute-done.1 = bf16[256,8192]{1,0:T(8,128)(2,1)S(1)} collective-permute-done((bf16[256,8192]{1,0:T(8,128)(2,1)S(1)}, bf16[256,8192]{1,0:T(8,128)(2,1)S(1)}, u32[]{:S(2)}, u32[]{:S(2)}) %collective-permute-start.1) | collective-permute-done | bytes 4194336 | tf_op jit(solution)/shard_map/ppermute | solution.py:35
  (124 shorter events, 181.7 us)
Async XLA Ops:
  6.5 8.5 copy-start
  6.5 8.5 copy-start.6
  6.5 8.5 copy-start.9
  6.5 416.0 %all-gather.4.cloned.1.call-start = ((), (), s32[]{:S(2)}) async-start(), calls=%async_computation | async-start | bytes 138412032 | tf_op jit(solution)/shard_map/all_gather | solution.py:22
  6.5 8.5 copy-start.2
  9.8 6.7 copy-start.10
  9.8 7.2 copy-start.5
  9.8 7.3 copy-start.8
  13.6 4.9 copy-start.3
  13.7 5.0 collective-permute-start
  730.8 6.2 copy-start.4
  730.8 6.2 copy-start.11
  752.0 9.0 %copy-start.7 = (f32[1,8192]{1,0:T(1,128)S(1)}, f32[1,8192]{1,0:T(1,128)}, u32[]{:S(2)}) copy-start(f32[1,8192]{1,0:T(1,128)} %param.19) | copy-start | bytes 98308
  761.0 92.5 %copy-start.1 = (bf16[1,8192,128]{2,1,0:T(8,128)(2,1)S(1)}, bf16[1,8192,128]{2,1,0:T(8,128)(2,1)}, u32[]{:S(2)}) copy-start(bf16[1,8192,128]{2,1,0:T(8,128)(2,1)} %param.14) | copy-start | bytes 6291460
  767.0 84.4 %collective-permute-start.1 = (bf16[256,8192]{1,0:T(8,128)(2,1)S(1)}, bf16[256,8192]{1,0:T(8,128)(2,1)S(1)}, u32[]{:S(2)}, u32[]{:S(2)}) collective-permute-start(bf16[256,8192]{1,0:T(8,128)(2,1)S(1)} %fusion.17), channel_id=1, source_target_pairs={{0,32},{32,64},{64,96},{96,0},{1,33},{33,65},{65,97},{97,1},{2,34}... | collective-permute-start | bytes 12582920 | tf_op jit(solution)/shard_map/ppermute | solution.py:35
Sparse Core Ops, SparseCore 0:
  45.8 376.6 all-gather.3
where the time goes:
time: 863 us; the launch traced here: 860 us
  waiting for transfers between devices  439 us (51%)
  other arithmetic  253 us (29%)
  local copies, waits for them, and re-layouts  104 us (12%)
  matrix products  26.9 us (3%)
  blocking collectives  20.9 us (2%)
  between operations  13.7 us (2%)
    all_gather x1, waiting for transfers between devices, entering(): gathered = jax.tree.map(lambda a: lax.all_gather(a, axis), part)  355 us
    add x31, other arithmetic, combine_states(): later[0][:, None, None] * earlier[1] + later[1]  221 us
    dynamic_slice x31, local copies, waits for them, and re-layouts, one(): lax.dynamic_index_in_dim(a, step, 0, False)  83.6 us
    ppermute x1, waiting for transfers between devices, from_behind_2(): lax.ppermute(array, axis, [(i, (i + by) % peers) for i in range(peers)])  83.2 us
    all_gather x1, blocking collectives, entering(): gathered = jax.tree.map(lambda a: lax.all_gather(a, axis), part)  20.9 us
  transfers between devices with their start and end apart: 3, of which 2 were waited for; matrix products, arithmetic and copies ran while one was open for 0% of the time, Pallas kernels for 0%

commit v1 on v0

v1 whole, which is shorter than its diff:
```python
import functools

import jax
import jax.numpy as jnp
from jax import lax
from jax.experimental import pallas as pl
from jax.experimental.pallas import tpu as pltpu
from jax.sharding import PartitionSpec as P

MESH = pl.DeviceIdType.MESH
F32 = jnp.float32
BF16 = jnp.bfloat16

ROWS = 256
STATE = 128
HEADS = 128
HEAD = 64
CONV = 4
HALO = 8
TILE = 512
CHIPS = 16
LOG2E = 1.4426950408889634
epsilon = 1e-05
VMEM_LIMIT = 56 * 1024 * 1024

HEADS_HOME = 64
HEADS_AWAY = HEADS - HEADS_HOME


def dot(a, b):
    return jnp.dot(a, b, preferred_element_type=F32)


def two_parts(x):
    high = x.astype(BF16)
    low = (x - high.astype(F32)).astype(BF16)
    return jnp.concatenate([high, low], axis=-1)


def spreader(first_head, width):
    head = lax.broadcasted_iota(jnp.int32, (HEADS, width), 0)
    feature = lax.broadcasted_iota(jnp.int32, (HEADS, width), 1)
    one = (head == first_head + feature // HEAD).astype(F32).astype(BF16)
    return jnp.concatenate([one, one], axis=0)


def project_kernel(x_ref, ws_ref, wt_ref, gain_ref, bias_ref, write_ref, read_ref, step_ref, scale_ref, acc):
    at = pl.program_id(0)
    width = ws_ref.shape[0]

    @pl.when(at == 0)
    def _():
        total = jnp.zeros((ROWS, 128), F32)
        for i in range(x_ref.shape[1] // 512):
            part = x_ref[:, i * 512 : (i + 1) * 512].astype(F32)
            part = part * part
            total = total + (part[:, :128] + part[:, 128:256]) + (part[:, 256:384] + part[:, 384:])
        meansq = jnp.sum(total, axis=-1, keepdims=True) * (1.0 / x_ref.shape[1])
        scale_ref[...] = jnp.broadcast_to(lax.rsqrt(meansq + epsilon), (ROWS, 128))
        acc[...] = jnp.zeros_like(acc)

    columns = pl.ds(pl.multiple_of(at * width, width), width)
    scale = scale_ref[:, :1]
    normed = (x_ref[:, columns].astype(F32) * scale * gain_ref[...]).astype(BF16)
    acc[:, : 2 * STATE] += dot(normed, ws_ref[...])
    acc[:, 2 * STATE :] += dot(normed, wt_ref[...])

    @pl.when(at == pl.num_programs(0) - 1)
    def _():
        write_ref[...] = acc[:, :STATE].astype(BF16)
        read_ref[...] = acc[:, STATE : 2 * STATE].astype(BF16)
        step_ref[...] = jax.nn.softplus(acc[:, 2 * STATE :] + bias_ref[...])


def project(x, proj_state, proj_step, gain, bias):
    features = x.shape[1]
    width = 1024
    return pl.pallas_call(
        project_kernel,
        grid=(features // width,),
        in_specs=[
            pl.BlockSpec((ROWS, features), lambda i: (0, 0)),
            pl.BlockSpec((width, 2 * STATE), lambda i: (i, 0)),
            pl.BlockSpec((width, HEADS), lambda i: (i, 0)),
            pl.BlockSpec((1, width), lambda i: (0, i)),
            pl.BlockSpec((1, HEADS), lambda i: (0, 0)),
        ],
        out_specs=[
            pl.BlockSpec((ROWS, STATE), lambda i: (0, 0)),
            pl.BlockSpec((ROWS, STATE), lambda i: (0, 0)),
            pl.BlockSpec((ROWS, HEADS), lambda i: (0, 0)),
            pl.BlockSpec((ROWS, 128), lambda i: (0, 0)),
        ],
        out_shape=[
            jax.ShapeDtypeStruct((ROWS, STATE), BF16),
            jax.ShapeDtypeStruct((ROWS, STATE), BF16),
            jax.ShapeDtypeStruct((ROWS, HEADS), F32),
            jax.ShapeDtypeStruct((ROWS, 128), F32),
        ],
        scratch_shapes=[pltpu.VMEM((ROWS, 3 * STATE), F32)],
        compiler_params=pltpu.CompilerParams(
            dimension_semantics=("arbitrary",), vmem_limit_bytes=VMEM_LIMIT
        ),
        cost_estimate=pl.CostEstimate(
            flops=2 * ROWS * features * 3 * STATE, bytes_accessed=12 << 20, transcendentals=0
        ),
        name="project",
    )(x, proj_state, proj_step, gain, bias)


def decay_kernel(step_ref, rate_ref, cum_ref, closing_ref, weight_ref, enter_ref, step2_ref):
    step = step_ref[...]
    log_decay = -step * rate_ref[...]
    row = lax.broadcasted_iota(jnp.int32, (ROWS, ROWS), 0)
    column = lax.broadcasted_iota(jnp.int32, (ROWS, ROWS), 1)
    lower = (row >= column).astype(F32).astype(BF16)
    first = log_decay.astype(BF16)
    rest = log_decay - first.astype(F32)
    second = rest.astype(BF16)
    third = (rest - second.astype(F32)).astype(BF16)
    cumulative = dot(lower, third) + dot(lower, second) + dot(lower, first)
    closing = cumulative[ROWS - 1 :, :]
    cum_ref[...] = (cumulative * LOG2E).T
    closing_ref[...] = jnp.broadcast_to(closing, (8, HEADS))
    weight_ref[...] = two_parts(jnp.exp(closing - cumulative) * step)
    enter_ref[...] = two_parts(jnp.exp(cumulative))
    step2_ref[...] = two_parts(step)


def decays(step, rate):
    pair = jax.ShapeDtypeStruct((ROWS, 2 * HEADS), BF16)
    return pl.pallas_call(
        decay_kernel,
        out_shape=[
            jax.ShapeDtypeStruct((HEADS, ROWS), F32),
            jax.ShapeDtypeStruct((8, HEADS), F32),
            pair,
            pair,
            pair,
        ],
        compiler_params=pltpu.CompilerParams(vmem_limit_bytes=VMEM_LIMIT),
        cost_estimate=pl.CostEstimate(flops=1 << 26, bytes_accessed=1 << 20, transcendentals=1 << 17),
        name="decays",
    )(step, rate)


def fresh_kernel(first, x_ref, halo_ref, vec_ref, scale_ref, weight_ref, write_ref, inner_ref, fresh_ref, padded):
    at = pl.program_id(0)
    normed = (x_ref[...].astype(F32) * scale_ref[:, :1] * vec_ref[4:5, :]).astype(BF16)
    padded[HALO:, :] = normed.astype(F32)
    padded[:HALO, :] = halo_ref[...].astype(F32)
    conv = vec_ref[0:1, :] * padded[HALO - 3 : HALO - 3 + ROWS, :]
    for tap in range(1, CONV):
        conv = conv + vec_ref[tap : tap + 1, :] * padded[HALO - 3 + tap : HALO - 3 + tap + ROWS, :]
    inner = (conv * jax.nn.sigmoid(conv)).astype(BF16)
    inner_ref[...] = inner
    spread = spreader(first + at * (TILE // HEAD), TILE)
    weighted = (inner.astype(F32) * dot(weight_ref[...], spread)).astype(BF16)
    fresh_ref[...] = lax.dot_general(
        write_ref[...], weighted, (((0,), (0,)), ((), ())), preferred_element_type=F32
    ).astype(BF16)


def fresh_states(first, x, halo, vec, scale, weight, write):
    heads = vec.shape[1] // HEAD
    features = heads * HEAD
    return pl.pallas_call(
        functools.partial(fresh_kernel, first),
        grid=(features // TILE,),
        in_specs=[
            pl.BlockSpec((ROWS, TILE), lambda i: (0, i)),
            pl.BlockSpec((HALO, TILE), lambda i: (0, i)),
            pl.BlockSpec((vec.shape[0], TILE), lambda i: (0, i)),
            pl.BlockSpec((ROWS, 128), lambda i: (0, 0)),
            pl.BlockSpec((ROWS, 2 * HEADS), lambda i: (0, 0)),
            pl.BlockSpec((ROWS, STATE), lambda i: (0, 0)),
        ],
        out_specs=[
            pl.BlockSpec((ROWS, TILE), lambda i: (0, i)),
            pl.BlockSpec((STATE, TILE), lambda i: (0, i)),
        ],
        out_shape=[
            jax.ShapeDtypeStruct((ROWS, features), BF16),
            jax.ShapeDtypeStruct((STATE, features), BF16),
        ],
        scratch_shapes=[pltpu.VMEM((ROWS + HALO, TILE), F32)],
        compiler_params=pltpu.CompilerParams(
            dimension_semantics=("arbitrary",), vmem_limit_bytes=VMEM_LIMIT
        ),
        cost_estimate=pl.CostEstimate(
            flops=40 * ROWS * features, bytes_accessed=10 * ROWS * features, transcendentals=ROWS * features
        ),
        name="fresh",
    )(x, halo, vec, scale, weight, write)


def prefix_kernel(
    first,
    fresh_ref,
    closing_ref,
    out_ref,
    peer,
    peer_closing,
    total,
    total_closing,
    got,
    got_closing,
    before,
    entering,
    theirs,
    landed,
    pair_send,
    pair_recv,
    send1,
    recv1,
    send2,
    recv2,
    send3,
    recv3,
):
    features = fresh_ref.shape[1]
    half, quarter = features // 2, features // 4
    heads = features // HEAD
    me = lax.axis_index("ctx")
    core = lax.rem(me, 2)
    chip = me // 2
    partner = chip * 2 + (1 - core)

    def device(index):
        return {"ctx": index}

    def place(of):
        return (
            pl.ds(pl.multiple_of(lax.rem(of, 8) * 16, 16), 16),
            pl.ds(pl.multiple_of((of // 8) * quarter, 128), quarter),
        )

    barrier = pltpu.get_barrier_semaphore()
    pl.semaphore_signal(barrier, inc=1, device_id=device(partner), device_id_type=MESH)

    def greet(d, carry):
        other = lax.rem(chip + d, CHIPS) * 2 + core
        pl.semaphore_signal(barrier, inc=1, device_id=device(other), device_id_type=MESH)
        return carry

    lax.fori_loop(1, CHIPS, greet, 0)
    pl.semaphore_wait(barrier, CHIPS)

    mine_columns = pl.ds(pl.multiple_of(core * half, 128), half)
    other_columns = pl.ds(pl.multiple_of((1 - core) * half, 128), half)

    to_pair = pltpu.make_async_remote_copy(
        fresh_ref.at[:, other_columns], peer, pair_send.at[0], pair_recv.at[0], device(partner), MESH
    )
    to_pair_closing = pltpu.make_async_remote_copy(
        closing_ref, peer_closing, pair_send.at[1], pair_recv.at[1], device(partner), MESH
    )
    to_pair.start()
    to_pair_closing.start()
    to_pair.wait()
    to_pair_closing.wait()
    is_first = core == 0
    own = fresh_ref[:, mine_columns].astype(F32)
    other = peer[...].astype(F32)
    state0 = jnp.where(is_first, own, other)
    state1 = jnp.where(is_first, other, own)
    closing0 = jnp.where(is_first, closing_ref[...], peer_closing[...])
    closing1 = jnp.where(is_first, peer_closing[...], closing_ref[...])
    spread = spreader(first + core * (heads // 2), half)
    decay0 = dot(two_parts(jnp.exp(closing0)), spread)[0:1, :]
    decay1 = dot(two_parts(jnp.exp(closing1)), spread)[0:1, :]
    total[...] = (decay1 * state0 + state1).astype(BF16)
    total_closing[...] = closing0 + closing1

    def out1(d):
        to = lax.rem(chip + d, CHIPS)
        rows, columns = place(to)
        return pltpu.make_async_remote_copy(
            total.at[rows, columns], got.at[chip], send1.at[to], recv1.at[chip], device(to * 2 + core), MESH
        )

    def out2(d):
        to = lax.rem(chip + d, CHIPS)
        return pltpu.make_async_remote_copy(
            total_closing, got_closing.at[chip], send2.at[to], recv2.at[chip], device(to * 2 + core), MESH
        )

    def in1(d):
        of = lax.rem(chip + d, CHIPS)
        rows, columns = place(of)
        return pltpu.make_async_remote_copy(
            total.at[rows, columns], got.at[of], send1.at[of], recv1.at[of], device(of * 2 + core), MESH
        )

    def in2(d):
        of = lax.rem(chip + d, CHIPS)
        return pltpu.make_async_remote_copy(
            total_closing, got_closing.at[of], send2.at[of], recv2.at[of], device(of * 2 + core), MESH
        )

    def start12(d, carry):
        out2(d).start()
        out1(d).start()
        return carry

    def wait12(d, carry):
        in2(d).wait_recv()
        in1(d).wait_recv()
        out2(d).wait_send()
        out1(d).wait_send()
        return carry

    lax.fori_loop(1, CHIPS, start12, 0)
    rows, columns = place(chip)
    got[chip] = total[rows, columns]
    got_closing[chip] = total_closing[...]
    lax.fori_loop(1, CHIPS, wait12, 0)

    spread = spreader(first + core * (heads // 2) + (chip // 8) * (heads // 4), quarter)
    decays_all = dot(two_parts(jnp.exp(got_closing[:, 0, :])), spread)
    state = jnp.zeros((16, quarter), F32)
    for k in range(CHIPS):
        before[k] = state.astype(BF16)
        if k < CHIPS - 1:
            state = decays_all[k : k + 1, :] * state + got[k].astype(F32)

    def out3(d):
        to = lax.rem(chip + d, CHIPS)
        rows, columns = place(chip)
        return pltpu.make_async_remote_copy(
            before.at[to], entering.at[rows, columns], send3.at[to], recv3.at[chip], device(to * 2 + core), MESH
        )

    def in3(d):
        of = lax.rem(chip + d, CHIPS)
        rows, columns = place(of)
        return pltpu.make_async_remote_copy(
            before.at[of], entering.at[rows, columns], send3.at[of], recv3.at[of], device(of * 2 + core), MESH
        )

    def start3(d, carry):
        out3(d).start()
        return carry

    def wait3(d, carry):
        in3(d).wait_recv()
        out3(d).wait_send()
        return carry

    lax.fori_loop(1, CHIPS, start3, 0)
    entering[rows, columns] = before[chip]
    lax.fori_loop(1, CHIPS, wait3, 0)

    for_first = entering[...]
    for_second = (decay0 * for_first.astype(F32) + state0).astype(BF16)
    theirs[...] = jnp.where(is_first, for_second, for_first)
    back = pltpu.make_async_remote_copy(
        theirs, landed, pair_send.at[2], pair_recv.at[2], device(partner), MESH
    )
    back.start()
    out_ref[:, mine_columns] = jnp.where(is_first, for_first, for_second)
    back.wait()
    out_ref[:, other_columns] = landed[...]


def prefix(first, fresh, closing, collective_id):
    features = fresh.shape[1]
    half, quarter = features // 2, features // 4
    dma = pltpu.SemaphoreType.DMA
    return pl.pallas_call(
        functools.partial(prefix_kernel, first),
        out_shape=jax.ShapeDtypeStruct((STATE, features), BF16),
        in_specs=[pl.BlockSpec(memory_space=pltpu.VMEM)] * 2,
        out_specs=pl.BlockSpec(memory_space=pltpu.VMEM),
        scratch_shapes=[
            pltpu.VMEM((STATE, half), BF16),
            pltpu.VMEM((8, HEADS), F32),
            pltpu.VMEM((STATE, half), BF16),
            pltpu.VMEM((8, HEADS), F32),
            pltpu.VMEM((CHIPS, 16, quarter), BF16),
            pltpu.VMEM((CHIPS, 8, HEADS), F32),
            pltpu.VMEM((CHIPS, 16, quarter), BF16),
            pltpu.VMEM((STATE, half), BF16),
            pltpu.VMEM((STATE, half), BF16),
            pltpu.VMEM((STATE, half), BF16),
            dma((3,)),
            dma((3,)),
            dma((CHIPS,)),
            dma((CHIPS,)),
            dma((CHIPS,)),
            dma((CHIPS,)),
            dma((CHIPS,)),
            dma((CHIPS,)),
        ],
        compiler_params=pltpu.CompilerParams(
            collective_id=collective_id, has_side_effects=True, vmem_limit_bytes=VMEM_LIMIT
        ),
        cost_estimate=pl.CostEstimate(
            flops=STATE * features * 1000, bytes_accessed=STATE * features * 50, transcendentals=0
        ),
        name="prefix",
    )(fresh, closing)


def output_kernel(
    first,
    x_ref,
    inner_ref,
    state_ref,
    vec_ref,
    skip_ref,
    write_ref,
    read_ref,
    cum_ref,
    enter_ref,
    step2_ref,
    out_ref,
    scores,
):
    at = pl.program_id(0)

    @pl.when(at == 0)
    def _():
        row = lax.broadcasted_iota(jnp.int32, (ROWS, ROWS), 0)
        column = lax.broadcasted_iota(jnp.int32, (ROWS, ROWS), 1)
        product = lax.dot_general(
            read_ref[...], write_ref[...], (((1,), (1,)), ((), ())), preferred_element_type=F32
        )
        scores[...] = jnp.where(row >= column, product, 0.0)

    spread = spreader(first + at * (TILE // HEAD), TILE)
    inner = inner_ref[...].astype(F32)
    stepped = (inner * dot(step2_ref[...], spread)).astype(BF16)
    cum = cum_ref[...]
    cum_columns = cum.T
    top, bottom = scores[:128, :128], scores[128:, :]
    lane = lax.broadcasted_iota(jnp.int32, (ROWS, 128), 1)
    pieces = []
    for pair in range(TILE // 128):
        values = stepped[:, pair * 128 : (pair + 1) * 128]
        upper = lower = None
        for side in range(2):
            h = pair * 2 + side
            column = cum_columns[:, h : h + 1]
            row = cum[h : h + 1, :]
            own = jnp.where((lane >= HEAD) == (side == 1), values, jnp.zeros_like(values))
            mix0 = (jnp.exp2(jnp.minimum(column[:128] - row[:, :128], 0.0)) * top).astype(BF16)
            mix1 = (jnp.exp2(jnp.minimum(column[128:] - row, 0.0)) * bottom).astype(BF16)
            up, low = dot(mix0, own[:128]), dot(mix1, own)
            upper = up if upper is None else upper + up
            lower = low if lower is None else lower + low
        pieces.append(jnp.concatenate([upper, lower], axis=0))
    within = jnp.concatenate(pieces, axis=1)
    carried = dot(read_ref[...], state_ref[...]) * dot(enter_ref[...], spread)
    skip = dot(two_parts(jnp.broadcast_to(skip_ref[...], (8, HEADS))), spread)[0:1, :]
    output = within + carried + skip * inner
    square = (output * output).astype(BF16)
    a = lax.broadcasted_iota(jnp.int32, (256, 256), 0) // HEAD
    b = lax.broadcasted_iota(jnp.int32, (256, 256), 1) // HEAD
    group = (a == b).astype(F32).astype(BF16)
    sums = jnp.concatenate(
        [dot(square[:, i * 256 : (i + 1) * 256], group) for i in range(TILE // 256)], axis=1
    )
    normed = output * lax.rsqrt(sums * (1.0 / HEAD) + epsilon)
    out_ref[...] = (x_ref[...].astype(F32) + normed * vec_ref[5:6, :]).astype(BF16)


def outputs(first, x, inner, state, vec, skip, write, read, cum, enter, step2, place=0, width=None):
    features = inner.shape[1]
    width = features if width is None else width
    base = first * HEAD // TILE
    whole = lambda i: (0, 0)
    return pl.pallas_call(
        functools.partial(output_kernel, first),
        grid=(features // TILE,),
        in_specs=[
            pl.BlockSpec((ROWS, TILE), lambda i: (0, i)),
            pl.BlockSpec((ROWS, TILE), lambda i: (0, i)),
            pl.BlockSpec((STATE, TILE), lambda i: (0, i)),
            pl.BlockSpec((vec.shape[0], TILE), lambda i: (0, i)),
            pl.BlockSpec((1, HEADS), whole),
            pl.BlockSpec((ROWS, STATE), whole),
            pl.BlockSpec((ROWS, STATE), whole),
            pl.BlockSpec((TILE // HEAD, ROWS), lambda i: (base + i, 0)),
            pl.BlockSpec((ROWS, 2 * HEADS), whole),
            pl.BlockSpec((ROWS, 2 * HEADS), whole),
        ],
        out_specs=pl.BlockSpec((ROWS, TILE), lambda i: (0, place + i)),
        out_shape=jax.ShapeDtypeStruct((ROWS, width), BF16),
        scratch_shapes=[pltpu.VMEM((ROWS, ROWS), F32)],
        compiler_params=pltpu.CompilerParams(
            dimension_semantics=("arbitrary",), vmem_limit_bytes=VMEM_LIMIT
        ),
        cost_estimate=pl.CostEstimate(
            flops=1000 * ROWS * features, bytes_accessed=10 * ROWS * features, transcendentals=ROWS * features
        ),
        name="output",
    )(x, inner, state, vec, skip, write, read, cum, enter, step2)


def onward(array):
    peers = lax.axis_size("pipe")
    return lax.ppermute(array, "pipe", [(i, (i + 1) % peers) for i in range(peers)])


def normalize(values_in, gain_row):
    values = values_in.astype(F32)
    meansq = jnp.mean(values * values, axis=-1, keepdims=True)
    return (values * lax.rsqrt(meansq + epsilon) * gain_row).astype(BF16)


def shards(
    incoming, norm_gain, proj_state, proj_step, conv_weight, decay_rate, step_bias, skip_gain, out_gain
):
    x = incoming[0]
    features = x.shape[1]
    home = HEADS_HOME * HEAD
    tokens_peers = lax.axis_size("ctx")

    x_away = onward(x[:, home:])
    vec = jnp.concatenate([conv_weight[0], norm_gain, out_gain], axis=0)
    vec_away = onward(vec[:, home:])
    small_away = onward(jnp.concatenate([decay_rate, skip_gain], axis=0))

    edge = lax.ppermute(x[ROWS - HALO :], "ctx", [(i, i + 1) for i in range(tokens_peers - 1)])
    write, read, step, scale = project(x, proj_state[0], proj_step[0], norm_gain, step_bias)
    halo = normalize(edge, norm_gain[0])
    halo_away = onward(halo[:, home:])
    maps_away = onward(jnp.concatenate([write, read], axis=1))
    step_away = onward(jnp.concatenate([step, scale], axis=1))

    cum, closing, weight, enter, step2 = decays(step, decay_rate)
    inner, fresh = fresh_states(0, x, halo, vec[:, :home], scale, weight, write)
    state = prefix(0, fresh, closing, 0)
    rows = outputs(0, x, inner, state, vec, skip_gain, write, read, cum, enter, step2)
    rows_in = onward(rows)

    write, read = maps_away[:, :STATE], maps_away[:, STATE:]
    step, scale = step_away[:, :HEADS], step_away[:, HEADS:]
    cum, closing, weight, enter, step2 = decays(step, small_away[0:1])
    inner, fresh = fresh_states(HEADS_HOME, x_away, halo_away, vec_away, scale, weight, write)
    state = prefix(HEADS_HOME, fresh, closing, 1)
    passed = outputs(
        HEADS_HOME, x_away, inner, state, vec_away, small_away[1:2], write, read, cum, enter, step2,
        place=home // TILE, width=features,
    )
    passed = lax.dynamic_update_slice(passed, rows_in, (0, 0))
    return passed[None]


def solution(mesh):
    return jax.shard_map(
        shards,
        mesh=mesh,
        in_specs=(
            P("pipe", "ctx", None),
            P("pipe", None),
            P("pipe", None, None),
            P("pipe", None, None),
            P("pipe", None, None),
            P("pipe", None),
            P("pipe", None),
            P("pipe", None),
            P("pipe", None),
        ),
        out_specs=P("pipe", "ctx", None),
        check_vma=False,
    )
```

time: 863 us -> 200 us (0.23)
  the two profiles are of different devices: /device:TPU:121 before, /device:TPU:1 now
where the time goes in v1:
time: 200 us; the launch traced here: 199 us
  Pallas kernels  121 us (60%)
  waiting for transfers between devices  58.6 us (29%)
  starting transfers between devices  9.84 us (5%)
  local copies, waits for them, and re-layouts  8.32 us (4%)
    pallas_call x2, Pallas kernels, prefix(): pl.pallas_call(functools.partial(prefix_kernel, first), out_shape=jax.Sha...  63.2 us
    ppermute x7, waiting for transfers between devices, onward(): lax.ppermute(array, 'pipe', [(i, (i + 1) % peers) for i in range(peers)])  58.6 us
    pallas_call x2, Pallas kernels, outputs(): pl.pallas_call(functools.partial(output_kernel, first), grid=(features //...  24.9 us
    pallas_call x2, Pallas kernels, fresh_states(): pl.pallas_call(functools.partial(fresh_kernel, first), grid=(features //...  18.8 us
    pallas_call x1, Pallas kernels, project(): pl.pallas_call(project_kernel, grid=(features // width,), in_specs=[pl.Bl...  10.5 us
    ppermute x7, starting transfers between devices, onward(): lax.ppermute(array, 'pipe', [(i, (i + 1) % peers) for i in range(peers)])  5.79 us
    ppermute x1, starting transfers between devices, shards(): lax.ppermute(x[ROWS - HALO:], 'ctx', [(i, i + 1) for i in range(tokens_pe...  4.05 us
    pallas_call x2, Pallas kernels, decays(): pl.pallas_call(decay_kernel, out_shape=[jax.ShapeDtypeStruct((HEADS, ROWS...  4 us
  transfers between devices with their start and end apart: 8, of which 3 were waited for; matrix products, arithmetic and copies ran while one was open for 2% of the time, Pallas kernels for 61%

profile of v1, /device:TPU:1, one launch (start us, length us, event | category | flops | bytes accessed | tf_op | source)
XLA Modules:
  0.0 199.3 jit_solution(18283352492260194246)
XLA Ops:
  0.0 1.8 slice.48
  1.9 2.1 %collective-permute-start = (bf16[256,4096]{1,0:T(8,128)(2,1)S(1)}, bf16[256,4096]{1,0:T(8,128)(2,1)S(1)}, u32[]{:S(2)}, u32[]{:S(2)}) collective-permute-start(bf16[256,4096]{1,0:T(8,128)(2,1)S(1)} %slice.48), channel_id=1, source_target_pairs={{0,32},{32,64},{64,96},{96,0},{1,33},{33,65},{65,97},{97,1},{2,34}... | collective-permute-start | bytes 6291464 | tf_op jit(solution)/shard_map/ppermute | solution.py:503
  4.0 0.9 slice_bitcast_fusion
  4.9 4.0 %collective-permute-start.1 = (bf16[8,8192]{1,0:T(8,128)(2,1)S(1)}, bf16[8,8192]{1,0:T(8,128)(2,1)S(1)}, u32[]{:S(2)}, u32[]{:S(2)}) collective-permute-start(bf16[8,8192]{1,0:T(8,128)(2,1)S(1)} %slice_bitcast_fusion), channel_id=1, source_target_pairs={{0,1},{1,2},{2,3},{3,4},{4,5},{5,6},{6,7},{7,8},{8,9},{9,10},{10,1... | collective-permute-start | bytes 393224 | tf_op jit(solution)/shard_map/ppermute | solution.py:525
  9.0 0.1 pad_maximum_fusion.vec_ref
  9.1 0.7 fusion.3
  9.8 10.5 %project.1 = (bf16[256,128]{1,0:T(8,128)(2,1)}, bf16[256,128]{1,0:T(8,128)(2,1)}, f32[256,128]{1,0:T(8,128)}, f32[256,128]{1,0:T(8,128)}) custom-call(bf16[256,8192]{1,0:T(8,128)(2,1)} %bitcast.11, bf16[8192,256]{1,0:T(8,128)(2,1)} %bitcast.15, bf16[8192,128]{1,0:T(8,128)(2,1)} %bitcast.16, f32[1,8192]{1,0:T(1,128)} %gain_ref.1, f32[1,128]{1,0:T(1,128)} %bias_ref.1), custom_call_target="tpu_custom_call" | custom-call | flops 1610612736 | bytes 12582912 | tf_op jit(solution)/shard_map/project/pallas_call | solution.py:78
  20.2 2.0 decays.3
  22.2 0.2 fusion
  22.4 0.8 fusion.2.halo_ref
  23.2 9.4 %fresh.3 = (bf16[256,4096]{1,0:T(8,128)(2,1)}, bf16[128,4096]{1,0:T(8,128)(2,1)}) custom-call(bf16[256,8192]{1,0:T(8,128)(2,1)} %bitcast.12, bf16[8,8192]{1,0:T(8,128)(2,1)} %fusion.2.halo_ref, f32[6,4096]{1,0:T(8,128)} %get-tuple-element.41.vec_ref, f32[256,128]{1,0:T(8,128)} %get-tuple-element.24.scale_ref, bf16[256,256]{1,0:T(8,128)(2,1)} %get-tuple-element.34.weight_ref, ...), custom_call_target="tpu_custom_call" | custom-call | flops 41943040 | bytes 10485760 | tf_op jit(solution)/shard_map/fresh/pallas_call | solution.py:167
  32.6 31.5 %prefix.3.state_ref = bf16[128,4096]{1,0:T(8,128)(2,1)} custom-call(bf16[128,4096]{1,0:T(8,128)(2,1)} %get-tuple-element.36.fresh_ref, f32[8,128]{1,0:T(8,128)} %get-tuple-element.37.closing_ref), custom_call_target="tpu_custom_call" | custom-call | flops 524288000 | bytes 26214400 | tf_op jit(solution)/shard_map/prefix/pallas_call | solution.py:370
  64.1 0.0 copy-start.13
  64.1 0.0 copy-start.14
  64.1 12.5 %output.3 = bf16[256,4096]{1,0:T(8,128)(2,1)} custom-call(bf16[256,8192]{1,0:T(8,128)(2,1)} %bitcast.13, bf16[256,4096]{1,0:T(8,128)(2,1)} %get-tuple-element.35.inner_ref, bf16[128,4096]{1,0:T(8,128)(2,1)} %prefix.3.state_ref, f32[6,8192]{1,0:T(8,128)} %copy-done.1, f32[1,128]{1,0:T(1,128)} %skip_ref.1, bf16[256,128]{1,0:T(8,128)(2,1)} %get-tuple-element.26.write_ref, ...), custom_call_target="tpu_custom_call" | custom-call | flops 1048576000 | bytes 10485760 | tf_op jit(solution)/shard_map/output/pallas_call | solution.py:473
  76.7 1.2 collective-permute-start.7
  77.8 0.9 collective-permute-start.3
  78.8 0.3 collective-permute-start.4
  79.1 1.3 collective-permute-start.5
  80.4 53.2 %collective-permute-done.5 = f32[2,128]{1,0:T(2,128)S(1)} collective-permute-done((f32[2,128]{1,0:T(2,128)S(1)}, f32[2,128]{1,0:T(2,128)S(1)}, u32[]{:S(2)}, u32[]{:S(2)}) %collective-permute-start.5) | collective-permute-done | bytes 1056 | tf_op jit(solution)/shard_map/ppermute | solution.py:503
  133.6 0.5 fusion.6
  134.2 4.5 %collective-permute-done.6 = bf16[256,256]{1,0:T(8,128)(2,1)S(1)} collective-permute-done((bf16[256,256]{1,0:T(8,128)(2,1)S(1)}, bf16[256,256]{1,0:T(8,128)(2,1)S(1)}, u32[]{:S(2)}, u32[]{:S(2)}) %collective-permute-start.6) | collective-permute-done | bytes 131104 | tf_op jit(solution)/shard_map/ppermute | solution.py:503
  138.6 0.7 fusion.5
  139.3 0.7 fusion.4
  140.0 2.0 %decays.2 = (f32[128,256]{1,0:T(8,128)}, f32[8,128]{1,0:T(8,128)}, bf16[256,256]{1,0:T(8,128)(2,1)}, bf16[256,256]{1,0:T(8,128)(2,1)}, bf16[256,256]{1,0:T(8,128)(2,1)}) custom-call(f32[256,128]{1,0:T(8,128)} %get-tuple-element.43.step_ref, f32[1,128]{1,0:T(1,128)} %get-tuple-element.48.rate_ref), custom_call_target="tpu_custom_call" | custom-call | flops 67108864 | bytes 1048576 | tf_op jit(solution)/shard_map/decays/pallas_call | solution.py:132
  142.1 0.9 collective-permute-done.2.halo_ref
  143.0 0.6 copy-done.11
  143.6 0.7 copy-done
  144.3 9.4 %fresh.2 = (bf16[256,4096]{1,0:T(8,128)(2,1)}, bf16[128,4096]{1,0:T(8,128)(2,1)}) custom-call(bf16[256,4096]{1,0:T(8,128)(2,1)} %copy-done, bf16[8,4096]{1,0:T(8,128)(2,1)} %copy-done.11, f32[6,4096]{1,0:T(8,128)} %copy-done.4, f32[256,128]{1,0:T(8,128)} %get-tuple-element.44.scale_ref, bf16[256,256]{1,0:T(8,128)(2,1)} %get-tuple-element.25.weight_ref, ...), custom_call_target="tpu_custom_call" | custom-call | flops 41943040 | bytes 10485760 | tf_op jit(solution)/shard_map/fresh/pallas_call | solution.py:167
  153.7 31.7 %prefix.2.state_ref = bf16[128,4096]{1,0:T(8,128)(2,1)} custom-call(bf16[128,4096]{1,0:T(8,128)(2,1)} %get-tuple-element.29.fresh_ref, f32[8,128]{1,0:T(8,128)} %get-tuple-element.30.closing_ref), custom_call_target="tpu_custom_call" | custom-call | flops 524288000 | bytes 26214400 | tf_op jit(solution)/shard_map/prefix/pallas_call | solution.py:370
  185.4 12.4 %output.2 = bf16[256,8192]{1,0:T(8,128)(2,1)} custom-call(bf16[256,4096]{1,0:T(8,128)(2,1)} %copy-done, bf16[256,4096]{1,0:T(8,128)(2,1)} %get-tuple-element.28.inner_ref, bf16[128,4096]{1,0:T(8,128)(2,1)} %prefix.2.state_ref, f32[6,4096]{1,0:T(8,128)} %copy-done.4, f32[1,128]{1,0:T(1,128)} %get-tuple-element.47.skip_ref, ...), custom_call_target="tpu_custom_call" | custom-call | flops 1048576000 | bytes 10485760 | tf_op jit(solution)/shard_map/output/pallas_call | solution.py:473
  197.8 1.5 bitcast_dynamic-update-slice_fusion
  (38 shorter events, 0.1 us)
Async XLA Ops:
  0.0 8.9 %copy-start.6 = (f32[1,8192]{1,0:T(1,128)S(1)}, f32[1,8192]{1,0:T(1,128)}, u32[]{:S(2)}) copy-start(f32[1,8192]{1,0:T(1,128)} %gain_ref.1) | copy-start | bytes 98308
  0.0 8.9 %copy-start.9 = (f32[1,4,8192]{2,1,0:T(4,128)S(1)}, f32[1,4,8192]{2,1,0:T(4,128)}, u32[]{:S(2)}) copy-start(f32[1,4,8192]{2,1,0:T(4,128)} %param.13) | copy-start | bytes 393220
  0.0 9.0 %copy-start.12 = (f32[1,8192]{1,0:T(1,128)S(1)}, f32[1,8192]{1,0:T(1,128)}, u32[]{:S(2)}) copy-start(f32[1,8192]{1,0:T(1,128)} %param.17) | copy-start | bytes 98308
  1.9 141.1 %collective-permute-start = (bf16[256,4096]{1,0:T(8,128)(2,1)S(1)}, bf16[256,4096]{1,0:T(8,128)(2,1)S(1)}, u32[]{:S(2)}, u32[]{:S(2)}) collective-permute-start(bf16[256,4096]{1,0:T(8,128)(2,1)S(1)} %slice.48), channel_id=1, source_target_pairs={{0,32},{32,64},{64,96},{96,0},{1,33},{33,65},{65,97},{97,1},{2,34}... | collective-permute-start | bytes 6291464 | tf_op jit(solution)/shard_map/ppermute | solution.py:503
  4.9 17.4 %collective-permute-start.1 = (bf16[8,8192]{1,0:T(8,128)(2,1)S(1)}, bf16[8,8192]{1,0:T(8,128)(2,1)S(1)}, u32[]{:S(2)}, u32[]{:S(2)}) collective-permute-start(bf16[8,8192]{1,0:T(8,128)(2,1)S(1)} %slice_bitcast_fusion), channel_id=1, source_target_pairs={{0,1},{1,2},{2,3},{3,4},{4,5},{5,6},{6,7},{7,8},{8,9},{9,10},{10,1... | collective-permute-start | bytes 393224 | tf_op jit(solution)/shard_map/ppermute | solution.py:525
  9.1 11.2 %copy-start.1 = (f32[6,8192]{1,0:T(8,128)}, f32[6,8192]{1,0:T(8,128)S(1)}, u32[]{:S(2)}) copy-start(f32[6,8192]{1,0:T(8,128)S(1)} %pad_maximum_fusion.vec_ref) | copy-start | bytes 589828
  9.8 12.6 %copy-start.7 = (f32[1,8192]{1,0:T(1,128)S(1)}, f32[1,8192]{1,0:T(1,128)}, u32[]{:S(2)}) copy-start(f32[1,8192]{1,0:T(1,128)} %gain_ref.1) | copy-start | bytes 98308
  64.1 14.7 %copy-start.5 = (f32[256,128]{1,0:T(8,128)S(1)}, f32[256,128]{1,0:T(8,128)}, u32[]{:S(2)}) copy-start(f32[256,128]{1,0:T(8,128)} %get-tuple-element.24.scale_ref) | copy-start | bytes 393220
  64.1 14.7 %copy-start.10 = (f32[256,128]{1,0:T(8,128)S(1)}, f32[256,128]{1,0:T(8,128)}, u32[]{:S(2)}) copy-start(f32[256,128]{1,0:T(8,128)} %get-tuple-element.23.step_ref) | copy-start | bytes 393220
  64.1 15.0 %copy-start.13 = (f32[1,128]{1,0:T(1,128)S(1)}, f32[1,128]{1,0:T(1,128)}, u32[]{:S(2)}) copy-start(f32[1,128]{1,0:T(1,128)} %skip_ref.1) | copy-start | bytes 1540
  64.1 14.9 %copy-start.14 = (f32[1,128]{1,0:T(1,128)S(1)}, f32[1,128]{1,0:T(1,128)}, u32[]{:S(2)}) copy-start(f32[1,128]{1,0:T(1,128)} %rate_ref.1) | copy-start | bytes 1540
  64.1 16.3 %copy-start.3 = (bf16[256,128]{1,0:T(8,128)(2,1)S(1)}, bf16[256,128]{1,0:T(8,128)(2,1)}, u32[]{:S(2)}) copy-start(bf16[256,128]{1,0:T(8,128)(2,1)} %get-tuple-element.26.write_ref) | copy-start | bytes 196612
  64.1 16.3 %copy-start.8 = (bf16[256,128]{1,0:T(8,128)(2,1)S(1)}, bf16[256,128]{1,0:T(8,128)(2,1)}, u32[]{:S(2)}) copy-start(bf16[256,128]{1,0:T(8,128)(2,1)} %get-tuple-element.27.read_ref) | copy-start | bytes 196612
  64.1 70.0 %copy-start.2 = (bf16[8,8192]{1,0:T(8,128)(2,1)S(1)}, bf16[8,8192]{1,0:T(8,128)(2,1)}, u32[]{:S(2)}) copy-start(bf16[8,8192]{1,0:T(8,128)(2,1)} %fusion.2.halo_ref) | copy-start | bytes 393220
  76.7 121.1 %collective-permute-start.7 = (bf16[256,4096]{1,0:T(8,128)(2,1)}, bf16[256,4096]{1,0:T(8,128)(2,1)S(1)}, u32[]{:S(2)}, u32[]{:S(2)}) collective-permute-start(bf16[256,4096]{1,0:T(8,128)(2,1)} %output.3), channel_id=1, source_target_pairs={{0,32},{32,64},{64,96},{96,0},{1,33},{33,65},{65,97},{97,1},{2,34}... | collective-permute-start | bytes 6291464 | tf_op jit(solution)/shard_map/ppermute | solution.py:503
  77.8 64.3 %collective-permute-start.3 = (f32[6,4096]{1,0:T(8,128)S(1)}, f32[6,4096]{1,0:T(8,128)S(1)}, u32[]{:S(2)}, u32[]{:S(2)}) collective-permute-start(f32[6,4096]{1,0:T(8,128)S(1)} %get-tuple-element.42), channel_id=1, source_target_pairs={{0,32},{32,64},{64,96},{96,0},{1,33},{33,65},{65,97},{97,1},{2,34}... | collective-permute-start | bytes 294920 | tf_op jit(solution)/shard_map/ppermute | solution.py:503
  78.8 60.6 %collective-permute-start.4 = (f32[256,256]{1,0:T(8,128)S(1)}, f32[256,256]{1,0:T(8,128)S(1)}, u32[]{:S(2)}, u32[]{:S(2)}) collective-permute-start(f32[256,256]{1,0:T(8,128)S(1)} %pad_maximum_fusion.1), channel_id=1, source_target_pairs={{0,32},{32,64},{64,96},{96,0},{1,33},{33,65},{65,97},{97,1},{2,34}... | collective-permute-start | bytes 786440 | tf_op jit(solution)/shard_map/ppermute | solution.py:503
  79.1 54.6 %collective-permute-start.5 = (f32[2,128]{1,0:T(2,128)S(1)}, f32[2,128]{1,0:T(2,128)S(1)}, u32[]{:S(2)}, u32[]{:S(2)}) collective-permute-start(f32[2,128]{1,0:T(2,128)S(1)} %pad_maximum_fusion.3), channel_id=1, source_target_pairs={{0,32},{32,64},{64,96},{96,0},{1,33},{33,65},{65,97},{97,1},{2,34}... | collective-permute-start | bytes 3080 | tf_op jit(solution)/shard_map/ppermute | solution.py:503
  133.6 5.0 %collective-permute-start.6 = (bf16[256,256]{1,0:T(8,128)(2,1)S(1)}, bf16[256,256]{1,0:T(8,128)(2,1)S(1)}, u32[]{:S(2)}, u32[]{:S(2)}) collective-permute-start(bf16[256,256]{1,0:T(8,128)(2,1)S(1)} %pad_maximum_fusion.2), channel_id=1, source_target_pairs={{0,32},{32,64},{64,96},{96,0},{1,33},{33,65},{65,97},{97,1},{2,34}... | collective-permute-start | bytes 393224 | tf_op jit(solution)/shard_map/ppermute | solution.py:503
  138.6 4.3 %collective-permute-start.2 = (bf16[8,4096]{1,0:T(8,128)(2,1)S(1)}, bf16[8,4096]{1,0:T(8,128)(2,1)S(1)}, u32[]{:S(2)}, u32[]{:S(2)}) collective-permute-start(bf16[8,4096]{1,0:T(8,128)(2,1)S(1)} %slice.49), channel_id=1, source_target_pairs={{0,32},{32,64},{64,96},{96,0},{1,33},{33,65},{65,97},{97,1},{2,34}... | collective-permute-start | bytes 196616 | tf_op jit(solution)/shard_map/ppermute | solution.py:503
  142.1 0.9 copy-start.4
  143.0 0.6 copy-start.11
  143.0 1.3 copy-start

commit v2 on v0

v2 whole, which is shorter than its diff:
```python
import functools

import jax
import jax.numpy as jnp
from jax import lax
from jax.experimental import pallas as pl
from jax.experimental.pallas import tpu as pltpu
from jax.sharding import PartitionSpec as P

MESH = pl.DeviceIdType.MESH
F32 = jnp.float32
BF16 = jnp.bfloat16

ROWS = 256
STATE = 128
HEADS = 128
HEAD = 64
CONV = 4
HALO = 8
TILE = 512
STEP_ROWS = ROWS + 8
CHIPS = 16
LOG2E = 1.4426950408889634
epsilon = 1e-05
VMEM_LIMIT = 56 * 1024 * 1024

HEADS_HOME = 64
HEADS_EARLY = 16
HEADS_AWAY = HEADS - HEADS_HOME


def dot(a, b):
    return jnp.dot(a, b, preferred_element_type=F32)


def three_parts(x):
    first = x.astype(BF16)
    rest = x - first.astype(F32)
    second = rest.astype(BF16)
    return first, second, (rest - second.astype(F32)).astype(BF16)


def spreader(rows, width):
    head = lax.broadcasted_iota(jnp.int32, (2 * rows, width), 0) % rows
    feature = lax.broadcasted_iota(jnp.int32, (2 * rows, width), 1) // HEAD
    return (head == feature).astype(F32).astype(BF16)


def spread_heads(values, width):
    high = values.astype(BF16).astype(F32)
    both = jnp.concatenate([high, values - high], axis=0).astype(BF16)
    return lax.dot_general(
        both, spreader(values.shape[0], width), (((0,), (0,)), ((), ())), preferred_element_type=F32
    )


def project_kernel(x_ref, ws_ref, wt_ref, gain_ref, bias_ref, rate_ref, skip_ref, maps_ref, step_ref, scale, acc):
    at = pl.program_id(0)
    width = ws_ref.shape[0]

    @pl.when(at == 0)
    def _():
        total = jnp.zeros((ROWS, 128), F32)
        for i in range(x_ref.shape[1] // 512):
            part = x_ref[:, i * 512 : (i + 1) * 512].astype(F32)
            part = part * part
            total = total + (part[:, :128] + part[:, 128:256]) + (part[:, 256:384] + part[:, 384:])
        meansq = jnp.sum(total, axis=-1, keepdims=True) * (1.0 / x_ref.shape[1])
        scale[...] = jnp.broadcast_to(lax.rsqrt(meansq + epsilon), (ROWS, 128))
        acc[...] = jnp.zeros_like(acc)

    columns = pl.ds(pl.multiple_of(at * width, width), width)
    normed = (x_ref[:, columns].astype(F32) * scale[:, :1] * gain_ref[...]).astype(BF16)
    acc[:, : 2 * STATE] += dot(normed, ws_ref[...])
    acc[:, 2 * STATE :] += dot(normed, wt_ref[...])

    @pl.when(at == pl.num_programs(0) - 1)
    def _():
        maps_ref[...] = acc[:, : 2 * STATE].astype(BF16)
        step_ref[:ROWS, :] = jax.nn.softplus(acc[:, 2 * STATE :] + bias_ref[...])
        flat = scale[...].T
        step_ref[ROWS : ROWS + 8, :] = jnp.concatenate(
            [flat[:1, :128], flat[:1, 128:], rate_ref[...], skip_ref[...], jnp.zeros((4, HEADS), F32)], axis=0
        )


def project(x, proj_state, proj_step, gain, bias, rate, skip):
    features = x.shape[1]
    width = 1024
    whole = lambda i: (0, 0)
    return pl.pallas_call(
        project_kernel,
        grid=(features // width,),
        in_specs=[
            pl.BlockSpec((ROWS, features), whole),
            pl.BlockSpec((width, 2 * STATE), lambda i: (i, 0)),
            pl.BlockSpec((width, HEADS), lambda i: (i, 0)),
            pl.BlockSpec((1, width), lambda i: (0, i)),
            pl.BlockSpec((1, HEADS), whole),
            pl.BlockSpec((1, HEADS), whole),
            pl.BlockSpec((1, HEADS), whole),
        ],
        out_specs=[pl.BlockSpec((ROWS, 2 * STATE), whole), pl.BlockSpec((STEP_ROWS, HEADS), whole)],
        out_shape=[
            jax.ShapeDtypeStruct((ROWS, 2 * STATE), BF16),
            jax.ShapeDtypeStruct((STEP_ROWS, HEADS), F32),
        ],
        scratch_shapes=[pltpu.VMEM((ROWS, 128), F32), pltpu.VMEM((ROWS, 3 * STATE), F32)],
        compiler_params=pltpu.CompilerParams(
            dimension_semantics=("arbitrary",), vmem_limit_bytes=VMEM_LIMIT
        ),
        cost_estimate=pl.CostEstimate(
            flops=ROWS * features, bytes_accessed=ROWS * features, transcendentals=0
        ),
        name="project",
    )(x, proj_state, proj_step, gain, bias, rate, skip)


def group_kernel(
    first,
    pieces,
    *refs,
):
    x_refs, refs = refs[: len(pieces)], refs[len(pieces) :]
    group_body(first, pieces, x_refs, *refs)


def group_body(
    first,
    pieces,
    x_refs,
    halo_ref,
    vec_ref,
    maps_ref,
    step_ref,
    out_ref,
    x_ref,
    x_sems,
    cum_heads,
    weight_heads,
    enter_heads,
    step_heads,
    skip_heads,
    closing,
    scale,
    scores,
    write_flat,
    inner_ref,
    within_ref,
    fresh,
    peer,
    peer_closing,
    total,
    total_closing,
    got,
    got_closing,
    before,
    entering,
    mine,
    theirs,
    landed,
    pair_send,
    pair_recv,
    send1,
    recv1,
    send2,
    recv2,
    send3,
    recv3,
):
    features = x_ref.shape[1]
    half, quarter = features // 2, features // 4
    heads = features // HEAD
    tiles = features // TILE
    in_tile = TILE // HEAD
    me = lax.axis_index("ctx")
    core = lax.rem(me, 2)
    chip = me // 2
    partner = chip * 2 + (1 - core)

    def device(index):
        return {"ctx": index}

    def tile_columns(i):
        return pl.ds(pl.multiple_of(i * TILE, TILE), TILE)

    def tile_heads(i):
        return pl.ds(pl.multiple_of(first + i * in_tile, in_tile), in_tile)

    def place(of):
        return (
            pl.ds(pl.multiple_of(lax.rem(of, 8) * 16, 16), 16),
            pl.ds(pl.multiple_of((of // 8) * quarter, 128), quarter),
        )

    barrier = pltpu.get_barrier_semaphore()
    pl.semaphore_signal(barrier, inc=1, device_id=device(partner), device_id_type=MESH)

    def greet(d, carry):
        other = lax.rem(chip + d, CHIPS) * 2 + core
        pl.semaphore_signal(barrier, inc=1, device_id=device(other), device_id_type=MESH)
        return carry

    lax.fori_loop(1, CHIPS, greet, 0)

    loads = []
    for k, width in enumerate(pieces):
        start = sum(pieces[:k])
        load = pltpu.make_async_copy(
            x_refs[k].at[:, :width], x_ref.at[:, start : start + width], x_sems.at[k]
        )
        load.start()
        loads.append(load)

    step = step_ref[:ROWS, :]
    extra = step_ref[ROWS:, :]
    log_decay = -step * extra[2:3, :]
    row = lax.broadcasted_iota(jnp.int32, (ROWS, ROWS), 0)
    column = lax.broadcasted_iota(jnp.int32, (ROWS, ROWS), 1)
    lower = (row >= column).astype(F32).astype(BF16)
    part1, part2, part3 = three_parts(log_decay)
    cumulative = dot(lower, part3) + dot(lower, part2) + dot(lower, part1)
    last = cumulative[ROWS - 1 :, :]
    cum_heads[...] = (cumulative * LOG2E).T
    weight_heads[...] = (jnp.exp(last - cumulative) * step).T
    enter_heads[...] = jnp.exp(cumulative).T
    step_heads[...] = step.T
    closing[...] = jnp.broadcast_to(last, (8, HEADS))
    extra_columns = extra.T
    skip_heads[...] = jnp.broadcast_to(extra_columns[:, 3:4], (HEADS, 128))
    scale[...] = jnp.broadcast_to(
        jnp.concatenate([extra_columns[:, 0:1], extra_columns[:, 1:2]], axis=0), (ROWS, 128)
    )
    write_flat[...] = maps_ref[:, :STATE].astype(F32).T.astype(BF16)
    product = dot(maps_ref[:, STATE:], write_flat[...])
    scores[...] = jnp.where(row >= column, product, 0.0)

    for load in loads:
        load.wait()

    def fresh_tile(i):
        columns = tile_columns(i)
        normed = (x_ref[:, columns].astype(F32) * scale[:, :1] * vec_ref[4:5, columns]).astype(BF16)
        normed = jnp.concatenate([halo_ref[:, columns].astype(F32), normed.astype(F32)], axis=0)
        shifted = pltpu.roll(normed, 1, 0)
        early = vec_ref[1:2, columns] * normed + vec_ref[0:1, columns] * shifted
        conv = vec_ref[3:4, columns] * normed[HALO:] + vec_ref[2:3, columns] * shifted[HALO:]
        conv = conv + pltpu.roll(early, 2, 0)[HALO:]
        conv = conv * 0.5
        inner = (conv + conv * jnp.tanh(conv)).astype(BF16)
        inner_ref[:, columns] = inner
        spread = spread_heads(weight_heads[tile_heads(i), :], TILE)
        weighted = (inner.astype(F32) * spread).astype(BF16)
        fresh[:, columns] = dot(write_flat[...], weighted).astype(BF16)

    def within_tile(i):
        columns = tile_columns(i)
        inner = inner_ref[:, columns].astype(F32)
        stepped = (inner * spread_heads(step_heads[tile_heads(i), :], TILE)).astype(BF16)
        cum = cum_heads[tile_heads(i), :]
        cum_columns = cum.T
        top, bottom = scores[:128, :128], scores[128:, :]
        lane = lax.broadcasted_iota(jnp.int32, (ROWS, 128), 1)
        for pair in range(TILE // 128):
            values = stepped[:, pair * 128 : (pair + 1) * 128]
            upper = lower = None
            for side in range(2):
                h = pair * 2 + side
                column = cum_columns[:, h : h + 1]
                row = cum[h : h + 1, :]
                own = jnp.where((lane >= HEAD) == (side == 1), values, jnp.zeros_like(values))
                mix0 = (jnp.exp2(jnp.minimum(column[:128] - row[:, :128], 0.0)) * top).astype(BF16)
                mix1 = (jnp.exp2(jnp.minimum(column[128:] - row, 0.0)) * bottom).astype(BF16)
                up, low = dot(mix0, own[:128]), dot(mix1, own)
                upper = up if upper is None else upper + up
                lower = low if lower is None else lower + low
            at = pl.ds(pl.multiple_of(i * TILE + pair * 128, 128), 128)
            within_ref[:128, at] = upper
            within_ref[128:, at] = lower

    def finish_tile(i, state):
        columns = tile_columns(i)
        inner = inner_ref[:, columns].astype(F32)
        carried = dot(maps_ref[:, STATE:], state) * spread_heads(enter_heads[tile_heads(i), :], TILE)
        skip = spread_heads(skip_heads[tile_heads(i), :8], TILE)[0:1, :]
        output = within_ref[:, columns] + carried + skip * inner
        square = (output * output).astype(BF16)
        a = lax.broadcasted_iota(jnp.int32, (256, 256), 0) // HEAD
        b = lax.broadcasted_iota(jnp.int32, (256, 256), 1) // HEAD
        same = (a == b).astype(F32).astype(BF16)
        sums = jnp.concatenate(
            [dot(square[:, k * 256 : (k + 1) * 256], same) for k in range(TILE // 256)], axis=1
        )
        normed = output * lax.rsqrt(sums * (1.0 / HEAD) + epsilon)
        out_ref[:, columns] = (x_ref[:, columns].astype(F32) + normed * vec_ref[5:6, columns]).astype(BF16)

    def run(body, start, stop):
        def one(i, carry):
            body(i)
            return carry

        lax.fori_loop(start, stop, one, 0)

    mine_columns = pl.ds(pl.multiple_of(core * half, 128), half)
    other_columns = pl.ds(pl.multiple_of((1 - core) * half, 128), half)
    mine_tile, other_tile = core * (tiles // 2), (1 - core) * (tiles // 2)

    run(lambda j: fresh_tile(other_tile + j), 0, tiles // 2)
    pl.semaphore_wait(barrier, CHIPS)
    to_pair = pltpu.make_async_remote_copy(
        fresh.at[:, other_columns], peer, pair_send.at[0], pair_recv.at[0], device(partner), MESH
    )
    to_pair_closing = pltpu.make_async_remote_copy(
        closing, peer_closing, pair_send.at[1], pair_recv.at[1], device(partner), MESH
    )
    to_pair.start()
    to_pair_closing.start()
    run(lambda j: fresh_tile(mine_tile + j), 0, tiles // 2)
    to_pair.wait()
    to_pair_closing.wait()

    is_first = core == 0
    own = fresh[:, mine_columns].astype(F32)
    other = peer[...].astype(F32)
    state0 = jnp.where(is_first, own, other)
    state1 = jnp.where(is_first, other, own)
    closing0 = jnp.where(is_first, closing[...], peer_closing[...])
    closing1 = jnp.where(is_first, peer_closing[...], closing[...])

    def decay_of(log_decays, first_head, width):
        values = jnp.exp(log_decays)
        high = values.astype(BF16)
        both = jnp.concatenate([high, (values - high.astype(F32)).astype(BF16)], axis=1)
        head = lax.broadcasted_iota(jnp.int32, (2 * HEADS, width), 0) % HEADS
        feature = lax.broadcasted_iota(jnp.int32, (2 * HEADS, width), 1) // HEAD
        return dot(both, (head == first_head + feature).astype(F32).astype(BF16))

    both = decay_of(jnp.concatenate([closing0, closing1], axis=0), first + core * (heads // 2), half)
    decay0, decay1 = both[0:1, :], both[8:9, :]
    total[...] = (decay1 * state0 + state1).astype(BF16)
    total_closing[...] = closing0 + closing1

    def state_copy(source, target, to):
        rows, columns = place(to)
        return pltpu.make_async_remote_copy(
            total.at[rows, columns], got.at[target], send1.at[to], recv1.at[source], device(to * 2 + core), MESH
        )

    def closing_copy(source, target, to):
        return pltpu.make_async_remote_copy(
            total_closing, got_closing.at[target], send2.at[to], recv2.at[source], device(to * 2 + core), MESH
        )

    def back_copy(source, to):
        rows, columns = place(source)
        return pltpu.make_async_remote_copy(
            before.at[to], entering.at[rows, columns], send3.at[to], recv3.at[source], device(to * 2 + core), MESH
        )

    def start12(d):
        to = lax.rem(chip + d, CHIPS)
        closing_copy(chip, chip, to).start()
        state_copy(chip, chip, to).start()

    def wait12(d):
        of = lax.rem(chip + d, CHIPS)
        closing_copy(of, of, of).wait_recv()
        state_copy(of, of, of).wait_recv()
        closing_copy(chip, chip, of).wait_send()
        state_copy(chip, chip, of).wait_send()

    run(start12, 1, CHIPS)
    rows, columns = place(chip)
    got[chip] = total[rows, columns]
    got_closing[chip] = total_closing[...]
    run(within_tile, 0, tiles // 2)
    run(wait12, 1, CHIPS)

    decays = decay_of(got_closing[:, 0, :], first + core * (heads // 2) + (chip // 8) * (heads // 4), quarter)
    state = jnp.zeros((16, quarter), F32)
    for k in range(CHIPS):
        before[k] = state.astype(BF16)
        if k < CHIPS - 1:
            state = decays[k : k + 1, :] * state + got[k].astype(F32)

    def start3(d):
        back_copy(chip, lax.rem(chip + d, CHIPS)).start()

    def wait3(d):
        of = lax.rem(chip + d, CHIPS)
        back_copy(of, of).wait_recv()
        back_copy(chip, of).wait_send()

    run(start3, 1, CHIPS)
    entering[rows, columns] = before[chip]
    run(within_tile, tiles // 2, tiles)
    run(wait3, 1, CHIPS)

    for_first = entering[...]
    for_second = (decay0 * for_first.astype(F32) + state0).astype(BF16)
    theirs[...] = jnp.where(is_first, for_second, for_first)
    back = pltpu.make_async_remote_copy(theirs, landed, pair_send.at[2], pair_recv.at[2], device(partner), MESH)
    back.start()
    mine[...] = jnp.where(is_first, for_first, for_second)
    run(lambda j: finish_tile(mine_tile + j, mine[:, tile_columns(j)]), 0, tiles // 2)
    back.wait()
    run(lambda j: finish_tile(other_tile + j, landed[:, tile_columns(j)]), 0, tiles // 2)


def group(first, pieces, xs, halo, vec, maps, step, collective_id):
    features = sum(pieces)
    half, quarter = features // 2, features // 4
    corner = lambda i: (0, 0)
    dma = pltpu.SemaphoreType.DMA
    vmem = pltpu.VMEM
    return pl.pallas_call(
        functools.partial(group_kernel, first, pieces),
        out_shape=jax.ShapeDtypeStruct((ROWS, features), BF16),
        grid=(1,),
        in_specs=[pl.BlockSpec(memory_space=pl.ANY)] * len(pieces)
        + [
            pl.BlockSpec((HALO, features), corner),
            pl.BlockSpec((vec.shape[0], features), corner),
            pl.BlockSpec((ROWS, 2 * STATE), corner),
            pl.BlockSpec((STEP_ROWS, HEADS), corner),
        ],
        out_specs=pl.BlockSpec((ROWS, features), corner),
        scratch_shapes=[
            vmem((ROWS, features), BF16),
            dma((len(pieces),)),
            vmem((HEADS, ROWS), F32),
            vmem((HEADS, ROWS), F32),
            vmem((HEADS, ROWS), F32),
            vmem((HEADS, ROWS), F32),
            vmem((HEADS, 128), F32),
            vmem((8, HEADS), F32),
            vmem((ROWS, 128), F32),
            vmem((ROWS, ROWS), F32),
            vmem((STATE, ROWS), BF16),
            vmem((ROWS, features), BF16),
            vmem((ROWS, features), F32),
            vmem((STATE, features), BF16),
            vmem((STATE, half), BF16),
            vmem((8, HEADS), F32),
            vmem((STATE, half), BF16),
            vmem((8, HEADS), F32),
            vmem((CHIPS, 16, quarter), BF16),
            vmem((CHIPS, 8, HEADS), F32),
            vmem((CHIPS, 16, quarter), BF16),
            vmem((STATE, half), BF16),
            vmem((STATE, half), BF16),
            vmem((STATE, half), BF16),
            vmem((STATE, half), BF16),
            dma((3,)),
            dma((3,)),
            dma((CHIPS,)),
            dma((CHIPS,)),
            dma((CHIPS,)),
            dma((CHIPS,)),
            dma((CHIPS,)),
            dma((CHIPS,)),
        ],
        compiler_params=pltpu.CompilerParams(
            collective_id=collective_id, has_side_effects=True, vmem_limit_bytes=VMEM_LIMIT
        ),
        cost_estimate=pl.CostEstimate(
            flops=ROWS * features, bytes_accessed=ROWS * features, transcendentals=0
        ),
        name="group",
    )(*xs, halo, vec, maps, step)


def widen_kernel(part_ref, out_ref):
    out_ref[...] = part_ref[...]


def widen(part, width):
    columns = part.shape[1]
    block = 1024
    skip = (width - columns) // block
    return pl.pallas_call(
        widen_kernel,
        grid=(columns // block,),
        in_specs=[pl.BlockSpec((ROWS, block), lambda i: (0, i))],
        out_specs=pl.BlockSpec((ROWS, block), lambda i: (0, skip + i)),
        out_shape=jax.ShapeDtypeStruct((ROWS, width), BF16),
        compiler_params=pltpu.CompilerParams(dimension_semantics=("arbitrary",)),
        cost_estimate=pl.CostEstimate(flops=1, bytes_accessed=ROWS * columns * 4, transcendentals=0),
        name="widen",
    )(part)


def onward(array):
    peers = lax.axis_size("pipe")
    return lax.ppermute(array, "pipe", [(i, (i + 1) % peers) for i in range(peers)])


def normalize(values_in, gain_row):
    values = values_in.astype(F32)
    meansq = jnp.mean(values * values, axis=-1, keepdims=True)
    return (values * lax.rsqrt(meansq + epsilon) * gain_row).astype(BF16)


def shards(
    incoming, norm_gain, proj_state, proj_step, conv_weight, decay_rate, step_bias, skip_gain, out_gain
):
    x = incoming[0]
    home, early = HEADS_HOME * HEAD, HEADS_EARLY * HEAD
    away = HEADS_AWAY * HEAD
    tokens_peers = lax.axis_size("ctx")

    x_early = onward(x[:, home : home + early])
    x_late = onward(x[:, home + early :])
    edge = lax.ppermute(x[ROWS - HALO :], "ctx", [(i, i + 1) for i in range(tokens_peers - 1)])
    vec = jnp.concatenate([conv_weight[0], norm_gain, out_gain], axis=0)
    vec_away = onward(vec[:, home:])
    maps, step = project(x, proj_state[0], proj_step[0], norm_gain, step_bias, decay_rate, skip_gain)
    maps, step, x_early = lax.optimization_barrier((maps, step, x_early))
    maps_away, step_away = onward(maps), onward(step)
    halo = normalize(edge, norm_gain[0])
    halo_away = onward(halo[:, home:])

    rows = group(0, (home,), (x,), halo, vec, maps, step, 0)
    rows, x_late, halo_away, vec_away, maps_away, step_away = lax.optimization_barrier(
        (rows, x_late, halo_away, vec_away, maps_away, step_away)
    )
    rows_in = onward(rows)

    rows_away = group(
        HEADS_HOME, (early, away - early), (x_early, x_late), halo_away, vec_away, maps_away, step_away, 1
    )
    passed = widen(rows_away, x.shape[1])
    return lax.dynamic_update_slice(passed, rows_in, (0, 0))[None]


def solution(mesh):
    return jax.shard_map(
        shards,
        mesh=mesh,
        in_specs=(
            P("pipe", "ctx", None),
            P("pipe", None),
            P("pipe", None, None),
            P("pipe", None, None),
            P("pipe", None, None),
            P("pipe", None),
            P("pipe", None),
            P("pipe", None),
            P("pipe", None),
        ),
        out_specs=P("pipe", "ctx", None),
        check_vma=False,
    )
```

time: 863 us -> 115 us (0.13)
  the two profiles are of different devices: /device:TPU:121 before, /device:TPU:1 now
where the time goes in v2:
time: 115 us; the launch traced here: 114 us
  Pallas kernels  89.1 us (77%)
  starting transfers between devices  11.6 us (10%)
  waiting for transfers between devices  6.02 us (5%)
  local copies, waits for them, and re-layouts  5.47 us (5%)
  other arithmetic  1.32 us (1%)
    pallas_call x2, Pallas kernels, group(): pl.pallas_call(functools.partial(group_kernel, first, pieces), out_shape=...  74.9 us
    pallas_call x1, Pallas kernels, project(): pl.pallas_call(project_kernel, grid=(features // width,), in_specs=[pl.Bl...  10.4 us
    ppermute x7, starting transfers between devices, onward(): lax.ppermute(array, 'pipe', [(i, (i + 1) % peers) for i in range(peers)])  7.01 us
    ppermute x7, waiting for transfers between devices, onward(): lax.ppermute(array, 'pipe', [(i, (i + 1) % peers) for i in range(peers)])  6.01 us
    ppermute x1, starting transfers between devices, shards(): lax.ppermute(x[ROWS - HALO:], 'ctx', [(i, i + 1) for i in range(tokens_pe...  4.59 us
    pallas_call x1, Pallas kernels, widen(): pl.pallas_call(widen_kernel, grid=(columns // block,), in_specs=[pl.Block...  3.79 us
  transfers between devices with their start and end apart: 8, of which 2 were waited for; matrix products, arithmetic and copies ran while one was open for 3% of the time, Pallas kernels for 78%

profile of v2, /device:TPU:1, one launch (start us, length us, event | category | flops | bytes accessed | tf_op | source)
XLA Modules:
  0.0 113.6 jit_solution(15163582295322317157)
XLA Ops:
  0.0 0.9 slice_bitcast_fusion
  0.9 4.6 %collective-permute-start.1 = (bf16[8,8192]{1,0:T(8,128)(2,1)S(1)}, bf16[8,8192]{1,0:T(8,128)(2,1)S(1)}, u32[]{:S(2)}, u32[]{:S(2)}) collective-permute-start(bf16[8,8192]{1,0:T(8,128)(2,1)S(1)} %slice_bitcast_fusion), channel_id=1, source_target_pairs={{0,1},{1,2},{2,3},{3,4},{4,5},{5,6},{6,7},{7,8},{8,9},{9,10},{10,1... | collective-permute-start | bytes 393224 | tf_op jit(solution)/shard_map/ppermute | solution.py:514
  5.5 1.1 slice.24
  6.6 1.3 %collective-permute-start = (bf16[256,1024]{1,0:T(8,128)(2,1)S(1)}, bf16[256,1024]{1,0:T(8,128)(2,1)S(1)}, u32[]{:S(2)}, u32[]{:S(2)}) collective-permute-start(bf16[256,1024]{1,0:T(8,128)(2,1)S(1)} %slice.24), channel_id=1, source_target_pairs={{0,32},{32,64},{64,96},{96,0},{1,33},{33,65},{65,97},{97,1},{2,34}... | collective-permute-start | bytes 1572872 | tf_op jit(solution)/shard_map/ppermute | solution.py:495
  7.9 1.0 pad_maximum_fusion.refs_2_
  8.9 0.0 copy-start
  8.9 1.3 %collective-permute-start.4 = (f32[6,4096]{1,0:T(8,128)S(1)}, f32[6,4096]{1,0:T(8,128)S(1)}, u32[]{:S(2)}, u32[]{:S(2)}) collective-permute-start(f32[6,4096]{1,0:T(8,128)S(1)} %slice.27), channel_id=1, source_target_pairs={{0,32},{32,64},{64,96},{96,0},{1,33},{33,65},{65,97},{97,1},{2,34}... | collective-permute-start | bytes 294920 | tf_op jit(solution)/shard_map/ppermute | solution.py:495
  10.2 1.5 %slice.25 = bf16[256,3072]{1,0:T(8,128)(2,1)S(1)} slice(bf16[256,8192]{1,0:T(8,128)(2,1)} %bitcast.11), slice={[0:256], [5120:8192]} | slice | bytes 3145728 | tf_op jit(solution)/shard_map/slice | solution.py:513
  11.7 1.0 collective-permute-start.2
  12.7 10.4 %project.1 = (bf16[256,256]{1,0:T(8,128)(2,1)}, f32[264,128]{1,0:T(8,128)}) custom-call(bf16[256,8192]{1,0:T(8,128)(2,1)} %bitcast.12, bf16[8192,256]{1,0:T(8,128)(2,1)} %bitcast.15, bf16[8192,128]{1,0:T(8,128)(2,1)} %bitcast.16, f32[1,8192]{1,0:T(1,128)} %gain_ref.1, f32[1,128]{1,0:T(1,128)} %bias_ref.1, f32[1,128]{1,0:T(1,128)} %rate_ref.1, f32[1,128]{1,0:T(1,128)} %skip_ref.1), custom_call_target="tpu_custom_call" | custom-call | flops 2097152 | bytes 2097152 | tf_op jit(solution)/shard_map/project/pallas_call | solution.py:91
  23.1 0.0 collective-permute-done.1
  23.1 0.2 fusion
  23.3 0.0 collective-permute-done.refs_0_
  23.3 0.0 copy-start.3
  23.4 0.3 collective-permute-start.5
  23.6 1.2 %collective-permute-start.6 = (f32[264,128]{1,0:T(8,128)}, f32[264,128]{1,0:T(8,128)S(1)}, u32[]{:S(2)}, u32[]{:S(2)}) collective-permute-start(f32[264,128]{1,0:T(8,128)} %get-tuple-element.20.refs_4_), channel_id=1, source_target_pairs={{0,32},{32,64},{64,96},{96,0},{1,33},{33,65},{65,97},{97,1},{2,34}... | collective-permute-start | bytes 405512 | tf_op jit(solution)/shard_map/ppermute | solution.py:495
  24.8 0.1 fusion.2.refs_1_
  25.0 1.3 %collective-permute-start.3 = (bf16[8,4096]{1,0:T(8,128)(2,1)S(1)}, bf16[8,4096]{1,0:T(8,128)(2,1)S(1)}, u32[]{:S(2)}, u32[]{:S(2)}) collective-permute-start(bf16[8,4096]{1,0:T(8,128)(2,1)S(1)} %slice.26), channel_id=1, source_target_pairs={{0,32},{32,64},{64,96},{96,0},{1,33},{33,65},{65,97},{97,1},{2,34}... | collective-permute-start | bytes 196616 | tf_op jit(solution)/shard_map/ppermute | solution.py:495
  26.2 0.0 copy-done.2
  26.2 36.6 %group.2 = bf16[256,4096]{1,0:T(8,128)(2,1)} custom-call(bf16[256,8192]{1,0:T(8,128)(2,1)} %bitcast.13, bf16[8,8192]{1,0:T(8,128)(2,1)} %copy-done.2, f32[6,8192]{1,0:T(8,128)} %copy-done, bf16[256,256]{1,0:T(8,128)(2,1)} %get-tuple-element.19.refs_3_, f32[264,128]{1,0:T(8,128)} %get-tuple-element.20.refs_4_), custom_call_target="tpu_custom_call" | custom-call | flops 1048576 | bytes 1048576 | tf_op jit(solution)/shard_map/group/pallas_call | solution.py:416
  62.9 0.0 collective-permute-done.4.refs_3_
  62.9 0.9 collective-permute-done.3.refs_2_
  63.8 0.0 collective-permute-done.5.refs_4_
  63.8 0.0 collective-permute-done.6.refs_5_
  63.8 0.0 collective-permute-done.2.refs_1_
  63.8 0.0 copy-start.1
  63.8 0.7 collective-permute-start.7
  64.6 0.5 copy-done.1
  65.1 38.2 %group.3.part_ref = bf16[256,4096]{1,0:T(8,128)(2,1)} custom-call(bf16[256,1024]{1,0:T(8,128)(2,1)} %copy-done.3, bf16[256,3072]{1,0:T(8,128)(2,1)} %copy-done.1, bf16[8,4096]{1,0:T(8,128)(2,1)} %copy-done.8, f32[6,4096]{1,0:T(8,128)} %copy-done.6, bf16[256,256]{1,0:T(8,128)(2,1)} %copy-done.7, f32[264,128]{1,0:T(8,128)} %copy-done.5), custom_call_target="tpu_custom_call" | custom-call | flops 1048576 | bytes 1048576 | tf_op jit(solution)/shard_map/group/pallas_call | solution.py:416
  103.3 3.8 %widen.1 = bf16[256,8192]{1,0:T(8,128)(2,1)} custom-call(bf16[256,4096]{1,0:T(8,128)(2,1)} %group.3.part_ref), custom_call_target="tpu_custom_call" | custom-call | flops 1 | bytes 4194304 | tf_op jit(solution)/shard_map/widen/pallas_call | solution.py:481
  107.1 5.1 %collective-permute-done.7 = bf16[256,4096]{1,0:T(8,128)(2,1)S(1)} collective-permute-done((bf16[256,4096]{1,0:T(8,128)(2,1)}, bf16[256,4096]{1,0:T(8,128)(2,1)S(1)}, u32[]{:S(2)}, u32[]{:S(2)}) %collective-permute-start.7) | collective-permute-done | bytes 2097184 | tf_op jit(solution)/shard_map/ppermute | solution.py:495
  112.2 1.5 %bitcast_dynamic-update-slice_fusion = bf16[1,256,8192]{2,1,0:T(8,128)(2,1)} fusion(bf16[1,256,8192]{2,1,0:T(8,128)(2,1)} %bitcast.14, bf16[256,4096]{1,0:T(8,128)(2,1)S(1)} %collective-permute-done.7), kind=kLoop, calls=%fused_computation | loop fusion | bytes 4194304 | tf_op jit(solution)/shard_map/dynamic_update_slice | solution.py:533
  (16 shorter events, 0.1 us)
Async XLA Ops:
  0.9 22.2 %collective-permute-start.1 = (bf16[8,8192]{1,0:T(8,128)(2,1)S(1)}, bf16[8,8192]{1,0:T(8,128)(2,1)S(1)}, u32[]{:S(2)}, u32[]{:S(2)}) collective-permute-start(bf16[8,8192]{1,0:T(8,128)(2,1)S(1)} %slice_bitcast_fusion), channel_id=1, source_target_pairs={{0,1},{1,2},{2,3},{3,4},{4,5},{5,6},{6,7},{7,8},{8,9},{9,10},{10,1... | collective-permute-start | bytes 393224 | tf_op jit(solution)/shard_map/ppermute | solution.py:514
  6.6 16.7 %collective-permute-start = (bf16[256,1024]{1,0:T(8,128)(2,1)S(1)}, bf16[256,1024]{1,0:T(8,128)(2,1)S(1)}, u32[]{:S(2)}, u32[]{:S(2)}) collective-permute-start(bf16[256,1024]{1,0:T(8,128)(2,1)S(1)} %slice.24), channel_id=1, source_target_pairs={{0,32},{32,64},{64,96},{96,0},{1,33},{33,65},{65,97},{97,1},{2,34}... | collective-permute-start | bytes 1572872 | tf_op jit(solution)/shard_map/ppermute | solution.py:495
  8.9 14.2 %copy-start = (f32[6,8192]{1,0:T(8,128)}, f32[6,8192]{1,0:T(8,128)S(1)}, u32[]{:S(2)}) copy-start(f32[6,8192]{1,0:T(8,128)S(1)} %pad_maximum_fusion.refs_2_) | copy-start | bytes 589828
  8.9 53.9 %collective-permute-start.4 = (f32[6,4096]{1,0:T(8,128)S(1)}, f32[6,4096]{1,0:T(8,128)S(1)}, u32[]{:S(2)}, u32[]{:S(2)}) collective-permute-start(f32[6,4096]{1,0:T(8,128)S(1)} %slice.27), channel_id=1, source_target_pairs={{0,32},{32,64},{64,96},{96,0},{1,33},{33,65},{65,97},{97,1},{2,34}... | collective-permute-start | bytes 294920 | tf_op jit(solution)/shard_map/ppermute | solution.py:495
  11.7 52.1 %collective-permute-start.2 = (bf16[256,3072]{1,0:T(8,128)(2,1)S(1)}, bf16[256,3072]{1,0:T(8,128)(2,1)S(1)}, u32[]{:S(2)}, u32[]{:S(2)}) collective-permute-start(bf16[256,3072]{1,0:T(8,128)(2,1)S(1)} %slice.25), channel_id=1, source_target_pairs={{0,32},{32,64},{64,96},{96,0},{1,33},{33,65},{65,97},{97,1},{2,34}... | collective-permute-start | bytes 4718600 | tf_op jit(solution)/shard_map/ppermute | solution.py:495
  12.7 12.1 %copy-start.4 = (f32[1,8192]{1,0:T(1,128)S(1)}, f32[1,8192]{1,0:T(1,128)}, u32[]{:S(2)}) copy-start(f32[1,8192]{1,0:T(1,128)} %gain_ref.1) | copy-start | bytes 98308
  23.3 41.2 %copy-start.3 = (bf16[256,1024]{1,0:T(8,128)(2,1)}, bf16[256,1024]{1,0:T(8,128)(2,1)S(1)}, u32[]{:S(2)}) copy-start(bf16[256,1024]{1,0:T(8,128)(2,1)S(1)} %collective-permute-done.refs_0_) | copy-start | bytes 1572868
  23.4 40.5 %collective-permute-start.5 = (bf16[256,256]{1,0:T(8,128)(2,1)}, bf16[256,256]{1,0:T(8,128)(2,1)S(1)}, u32[]{:S(2)}, u32[]{:S(2)}) collective-permute-start(bf16[256,256]{1,0:T(8,128)(2,1)} %get-tuple-element.19.refs_3_), channel_id=1, source_target_pairs={{0,32},{32,64},{64,96},{96,0},{1,33},{33,65},{65,97},{97,1},{2,34}... | collective-permute-start | bytes 393224 | tf_op jit(solution)/shard_map/ppermute | solution.py:495
  23.6 40.2 %collective-permute-start.6 = (f32[264,128]{1,0:T(8,128)}, f32[264,128]{1,0:T(8,128)S(1)}, u32[]{:S(2)}, u32[]{:S(2)}) collective-permute-start(f32[264,128]{1,0:T(8,128)} %get-tuple-element.20.refs_4_), channel_id=1, source_target_pairs={{0,32},{32,64},{64,96},{96,0},{1,33},{33,65},{65,97},{97,1},{2,34}... | collective-permute-start | bytes 405512 | tf_op jit(solution)/shard_map/ppermute | solution.py:495
  24.9 1.3 %copy-start.2 = (bf16[8,8192]{1,0:T(8,128)(2,1)}, bf16[8,8192]{1,0:T(8,128)(2,1)S(1)}, u32[]{:S(2)}) copy-start(bf16[8,8192]{1,0:T(8,128)(2,1)S(1)} %fusion.2.refs_1_) | copy-start | bytes 393220
  25.0 38.8 %collective-permute-start.3 = (bf16[8,4096]{1,0:T(8,128)(2,1)S(1)}, bf16[8,4096]{1,0:T(8,128)(2,1)S(1)}, u32[]{:S(2)}, u32[]{:S(2)}) collective-permute-start(bf16[8,4096]{1,0:T(8,128)(2,1)S(1)} %slice.26), channel_id=1, source_target_pairs={{0,32},{32,64},{64,96},{96,0},{1,33},{33,65},{65,97},{97,1},{2,34}... | collective-permute-start | bytes 196616 | tf_op jit(solution)/shard_map/ppermute | solution.py:495
  62.9 1.7 %copy-start.6 = (f32[6,4096]{1,0:T(8,128)}, f32[6,4096]{1,0:T(8,128)S(1)}, u32[]{:S(2)}) copy-start(f32[6,4096]{1,0:T(8,128)S(1)} %collective-permute-done.4.refs_3_) | copy-start | bytes 294916
  63.8 0.8 copy-start.8
  63.8 0.8 copy-start.7
  63.8 0.8 copy-start.5
  63.8 1.2 %copy-start.1 = (bf16[256,3072]{1,0:T(8,128)(2,1)}, bf16[256,3072]{1,0:T(8,128)(2,1)S(1)}, u32[]{:S(2)}) copy-start(bf16[256,3072]{1,0:T(8,128)(2,1)S(1)} %collective-permute-done.2.refs_1_) | copy-start | bytes 4718596
  63.8 48.3 %collective-permute-start.7 = (bf16[256,4096]{1,0:T(8,128)(2,1)}, bf16[256,4096]{1,0:T(8,128)(2,1)S(1)}, u32[]{:S(2)}, u32[]{:S(2)}) collective-permute-start(bf16[256,4096]{1,0:T(8,128)(2,1)} %group.2), channel_id=1, source_target_pairs={{0,32},{32,64},{64,96},{96,0},{1,33},{33,65},{65,97},{97,1},{2,34}... | collective-permute-start | bytes 6291464 | tf_op jit(solution)/shard_map/ppermute | solution.py:495

commit v3 on v2

--- a/solution.py
+++ b/solution.py
@@ -25,8 +25,11 @@
 VMEM_LIMIT = 56 * 1024 * 1024
 
 HEADS_HOME = 64
-HEADS_EARLY = 16
+HEADS_BACK = 12
+HEADS_EARLY = 12
+HEADS_ROUND = 12
 HEADS_AWAY = HEADS - HEADS_HOME
+HEADS_LATE = HEADS_AWAY - HEADS_EARLY - HEADS_ROUND
 
 
 def dot(a, b):
@@ -54,23 +57,79 @@
     )
 
 
-def project_kernel(x_ref, ws_ref, wt_ref, gain_ref, bias_ref, rate_ref, skip_ref, maps_ref, step_ref, scale, acc):
+def project_kernel(
+    first,
+    x_ref,
+    ws_ref,
+    wt_ref,
+    gain_ref,
+    conv_ref,
+    out_gain_ref,
+    bias_ref,
+    rate_ref,
+    skip_ref,
+    maps_ref,
+    step_ref,
+    vec_ref,
+    vec_away_ref,
+    halo_ref,
+    halo_away_ref,
+    early_ref,
+    late_ref,
+    round_ref,
+    scale,
+    acc,
+    edge,
+    send,
+    recv,
+    late_sem,
+):
     at = pl.program_id(0)
     width = ws_ref.shape[0]
+    features = x_ref.shape[1]
+    away = vec_away_ref.shape[1]
+    me = lax.axis_index("ctx")
+    peers = lax.axis_size("ctx")
+    after, ahead = lax.rem(me + 1, peers), lax.rem(me + peers - 1, peers)
+    edge_copy = pltpu.make_async_remote_copy(
+        x_ref.at[ROWS - 16 :, :], edge, send.at[0], recv.at[0], {"ctx": after}, MESH
+    )
+    section = lax.axis_index("pipe")
+    sections = lax.axis_size("pipe")
+    behind, beyond = lax.rem(section + sections - 1, sections), lax.rem(section + 1, sections)
+    second = first + early_ref.shape[1]
+    third = second + late_ref.shape[1]
+    early_copy = pltpu.make_async_remote_copy(
+        x_ref.at[:, first:second], early_ref, send.at[1], recv.at[1], {"pipe": beyond}, MESH
+    )
+    late_copy = pltpu.make_async_copy(x_ref.at[:, second:third], late_ref, late_sem)
+    round_copy = pltpu.make_async_remote_copy(
+        x_ref.at[:, third:], round_ref, send.at[2], recv.at[2], {"pipe": behind}, MESH
+    )
 
     @pl.when(at == 0)
     def _():
+        barrier = pltpu.get_barrier_semaphore()
+        for other in (after, ahead):
+            pl.semaphore_signal(barrier, inc=1, device_id={"ctx": other}, device_id_type=MESH)
+        for other in (behind, beyond):
+            pl.semaphore_signal(barrier, inc=1, device_id={"pipe": other}, device_id_type=MESH)
+        pl.semaphore_wait(barrier, 4)
+        early_copy.start()
+        round_copy.start()
+        edge_copy.start()
+        late_copy.start()
         total = jnp.zeros((ROWS, 128), F32)
-        for i in range(x_ref.shape[1] // 512):
+        for i in range(features // 512):
             part = x_ref[:, i * 512 : (i + 1) * 512].astype(F32)
             part = part * part
             total = total + (part[:, :128] + part[:, 128:256]) + (part[:, 256:384] + part[:, 384:])
-        meansq = jnp.sum(total, axis=-1, keepdims=True) * (1.0 / x_ref.shape[1])
+        meansq = jnp.sum(total, axis=-1, keepdims=True) * (1.0 / features)
         scale[...] = jnp.broadcast_to(lax.rsqrt(meansq + epsilon), (ROWS, 128))
         acc[...] = jnp.zeros_like(acc)
 
     columns = pl.ds(pl.multiple_of(at * width, width), width)
-    normed = (x_ref[:, columns].astype(F32) * scale[:, :1] * gain_ref[...]).astype(BF16)
+    normed = (x_ref[:, columns].astype(F32) * scale[:, :1] * gain_ref[:, columns]).astype(BF16)
     acc[:, : 2 * STATE] += dot(normed, ws_ref[...])
     acc[:, 2 * STATE :] += dot(normed, wt_ref[...])
 
@@ -82,58 +141,118 @@
         step_ref[ROWS : ROWS + 8, :] = jnp.concatenate(
             [flat[:1, :128], flat[:1, 128:], rate_ref[...], skip_ref[...], jnp.zeros((4, HEADS), F32)], axis=0
         )
-
-
-def project(x, proj_state, proj_step, gain, bias, rate, skip):
+        vec_ref[:4, :] = conv_ref[...]
+        vec_ref[4:5, :] = gain_ref[...]
+        vec_ref[5:6, :] = out_gain_ref[...]
+        vec_ref[6:8, :] = jnp.zeros((2, features), F32)
+        vec_away_ref[...] = vec_ref[:, features - away :]
+        edge_copy.wait()
+        rows = edge[...].astype(F32)[16 - HALO :, :]
+        meansq = jnp.sum(rows * rows, axis=-1, keepdims=True) * (1.0 / features)
+        rows = rows * lax.rsqrt(meansq + epsilon) * gain_ref[...]
+        rows = jnp.where(me == 0, jnp.zeros_like(rows), rows).astype(BF16)
+        halo_ref[...] = rows
+        halo_away_ref[...] = rows[:, features - away :]
+        late_copy.wait()
+        early_copy.wait()
+        round_copy.wait()
+
+
+def project(x, proj_state, proj_step, gain, conv, out_gain, bias, rate, skip, widths, collective_id):
     features = x.shape[1]
+    away = sum(widths)
     width = 1024
     whole = lambda i: (0, 0)
+    dma = pltpu.SemaphoreType.DMA
+    row = pl.BlockSpec((1, features), whole)
+    small = pl.BlockSpec((1, HEADS), whole)
     return pl.pallas_call(
-        project_kernel,
+        functools.partial(project_kernel, features - away),
         grid=(features // width,),
         in_specs=[
             pl.BlockSpec((ROWS, features), whole),
             pl.BlockSpec((width, 2 * STATE), lambda i: (i, 0)),
             pl.BlockSpec((width, HEADS), lambda i: (i, 0)),
-            pl.BlockSpec((1, width), lambda i: (0, i)),
-            pl.BlockSpec((1, HEADS), whole),
-            pl.BlockSpec((1, HEADS), whole),
-            pl.BlockSpec((1, HEADS), whole),
+            row,
+            pl.BlockSpec((CONV, features), whole),
+            row,
+            small,
+            small,
+            small,
         ],
-        out_specs=[pl.BlockSpec((ROWS, 2 * STATE), whole), pl.BlockSpec((STEP_ROWS, HEADS), whole)],
+        out_specs=[
+            pl.BlockSpec((ROWS, 2 * STATE), whole),
+            pl.BlockSpec((STEP_ROWS, HEADS), whole),
+            pl.BlockSpec((8, features), whole),
+            pl.BlockSpec((8, away), whole),
+            pl.BlockSpec((HALO, features), whole),
+            pl.BlockSpec((HALO, away), whole),
+        ]
+        + [pl.BlockSpec(memory_space=pl.ANY)] * 3,
         out_shape=[
             jax.ShapeDtypeStruct((ROWS, 2 * STATE), BF16),
             jax.ShapeDtypeStruct((STEP_ROWS, HEADS), F32),
+            jax.ShapeDtypeStruct((8, features), F32),
+            jax.ShapeDtypeStruct((8, away), F32),
+            jax.ShapeDtypeStruct((HALO, features), BF16),
+            jax.ShapeDtypeStruct((HALO, away), BF16),
+        ]
+        + [jax.ShapeDtypeStruct((ROWS, columns), BF16) for columns in widths],
+        scratch_shapes=[
+            pltpu.VMEM((ROWS, 128), F32),
+            pltpu.VMEM((ROWS, 3 * STATE), F32),
+            pltpu.VMEM((16, features), BF16),
+            dma((3,)),
+            dma((3,)),
+            dma,
         ],
-        scratch_shapes=[pltpu.VMEM((ROWS, 128), F32), pltpu.VMEM((ROWS, 3 * STATE), F32)],
         compiler_params=pltpu.CompilerParams(
-            dimension_semantics=("arbitrary",), vmem_limit_bytes=VMEM_LIMIT
+            dimension_semantics=("arbitrary",),
+            vmem_limit_bytes=VMEM_LIMIT,
+            collective_id=collective_id,
+            has_side_effects=True,
         ),
         cost_estimate=pl.CostEstimate(
-            flops=ROWS * features, bytes_accessed=ROWS * features, transcendentals=0
+            flops=2 * ROWS * features * 3 * STATE, bytes_accessed=36 << 20, transcendentals=0
         ),
         name="project",
-    )(x, proj_state, proj_step, gain, bias, rate, skip)
-
-
-def group_kernel(
-    first,
-    pieces,
-    *refs,
-):
-    x_refs, refs = refs[: len(pieces)], refs[len(pieces) :]
-    group_body(first, pieces, x_refs, *refs)
+    )(x, proj_state, proj_step, gain, conv, out_gain, bias, rate, skip)
+
+
+def group_kernel(first, pieces, hops, outs, *refs):
+    refs = list(refs)
+
+    def take(n):
+        taken = refs[:n]
+        del refs[:n]
+        return taken
+
+    x_refs = take(len(pieces))
+    shared = take(4)
+    relay_in = take(1)[0]
+    out_refs = take(len(outs))
+    relay_out = take(1)[0]
+    group_body(first, pieces, hops, outs, x_refs, *shared, relay_in, out_refs, relay_out, *refs)
 
 
 def group_body(
     first,
     pieces,
+    hops,
+    outs,
     x_refs,
     halo_ref,
     vec_ref,
     maps_ref,
     step_ref,
+    relay_in,
+    out_refs,
+    relay_out,
+    relay_slots,
+    relay_send,
+    relay_recv,
     out_ref,
+    out_sems,
     x_ref,
     x_sems,
     cum_heads,
@@ -181,6 +300,21 @@
     def device(index):
         return {"ctx": index}
 
+    section = lax.axis_index("pipe")
+    sections = lax.axis_size("pipe")
+    behind, ahead = lax.rem(section + sections - 1, sections), lax.rem(section + 1, sections)
+
+    def hop(k):
+        source = relay_in if k == 0 else relay_slots.at[k - 1]
+        return pltpu.make_async_remote_copy(
+            source, relay_slots.at[k], relay_send.at[k], relay_recv.at[k], {"pipe": behind}, MESH
+        )
+
+    def pass_on(k):
+        if k > 0:
+            hop(k - 1).wait_recv()
+        hop(k).start()
+
     def tile_columns(i):
         return pl.ds(pl.multiple_of(i * TILE, TILE), TILE)
 
@@ -202,6 +336,8 @@
         return carry
 
     lax.fori_loop(1, CHIPS, greet, 0)
+    for other in (behind, ahead):
+        pl.semaphore_signal(barrier, inc=1, device_id={"pipe": other}, device_id_type=MESH)
 
     loads = []
     for k, width in enumerate(pieces):
@@ -237,6 +373,8 @@
 
     for load in loads:
         load.wait()
+    pl.semaphore_wait(barrier, CHIPS + 2)
+    pass_on(0)
 
     def fresh_tile(i):
         columns = tile_columns(i)
@@ -306,7 +444,6 @@
     mine_tile, other_tile = core * (tiles // 2), (1 - core) * (tiles // 2)
 
     run(lambda j: fresh_tile(other_tile + j), 0, tiles // 2)
-    pl.semaphore_wait(barrier, CHIPS)
     to_pair = pltpu.make_async_remote_copy(
         fresh.at[:, other_columns], peer, pair_send.at[0], pair_recv.at[0], device(partner), MESH
     )
@@ -373,7 +510,11 @@
     rows, columns = place(chip)
     got[chip] = total[rows, columns]
     got_closing[chip] = total_closing[...]
+    if hops == 3:
+        pass_on(1)
     run(within_tile, 0, tiles // 2)
+    if hops == 2:
+        pass_on(1)
     run(wait12, 1, CHIPS)
 
     decays = decay_of(got_closing[:, 0, :], first + core * (heads // 2) + (chip // 8) * (heads // 4), quarter)
@@ -393,6 +534,8 @@
 
     run(start3, 1, CHIPS)
     entering[rows, columns] = before[chip]
+    if hops == 3:
+        pass_on(2)
     run(within_tile, tiles // 2, tiles)
     run(wait3, 1, CHIPS)
 
@@ -405,17 +548,31 @@
     run(lambda j: finish_tile(mine_tile + j, mine[:, tile_columns(j)]), 0, tiles // 2)
     back.wait()
     run(lambda j: finish_tile(other_tile + j, landed[:, tile_columns(j)]), 0, tiles // 2)
-
-
-def group(first, pieces, xs, halo, vec, maps, step, collective_id):
+    stores = []
+    for k, width in enumerate(outs):
+        start = sum(outs[:k])
+        store = pltpu.make_async_copy(out_ref.at[:, start : start + width], out_refs[k], out_sems.at[k])
+        store.start()
+        stores.append(store)
+    hop(hops - 1).wait_recv()
+    last = pltpu.make_async_copy(relay_slots.at[hops - 1], relay_out, out_sems.at[len(outs)])
+    last.start()
+    for k in range(hops):
+        hop(k).wait_send()
+    for store in stores + [last]:
+        store.wait()
+
+
+def group(first, pieces, xs, halo, vec, maps, step, relay, hops, outs, collective_id):
     features = sum(pieces)
     half, quarter = features // 2, features // 4
     corner = lambda i: (0, 0)
     dma = pltpu.SemaphoreType.DMA
     vmem = pltpu.VMEM
     return pl.pallas_call(
-        functools.partial(group_kernel, first, pieces),
-        out_shape=jax.ShapeDtypeStruct((ROWS, features), BF16),
+        functools.partial(group_kernel, first, pieces, hops, outs),
+        out_shape=[jax.ShapeDtypeStruct((ROWS, columns), BF16) for columns in outs]
+        + [jax.ShapeDtypeStruct(relay.shape, BF16)],
         grid=(1,),
         in_specs=[pl.BlockSpec(memory_space=pl.ANY)] * len(pieces)
         + [
@@ -423,9 +580,15 @@
             pl.BlockSpec((vec.shape[0], features), corner),
             pl.BlockSpec((ROWS, 2 * STATE), corner),
             pl.BlockSpec((STEP_ROWS, HEADS), corner),
+            pl.BlockSpec(memory_space=pl.ANY),
         ],
-        out_specs=pl.BlockSpec((ROWS, features), corner),
+        out_specs=[pl.BlockSpec(memory_space=pl.ANY)] * (len(outs) + 1),
         scratch_shapes=[
+            vmem((hops,) + relay.shape, BF16),
+            dma((hops,)),
+            dma((hops,)),
+            vmem((ROWS, features), BF16),
+            dma((len(outs) + 1,)),
             vmem((ROWS, features), BF16),
             dma((len(pieces),)),
             vmem((HEADS, ROWS), F32),
@@ -467,69 +630,67 @@
             flops=ROWS * features, bytes_accessed=ROWS * features, transcendentals=0
         ),
         name="group",
-    )(*xs, halo, vec, maps, step)
-
-
-def widen_kernel(part_ref, out_ref):
-    out_ref[...] = part_ref[...]
-
-
-def widen(part, width):
-    columns = part.shape[1]
-    block = 1024
-    skip = (width - columns) // block
+    )(*xs, halo, vec, maps, step, relay)
+
+
+def widen_kernel(*refs):
+    parts, out, sems = refs[:-2], refs[-2], refs[-1]
+    start = out.shape[1] - sum(part.shape[1] for part in parts)
+    copies = []
+    for k, part in enumerate(parts):
+        copies.append(pltpu.make_async_copy(part, out.at[:, start : start + part.shape[1]], sems.at[k]))
+        start += part.shape[1]
+    for copy in copies:
+        copy.start()
+    for copy in copies:
+        copy.wait()
+
+
+def widen(parts, width):
     return pl.pallas_call(
         widen_kernel,
-        grid=(columns // block,),
-        in_specs=[pl.BlockSpec((ROWS, block), lambda i: (0, i))],
-        out_specs=pl.BlockSpec((ROWS, block), lambda i: (0, skip + i)),
+        in_specs=[pl.BlockSpec(memory_space=pltpu.VMEM)] * len(parts),
+        out_specs=pl.BlockSpec(memory_space=pl.ANY),
         out_shape=jax.ShapeDtypeStruct((ROWS, width), BF16),
-        compiler_params=pltpu.CompilerParams(dimension_semantics=("arbitrary",)),
-        cost_estimate=pl.CostEstimate(flops=1, bytes_accessed=ROWS * columns * 4, transcendentals=0),
+        scratch_shapes=[pltpu.SemaphoreType.DMA((len(parts),))],
+        cost_estimate=pl.CostEstimate(flops=1, bytes_accessed=ROWS * width * 2, transcendentals=0),
         name="widen",
-    )(part)
-
-
-def onward(array):
+    )(*parts)
+
+
+def moved(array, by):
     peers = lax.axis_size("pipe")
-    return lax.ppermute(array, "pipe", [(i, (i + 1) % peers) for i in range(peers)])
-
-
-def normalize(values_in, gain_row):
-    values = values_in.astype(F32)
-    meansq = jnp.mean(values * values, axis=-1, keepdims=True)
-    return (values * lax.rsqrt(meansq + epsilon) * gain_row).astype(BF16)
+    return lax.ppermute(array, "pipe", [(i, (i + by) % peers) for i in range(peers)])
 
 
 def shards(
     incoming, norm_gain, proj_state, proj_step, conv_weight, decay_rate, step_bias, skip_gain, out_gain
 ):
     x = incoming[0]
-    home, early = HEADS_HOME * HEAD, HEADS_EARLY * HEAD
-    away = HEADS_AWAY * HEAD
-    tokens_peers = lax.axis_size("ctx")
-
-    x_early = onward(x[:, home : home + early])
-    x_late = onward(x[:, home + early :])
-    edge = lax.ppermute(x[ROWS - HALO :], "ctx", [(i, i + 1) for i in range(tokens_peers - 1)])
-    vec = jnp.concatenate([conv_weight[0], norm_gain, out_gain], axis=0)
-    vec_away = onward(vec[:, home:])
-    maps, step = project(x, proj_state[0], proj_step[0], norm_gain, step_bias, decay_rate, skip_gain)
-    maps, step, x_early = lax.optimization_barrier((maps, step, x_early))
-    maps_away, step_away = onward(maps), onward(step)
-    halo = normalize(edge, norm_gain[0])
-    halo_away = onward(halo[:, home:])
-
-    rows = group(0, (home,), (x,), halo, vec, maps, step, 0)
+    features = x.shape[1]
+    home, back, away = HEADS_HOME * HEAD, HEADS_BACK * HEAD, HEADS_AWAY * HEAD
+    early, late, round_ = HEADS_EARLY * HEAD, HEADS_LATE * HEAD, HEADS_ROUND * HEAD
+
+    maps, step, vec, vec_away, halo, halo_away, x_early, x_late, x_round = project(
+        x, proj_state[0], proj_step[0], norm_gain, conv_weight[0], out_gain, step_bias, decay_rate, skip_gain,
+        (early, late, round_), 2,
+    )
+    x_late, vec_away, halo_away = moved(x_late, 1), moved(vec_away, 1), moved(halo_away, 1)
+    maps_away, step_away = moved(maps, 1), moved(step, 1)
+
+    rows, rows_back, x_round = group(
+        0, (home,), (x,), halo, vec, maps, step, x_round, 2, (home - back, back), 0
+    )
     rows, x_late, halo_away, vec_away, maps_away, step_away = lax.optimization_barrier(
         (rows, x_late, halo_away, vec_away, maps_away, step_away)
     )
-    rows_in = onward(rows)
-
-    rows_away = group(
-        HEADS_HOME, (early, away - early), (x_early, x_late), halo_away, vec_away, maps_away, step_away, 1
-    )
-    passed = widen(rows_away, x.shape[1])
+    rows_in = moved(rows, 1)
+
+    rows_away, rows_back = group(
+        HEADS_HOME, (early, late, round_), (x_early, x_late, x_round), halo_away, vec_away, maps_away, step_away,
+        rows_back, 3, (away,), 1,
+    )
+    passed = widen((rows_back, rows_away), features)
     return lax.dynamic_update_slice(passed, rows_in, (0, 0))[None]
 
 

time: 115 us -> 104 us (0.904); the launches traced: 114 us -> 104 us
  Pallas kernels: 89.1 us -> 97.2 us
  starting transfers between devices: 11.6 us -> 5.26 us
  waiting for transfers between devices: 6.02 us -> 0.02 us
  local copies, waits for them, and re-layouts: 5.47 us -> 1.35 us
  other arithmetic: 1.32 us -> 0 us
    pallas_call x4, Pallas kernels: 89.1 us -> 97.2 us  [the longest x2 79.7 us: group(): pl.pallas_call(functools.partial(group_kernel, first, pieces, hops, outs)...]
    ppermute x8 -> x6, starting transfers between devices: 11.6 us -> 5.26 us  [moved(): lax.ppermute(array, 'pipe', [(i, (i + by) % peers) for i in range(peers)])]
    ppermute x8 -> x6, waiting for transfers between devices: 6.02 us -> 0.02 us  [moved(): lax.ppermute(array, 'pipe', [(i, (i + by) % peers) for i in range(peers)])]
    slice x5 -> x0, local copies, waits for them, and re-layouts: 3.52 us -> none  [the longest x1 1.51 us: shards(): x_late = onward(x[:, home + early:])]
  transfers between devices with their start and end apart: 8 -> 6, of which waited for: 2 -> 0; matrix products, arithmetic and copies ran while one was open for 3% -> 0% of each run, Pallas kernels for 78% -> 80%
where the time goes in v3:
time: 104 us
  Pallas kernels  97.2 us (93%)
  starting transfers between devices  5.26 us (5%)
  local copies, waits for them, and re-layouts  1.35 us (1%)
    pallas_call x2, Pallas kernels, group(): pl.pallas_call(functools.partial(group_kernel, first, pieces, hops, outs)...  79.7 us
    pallas_call x1, Pallas kernels, project(): pl.pallas_call(functools.partial(project_kernel, features - away), grid=(...  14.3 us
    ppermute x6, starting transfers between devices, moved(): lax.ppermute(array, 'pipe', [(i, (i + by) % peers) for i in range(peers)])  5.26 us
    pallas_call x1, Pallas kernels, widen(): pl.pallas_call(widen_kernel, in_specs=[pl.BlockSpec(memory_space=pltpu.VM...  3.2 us
  transfers between devices with their start and end apart: 6, of which 0 were waited for; matrix products, arithmetic and copies ran while one was open for 0% of the time, Pallas kernels for 80%

profile of v3, /device:TPU:1, one launch (start us, length us, event | category | flops | bytes accessed | tf_op | source)
XLA Modules:
  0.0 104.0 jit_solution(6876171819802979583)
XLA Ops:
  0.0 14.3 %project.1 = (bf16[256,256]{1,0:T(8,128)(2,1)}, f32[264,128]{1,0:T(8,128)}, f32[8,8192]{1,0:T(8,128)}, f32[8,4096]{1,0:T(8,128)}, bf16[8,8192]{1,0:T(8,128)(2,1)...) custom-call(bf16[256,8192]{1,0:T(8,128)(2,1)} %bitcast.7, ...), custom_call_target="tpu_custom_call" | custom-call | flops 1610612736 | bytes 37748736 | tf_op jit(solution)/shard_map/project/pallas_call | solution.py:169
  14.3 0.6 collective-permute-start
  15.0 1.2 %collective-permute-start.4 = (f32[264,128]{1,0:T(8,128)}, f32[264,128]{1,0:T(8,128)S(1)}, u32[]{:S(2)}, u32[]{:S(2)}) collective-permute-start(f32[264,128]{1,0:T(8,128)} %get-tuple-element.29.refs_4_), channel_id=1, source_target_pairs={{0,32},{32,64},{64,96},{96,0},{1,33},{33,65},{65,97},{97,1},{2,34}... | collective-permute-start | bytes 405512 | tf_op jit(solution)/shard_map/ppermute | solution.py:663
  16.2 0.9 collective-permute-start.2
  17.1 0.8 collective-permute-start.3
  17.9 0.6 collective-permute-start.1
  18.5 42.7 %group.2 = (bf16[256,3328]{1,0:T(8,128)(2,1)}, bf16[256,768]{1,0:T(8,128)(2,1)}, bf16[256,768]{1,0:T(8,128)(2,1)}) custom-call(bf16[256,8192]{1,0:T(8,128)(2,1)} %bitcast.8, bf16[8,8192]{1,0:T(8,128)(2,1)} %get-tuple-element.26.refs_1_, f32[8,8192]{1,0:T(8,128)} %get-tuple-element.27.refs_2_, bf16[256,256]{1,0:T(8,128)(2,1)} %get-tuple-element.28.refs_3_, ...), custom_call_target="tpu_custom_call" | custom-call | flops 1048576 | bytes 1048576 | tf_op jit(solution)/shard_map/group/pallas_call | solution.py:572
  61.3 0.0 collective-permute-done.1.refs_3_
  61.3 0.0 copy-start.4
  61.3 0.0 collective-permute-done.2.refs_4_
  61.3 0.0 copy-start.2
  61.3 0.0 collective-permute-done.3.refs_5_
  61.3 0.0 copy-start.3
  61.3 0.0 collective-permute-done.4.refs_6_
  61.3 0.0 copy-start.1
  61.3 0.0 collective-permute-done.refs_1_
  61.4 0.0 copy-start
  61.4 1.1 %collective-permute-start.5 = (bf16[256,3328]{1,0:T(8,128)(2,1)}, bf16[256,3328]{1,0:T(8,128)(2,1)S(1)}, u32[]{:S(2)}, u32[]{:S(2)}) collective-permute-start(bf16[256,3328]{1,0:T(8,128)(2,1)} %get-tuple-element.44), channel_id=1, source_target_pairs={{0,32},{32,64},{64,96},{96,0},{1,33},{33,65},{65,97},{97,1},{2,34}... | collective-permute-start | bytes 5111816 | tf_op jit(solution)/shard_map/ppermute | solution.py:663
  62.4 0.0 copy-done.4
  62.4 0.0 copy-done.2
  62.4 0.0 copy-done.3
  62.4 0.0 copy-done.1
  62.4 0.0 copy-done
  62.5 37.0 %group.3 = (bf16[256,4096]{1,0:T(8,128)(2,1)}, bf16[256,768]{1,0:T(8,128)(2,1)}) custom-call(bf16[256,768]{1,0:T(8,128)(2,1)} %get-tuple-element.25.refs_0_, bf16[256,2560]{1,0:T(8,128)(2,1)} %copy-done, bf16[256,768]{1,0:T(8,128)(2,1)} %get-tuple-element.36.refs_2_, bf16[8,4096]{1,0:T(8,128)(2,1)} %copy-done.4, f32[8,4096]{1,0:T(8,128)} %copy-done.2, ...), custom_call_target="tpu_custom_call" | custom-call | flops 1048576 | bytes 1048576 | tf_op jit(solution)/shard_map/group/pallas_call | solution.py:572
  99.4 3.2 %widen.1 = bf16[256,8192]{1,0:T(8,128)(2,1)} custom-call(bf16[256,768]{1,0:T(8,128)(2,1)} %get-tuple-element.42.refs_0_, bf16[256,4096]{1,0:T(8,128)(2,1)} %get-tuple-element.43.refs_1_), custom_call_target="tpu_custom_call" | custom-call | flops 1 | bytes 4194304 | tf_op jit(solution)/shard_map/widen/pallas_call | solution.py:650
  102.7 0.0 collective-permute-done.5
  102.7 1.3 %bitcast_dynamic-update-slice_fusion = bf16[1,256,8192]{2,1,0:T(8,128)(2,1)} fusion(bf16[1,256,8192]{2,1,0:T(8,128)(2,1)} %bitcast.10, bf16[256,3328]{1,0:T(8,128)(2,1)S(1)} %collective-permute-done.5), kind=kLoop, calls=%fused_computation | loop fusion | bytes 3407872 | tf_op jit(solution)/shard_map/dynamic_update_slice | solution.py:694
Async XLA Ops:
  14.3 47.0 %collective-permute-start = (bf16[256,2560]{1,0:T(8,128)(2,1)}, bf16[256,2560]{1,0:T(8,128)(2,1)S(1)}, u32[]{:S(2)}, u32[]{:S(2)}) collective-permute-start(bf16[256,2560]{1,0:T(8,128)(2,1)} %get-tuple-element.32), channel_id=1, source_target_pairs={{0,32},{32,64},{64,96},{96,0},{1,33},{33,65},{65,97},{97,1},{2,34}... | collective-permute-start | bytes 3932168 | tf_op jit(solution)/shard_map/ppermute | solution.py:663
  15.0 46.3 %collective-permute-start.4 = (f32[264,128]{1,0:T(8,128)}, f32[264,128]{1,0:T(8,128)S(1)}, u32[]{:S(2)}, u32[]{:S(2)}) collective-permute-start(f32[264,128]{1,0:T(8,128)} %get-tuple-element.29.refs_4_), channel_id=1, source_target_pairs={{0,32},{32,64},{64,96},{96,0},{1,33},{33,65},{65,97},{97,1},{2,34}... | collective-permute-start | bytes 405512 | tf_op jit(solution)/shard_map/ppermute | solution.py:663
  16.2 45.1 %collective-permute-start.2 = (f32[8,4096]{1,0:T(8,128)}, f32[8,4096]{1,0:T(8,128)S(1)}, u32[]{:S(2)}, u32[]{:S(2)}) collective-permute-start(f32[8,4096]{1,0:T(8,128)} %get-tuple-element.34), channel_id=1, source_target_pairs={{0,32},{32,64},{64,96},{96,0},{1,33},{33,65},{65,97},{97,1},{2,34}... | collective-permute-start | bytes 393224 | tf_op jit(solution)/shard_map/ppermute | solution.py:663
  17.1 44.2 %collective-permute-start.3 = (bf16[256,256]{1,0:T(8,128)(2,1)}, bf16[256,256]{1,0:T(8,128)(2,1)S(1)}, u32[]{:S(2)}, u32[]{:S(2)}) collective-permute-start(bf16[256,256]{1,0:T(8,128)(2,1)} %get-tuple-element.28.refs_3_), channel_id=1, source_target_pairs={{0,32},{32,64},{64,96},{96,0},{1,33},{33,65},{65,97},{97,1},{2,34}... | collective-permute-start | bytes 393224 | tf_op jit(solution)/shard_map/ppermute | solution.py:663
  17.9 43.3 %collective-permute-start.1 = (bf16[8,4096]{1,0:T(8,128)(2,1)}, bf16[8,4096]{1,0:T(8,128)(2,1)S(1)}, u32[]{:S(2)}, u32[]{:S(2)}) collective-permute-start(bf16[8,4096]{1,0:T(8,128)(2,1)} %get-tuple-element.33), channel_id=1, source_target_pairs={{0,32},{32,64},{64,96},{96,0},{1,33},{33,65},{65,97},{97,1},{2,34}... | collective-permute-start | bytes 196616 | tf_op jit(solution)/shard_map/ppermute | solution.py:663
  61.3 1.2 %copy-start.4 = (bf16[8,4096]{1,0:T(8,128)(2,1)}, bf16[8,4096]{1,0:T(8,128)(2,1)S(1)}, u32[]{:S(2)}) copy-start(bf16[8,4096]{1,0:T(8,128)(2,1)S(1)} %collective-permute-done.1.refs_3_) | copy-start | bytes 196612
  61.3 1.1 %copy-start.2 = (f32[8,4096]{1,0:T(8,128)}, f32[8,4096]{1,0:T(8,128)S(1)}, u32[]{:S(2)}) copy-start(f32[8,4096]{1,0:T(8,128)S(1)} %collective-permute-done.2.refs_4_) | copy-start | bytes 393220
  61.3 1.1 %copy-start.3 = (bf16[256,256]{1,0:T(8,128)(2,1)}, bf16[256,256]{1,0:T(8,128)(2,1)S(1)}, u32[]{:S(2)}) copy-start(bf16[256,256]{1,0:T(8,128)(2,1)S(1)} %collective-permute-done.3.refs_5_) | copy-start | bytes 393220
  61.3 1.1 %copy-start.1 = (f32[264,128]{1,0:T(8,128)}, f32[264,128]{1,0:T(8,128)S(1)}, u32[]{:S(2)}) copy-start(f32[264,128]{1,0:T(8,128)S(1)} %collective-permute-done.4.refs_6_) | copy-start | bytes 405508
  61.4 1.1 %copy-start = (bf16[256,2560]{1,0:T(8,128)(2,1)}, bf16[256,2560]{1,0:T(8,128)(2,1)S(1)}, u32[]{:S(2)}) copy-start(bf16[256,2560]{1,0:T(8,128)(2,1)S(1)} %collective-permute-done.refs_1_) | copy-start | bytes 3932164
  61.4 41.3 %collective-permute-start.5 = (bf16[256,3328]{1,0:T(8,128)(2,1)}, bf16[256,3328]{1,0:T(8,128)(2,1)S(1)}, u32[]{:S(2)}, u32[]{:S(2)}) collective-permute-start(bf16[256,3328]{1,0:T(8,128)(2,1)} %get-tuple-element.44), channel_id=1, source_target_pairs={{0,32},{32,64},{64,96},{96,0},{1,33},{33,65},{65,97},{97,1},{2,34}... | collective-permute-start | bytes 5111816 | tf_op jit(solution)/shard_map/ppermute | solution.py:663

commit v4 on v3

v4 whole, which is shorter than its diff:
```python
import functools

import jax
import jax.numpy as jnp
from jax import lax
from jax.experimental import pallas as pl
from jax.experimental.pallas import tpu as pltpu
from jax.sharding import PartitionSpec as P

MESH = pl.DeviceIdType.MESH
F32 = jnp.float32
BF16 = jnp.bfloat16

ROWS = 256
STATE = 128
HEADS = 128
HEAD = 64
CONV = 4
HALO = 8
TILE = 512
CHUNK = 2048
CHIPS = 16
BATCHES = 2
LOG2E = 1.4426950408889634
epsilon = 1e-05
VMEM_LIMIT = 56 * 1024 * 1024

HEADS_HOME = 64
HEADS_BACK = 12
HEADS_EARLY = 12
HEADS_ROUND = 12
HEADS_AWAY = HEADS - HEADS_HOME
HEADS_LATE = HEADS_AWAY - HEADS_EARLY - HEADS_ROUND


def dot(a, b):
    return jnp.dot(a, b, preferred_element_type=F32)


def three_parts(x):
    first = x.astype(BF16)
    rest = x - first.astype(F32)
    second = rest.astype(BF16)
    return first, second, (rest - second.astype(F32)).astype(BF16)


def spreader(rows, width):
    head = lax.broadcasted_iota(jnp.int32, (2 * rows, width), 0) % rows
    feature = lax.broadcasted_iota(jnp.int32, (2 * rows, width), 1) // HEAD
    return (head == feature).astype(F32).astype(BF16)


def spread_heads(values, width):
    high = values.astype(BF16).astype(F32)
    both = jnp.concatenate([high, values - high], axis=0).astype(BF16)
    return lax.dot_general(
        both, spreader(values.shape[0], width), (((0,), (0,)), ((), ())), preferred_element_type=F32
    )


def project_kernel(
    first,
    x_ref,
    ws_ref,
    wt_ref,
    gain_ref,
    conv_ref,
    out_gain_ref,
    bias_ref,
    rate_ref,
    skip_ref,
    maps_ref,
    step_ref,
    step_away_ref,
    vec_ref,
    halo_ref,
    halo_away_ref,
    vec_away_ref,
    early_ref,
    late_ref,
    round_ref,
    x,
    ws,
    wt,
    edge,
    x_sems,
    w_sems,
    send,
    recv,
    late_sem,
):
    features = x.shape[1]
    away = vec_away_ref.shape[1]
    chunks = features // CHUNK
    me = lax.axis_index("ctx")
    peers = lax.axis_size("ctx")
    after, ahead = lax.rem(me + 1, peers), lax.rem(me + peers - 1, peers)
    section = lax.axis_index("pipe")
    sections = lax.axis_size("pipe")
    behind, beyond = lax.rem(section + sections - 1, sections), lax.rem(section + 1, sections)

    barrier = pltpu.get_barrier_semaphore()
    for other in (after, ahead):
        pl.semaphore_signal(barrier, inc=1, device_id={"ctx": other}, device_id_type=MESH)
    for other in (behind, beyond):
        pl.semaphore_signal(barrier, inc=1, device_id={"pipe": other}, device_id_type=MESH)

    def part(k):
        return slice(k * CHUNK, (k + 1) * CHUNK)

    x_loads = [pltpu.make_async_copy(x_ref.at[:, part(k)], x.at[:, part(k)], x_sems.at[k]) for k in range(chunks)]
    w_loads = [
        (
            pltpu.make_async_copy(ws_ref.at[part(k), :], ws.at[part(k), :], w_sems.at[2 * k]),
            pltpu.make_async_copy(wt_ref.at[part(k), :], wt.at[part(k), :], w_sems.at[2 * k + 1]),
        )
        for k in range(chunks)
    ]
    second = first + early_ref.shape[1]
    third = second + late_ref.shape[1]
    early_copy = pltpu.make_async_remote_copy(
        x_ref.at[:, first:second], early_ref, send.at[0], recv.at[0], {"pipe": beyond}, MESH
    )
    round_copy = pltpu.make_async_remote_copy(
        x_ref.at[:, third:], round_ref, send.at[1], recv.at[1], {"pipe": behind}, MESH
    )
    edge_copy = pltpu.make_async_remote_copy(
        x_ref.at[ROWS - 16 :, :], edge, send.at[2], recv.at[2], {"ctx": after}, MESH
    )
    vec_copy = pltpu.make_async_remote_copy(
        vec_ref.at[:, first:], vec_away_ref, send.at[3], recv.at[3], {"pipe": beyond}, MESH
    )
    late_copy = pltpu.make_async_copy(x.at[:, second:third], late_ref, late_sem)

    for load in x_loads:
        load.start()
    for pair in w_loads:
        for load in pair:
            load.start()
    pl.semaphore_wait(barrier, 4)
    early_copy.start()
    round_copy.start()
    edge_copy.start()

    vec_ref[:4, :] = conv_ref[...]
    vec_ref[4:5, :] = gain_ref[...]
    vec_ref[5:6, :] = out_gain_ref[...]
    vec_ref[6:8, :] = jnp.zeros((2, features), F32)
    vec_copy.start()

    total = jnp.zeros((ROWS, 128), F32)
    for k in range(chunks):
        x_loads[k].wait()
        for i in range(k * CHUNK, (k + 1) * CHUNK, 512):
            square = x[:, i : i + 512].astype(F32)
            square = square * square
            total = total + (square[:, :128] + square[:, 128:256]) + (square[:, 256:384] + square[:, 384:])
    late_copy.start()
    scale = lax.rsqrt(jnp.sum(total, axis=-1, keepdims=True) * (1.0 / features) + epsilon)

    maps = jnp.zeros((ROWS, 2 * STATE), F32)
    step = jnp.zeros((ROWS, HEADS), F32)
    for k in range(chunks):
        for load in w_loads[k]:
            load.wait()
        normed = (x[:, part(k)].astype(F32) * scale * gain_ref[:, part(k)]).astype(BF16)
        maps = maps + dot(normed, ws[part(k), :])
        step = step + dot(normed, wt[part(k), :])
    maps_ref[...] = maps.astype(BF16)
    step = jax.nn.softplus(step + bias_ref[...]).T
    flat = jnp.broadcast_to(scale, (ROWS, 128)).T[:1, :]
    home = step_ref.shape[0] - 8
    for ref, start, stop in ((step_ref, 0, home), (step_away_ref, home, HEADS)):
        ref[: stop - start, :] = step[start:stop, :]
        pad = jnp.zeros((1, ROWS - (stop - start)), F32)
        rate = jnp.concatenate([rate_ref[:, start:stop], pad], axis=1)
        skip = jnp.concatenate([skip_ref[:, start:stop], pad], axis=1)
        ref[stop - start :, :] = jnp.concatenate([flat, rate, skip, jnp.zeros((5, ROWS), F32)], axis=0)

    edge_copy.wait()
    rows = edge[...].astype(F32)[16 - HALO :, :]
    meansq = jnp.sum(rows * rows, axis=-1, keepdims=True) * (1.0 / features)
    rows = rows * lax.rsqrt(meansq + epsilon) * gain_ref[...]
    rows = jnp.where(me == 0, jnp.zeros_like(rows), rows).astype(BF16)
    halo_ref[...] = rows
    halo_away_ref[...] = rows[:, features - away :]
    late_copy.wait()
    vec_copy.wait()
    early_copy.wait()
    round_copy.wait()


def project(x, proj_state, proj_step, gain, conv, out_gain, bias, rate, skip, widths, collective_id):
    features = x.shape[1]
    away = sum(widths)
    chunks = features // CHUNK
    any_ = pl.BlockSpec(memory_space=pl.ANY)
    vmem = pl.BlockSpec(memory_space=pltpu.VMEM)
    dma = pltpu.SemaphoreType.DMA
    return pl.pallas_call(
        functools.partial(project_kernel, features - away),
        in_specs=[any_] * 3 + [vmem] * 6,
        out_specs=[vmem] * 6 + [any_] * 4,
        out_shape=[
            jax.ShapeDtypeStruct((ROWS, 2 * STATE), BF16),
            jax.ShapeDtypeStruct((HEADS - away // HEAD + 8, ROWS), F32),
            jax.ShapeDtypeStruct((away // HEAD + 8, ROWS), F32),
            jax.ShapeDtypeStruct((8, features), F32),
            jax.ShapeDtypeStruct((HALO, features), BF16),
            jax.ShapeDtypeStruct((HALO, away), BF16),
            jax.ShapeDtypeStruct((8, away), F32),
        ]
        + [jax.ShapeDtypeStruct((ROWS, columns), BF16) for columns in widths],
        scratch_shapes=[
            pltpu.VMEM(x.shape, BF16),
            pltpu.VMEM(proj_state.shape, BF16),
            pltpu.VMEM(proj_step.shape, BF16),
            pltpu.VMEM((16, features), BF16),
            dma((chunks,)),
            dma((2 * chunks,)),
            dma((4,)),
            dma((4,)),
            dma,
        ],
        compiler_params=pltpu.CompilerParams(
            vmem_limit_bytes=VMEM_LIMIT, collective_id=collective_id, has_side_effects=True
        ),
        cost_estimate=pl.CostEstimate(
            flops=2 * ROWS * features * 3 * STATE, bytes_accessed=36 << 20, transcendentals=0
        ),
        name="project",
    )(x, proj_state, proj_step, gain, conv, out_gain, bias, rate, skip)


def group_kernel(pieces, hops, outs, *refs):
    refs = list(refs)

    def take(n):
        taken = refs[:n]
        del refs[:n]
        return taken

    x_refs = take(len(pieces))
    shared = take(4)
    relay_in = take(1)[0]
    out_refs = take(len(outs))
    relay_out = take(1)[0]
    group_body(pieces, hops, outs, x_refs, *shared, relay_in, out_refs, relay_out, *refs)


def group_body(
    pieces,
    hops,
    outs,
    x_refs,
    halo_ref,
    vec_ref,
    maps_ref,
    step_ref,
    relay_in,
    out_refs,
    relay_out,
    relay_slots,
    relay_send,
    relay_recv,
    out_ref,
    out_sems,
    x_ref,
    x_sems,
    cum_heads,
    weight_heads,
    enter_heads,
    skip_heads,
    pair_heads,
    chip_heads,
    closing,
    scale,
    scores,
    write_flat,
    inner_ref,
    within_ref,
    fresh,
    peer,
    peer_closing,
    total,
    total_closing,
    got,
    got_closing,
    before,
    entering,
    mine,
    theirs,
    landed,
    pair_send,
    pair_recv,
    send1,
    recv1,
    send2,
    recv2,
    send3,
    recv3,
):
    features = x_ref.shape[1]
    heads = features // HEAD
    batch = features // BATCHES
    half, quarter = batch // 2, batch // 4
    batch_tiles = batch // TILE
    half_tiles = batch_tiles // 2
    in_tile = TILE // HEAD
    me = lax.axis_index("ctx")
    core = lax.rem(me, 2)
    chip = me // 2
    partner = chip * 2 + (1 - core)

    def device(index):
        return {"ctx": index}

    section = lax.axis_index("pipe")
    sections = lax.axis_size("pipe")
    behind, ahead = lax.rem(section + sections - 1, sections), lax.rem(section + 1, sections)

    def hop(k):
        source = relay_in if k == 0 else relay_slots.at[k - 1]
        return pltpu.make_async_remote_copy(
            source, relay_slots.at[k], relay_send.at[k], relay_recv.at[k], {"pipe": behind}, MESH
        )

    def pass_on(k):
        if k > 0:
            hop(k - 1).wait_recv()
        hop(k).start()

    def tile_columns(i):
        return pl.ds(pl.multiple_of(i * TILE, TILE), TILE)

    def tile_heads(i):
        return pl.ds(pl.multiple_of(i * in_tile, in_tile), in_tile)

    barrier = pltpu.get_barrier_semaphore()
    pl.semaphore_signal(barrier, inc=1, device_id=device(partner), device_id_type=MESH)

    def greet(d, carry):
        other = lax.rem(chip + d, CHIPS) * 2 + core
        pl.semaphore_signal(barrier, inc=1, device_id=device(other), device_id_type=MESH)
        return carry

    lax.fori_loop(1, CHIPS, greet, 0)
    for other in (behind, ahead):
        pl.semaphore_signal(barrier, inc=1, device_id={"pipe": other}, device_id_type=MESH)

    loads = []
    for k, width in enumerate(pieces):
        start = sum(pieces[:k])
        load = pltpu.make_async_copy(
            x_refs[k].at[:, :width], x_ref.at[:, start : start + width], x_sems.at[k]
        )
        load.start()
        loads.append(load)

    step = step_ref[:heads, :]
    extra = step_ref[heads:, :].T
    log_decay = -step * extra[:heads, 1:2]
    row = lax.broadcasted_iota(jnp.int32, (ROWS, ROWS), 0)
    column = lax.broadcasted_iota(jnp.int32, (ROWS, ROWS), 1)
    upper = (row <= column).astype(F32).astype(BF16)
    part1, part2, part3 = three_parts(log_decay)
    cumulative = dot(part3, upper) + dot(part2, upper) + dot(part1, upper)
    last = cumulative[:, ROWS - 1 :]
    cum_heads[...] = cumulative * LOG2E
    weight_heads[...] = jnp.exp(last - cumulative) * step
    enter_heads[...] = jnp.exp(cumulative)
    closing[...] = jnp.concatenate(
        [jnp.broadcast_to(last, (heads, 128)), jnp.zeros((HEADS - heads, 128), F32)], axis=0
    ).T[:8, :]
    skip_heads[...] = jnp.broadcast_to(extra[:heads, 2:3], (heads, 128))
    scale[...] = jnp.broadcast_to(extra[:, 0:1], (ROWS, 128))
    write_flat[...] = maps_ref[:, :STATE].astype(F32).T.astype(BF16)

    for load in loads:
        load.wait()

    def fresh_tile(i):
        columns = tile_columns(i)
        normed = (x_ref[:, columns].astype(F32) * scale[:, :1] * vec_ref[4:5, columns]).astype(BF16)
        normed = jnp.concatenate([halo_ref[:, columns].astype(F32), normed.astype(F32)], axis=0)
        shifted = pltpu.roll(normed, 1, 0)
        early = vec_ref[1:2, columns] * normed + vec_ref[0:1, columns] * shifted
        conv = vec_ref[3:4, columns] * normed[HALO:] + vec_ref[2:3, columns] * shifted[HALO:]
        conv = conv + pltpu.roll(early, 2, 0)[HALO:]
        conv = conv * 0.5
        inner = (conv + conv * jnp.tanh(conv)).astype(BF16)
        inner_ref[:, columns] = inner
        spread = spread_heads(weight_heads[tile_heads(i), :], TILE)
        weighted = (inner.astype(F32) * spread).astype(BF16)
        fresh[:, columns] = dot(write_flat[...], weighted).astype(BF16)

    def within_tile(i):
        columns = tile_columns(i)
        inner = inner_ref[:, columns].astype(F32)
        stepped = (inner * spread_heads(step_ref[tile_heads(i), :], TILE)).astype(BF16)
        cum = cum_heads[tile_heads(i), :]
        cum_columns = cum.T
        top, bottom = scores[:128, :128], scores[128:, :]
        lane = lax.broadcasted_iota(jnp.int32, (ROWS, 128), 1)
        for pair in range(TILE // 128):
            values = stepped[:, pair * 128 : (pair + 1) * 128]
            upper = lower = None
            for side in range(2):
                h = pair * 2 + side
                column = cum_columns[:, h : h + 1]
                row = cum[h : h + 1, :]
                own = jnp.where((lane >= HEAD) == (side == 1), values, jnp.zeros_like(values))
                mix0 = (jnp.exp2(jnp.minimum(column[:128] - row[:, :128], 0.0)) * top).astype(BF16)
                mix1 = (jnp.exp2(jnp.minimum(column[128:] - row, 0.0)) * bottom).astype(BF16)
                up, low = dot(mix0, own[:128]), dot(mix1, own)
                upper = up if upper is None else upper + up
                lower = low if lower is None else lower + low
            at = pl.ds(pl.multiple_of(i * TILE + pair * 128, 128), 128)
            within_ref[:128, at] = upper
            within_ref[128:, at] = lower

    def finish_tile(i, state):
        columns = tile_columns(i)
        inner = inner_ref[:, columns].astype(F32)
        carried = dot(maps_ref[:, STATE:], state) * spread_heads(enter_heads[tile_heads(i), :], TILE)
        skip = spread_heads(skip_heads[tile_heads(i), :8], TILE)[0:1, :]
        output = within_ref[:, columns] + carried + skip * inner
        square = (output * output).astype(BF16)
        a = lax.broadcasted_iota(jnp.int32, (256, 256), 0) // HEAD
        b = lax.broadcasted_iota(jnp.int32, (256, 256), 1) // HEAD
        same = (a == b).astype(F32).astype(BF16)
        sums = jnp.concatenate(
            [dot(square[:, k * 256 : (k + 1) * 256], same) for k in range(TILE // 256)], axis=1
        )
        normed = output * lax.rsqrt(sums * (1.0 / HEAD) + epsilon)
        out_ref[:, columns] = (x_ref[:, columns].astype(F32) + normed * vec_ref[5:6, columns]).astype(BF16)

    def run(body, start, stop):
        def one(i, carry):
            body(i)
            return carry

        lax.fori_loop(start, stop, one, 0)

    is_first = core == 0

    def columns_of(b, which, width):
        return pl.ds(pl.multiple_of(b * batch + which * width, 128), width)

    def half_tile(b, which, j):
        return b * batch_tiles + which * half_tiles + j

    def place(of):
        return (
            pl.ds(pl.multiple_of(lax.rem(of, 8) * 16, 16), 16),
            pl.ds(pl.multiple_of((of // 8) * quarter, 128), quarter),
        )

    def pair_copy(b):
        return pltpu.make_async_remote_copy(
            fresh.at[:, columns_of(b, 1 - core, half)], peer.at[b], pair_send.at[b], pair_recv.at[b], device(partner), MESH
        )

    def back_pair_copy(b):
        return pltpu.make_async_remote_copy(
            theirs.at[b], landed.at[b], pair_send.at[BATCHES + b], pair_recv.at[BATCHES + b], device(partner), MESH
        )

    closing_pair_copy = pltpu.make_async_remote_copy(
        closing, peer_closing, pair_send.at[2 * BATCHES], pair_recv.at[2 * BATCHES], device(partner), MESH
    )

    def own_states(b):
        own = fresh[:, columns_of(b, core, half)].astype(F32)
        other = peer[b].astype(F32)
        return jnp.where(is_first, own, other), jnp.where(is_first, other, own)

    def pair_decays(b):
        first = pl.multiple_of((b * batch + core * half) // HEAD, 8)
        return spread_heads(pair_heads[pl.ds(first, half // HEAD), :16], half)

    def combine(b):
        state0, state1 = own_states(b)
        total[b] = (pair_decays(b)[8:9, :] * state0 + state1).astype(BF16)

    def state_copy(b, to):
        rows, columns = place(to)
        return pltpu.make_async_remote_copy(
            total.at[b, rows, columns], got.at[b, chip], send1.at[b], recv1.at[b], device(to * 2 + core), MESH
        )

    def closing_copy(to):
        return pltpu.make_async_remote_copy(
            total_closing, got_closing.at[chip], send2, recv2, device(to * 2 + core), MESH
        )

    def back_copy(b, to):
        rows, columns = place(chip)
        return pltpu.make_async_remote_copy(
            before.at[b, to], entering.at[b, rows, columns], send3.at[b], recv3.at[b], device(to * 2 + core), MESH
        )

    def send_states(b):
        def one(d):
            to = lax.rem(chip + d, CHIPS)
            if b == 0:
                closing_copy(to).start()
            state_copy(b, to).start()

        run(one, 1, CHIPS)
        rows, columns = place(chip)
        got[b, chip] = total[b, rows, columns]

    def all_of(ref, send, recv):
        pieces = ref.at[: CHIPS - 1]
        return pltpu.make_async_remote_copy(pieces, pieces, send, recv, device(partner), MESH)

    def scan_states(b):
        all_of(got.at[b], send1.at[b], recv1.at[b]).wait_recv()
        if b == 0:
            all_of(got_closing, send2, recv2).wait_recv()
            chip_heads[:, :CHIPS] = jnp.exp(got_closing[:, 0, :]).T
        first = pl.multiple_of((b * batch + core * half) // HEAD + (chip // 8) * (quarter // HEAD), 8)
        decays = spread_heads(chip_heads[pl.ds(first, quarter // HEAD), :CHIPS], quarter)
        state = jnp.zeros((16, quarter), F32)
        for k in range(CHIPS):
            before[b, k] = state.astype(BF16)
            if k < CHIPS - 1:
                state = decays[k : k + 1, :] * state + got[b, k].astype(F32)

    def send_back(b):
        run(lambda d: back_copy(b, lax.rem(chip + d, CHIPS)).start(), 1, CHIPS)
        rows, columns = place(chip)
        entering[b, rows, columns] = before[b, chip]

    def take_back(b):
        all_of(before.at[b], send3.at[b], recv3.at[b]).wait_recv()
        for_first = entering[b]
        for_second = (pair_decays(b)[0:1, :] * for_first.astype(F32) + own_states(b)[0]).astype(BF16)
        theirs[b] = jnp.where(is_first, for_second, for_first)
        back_pair_copy(b).start()
        mine[b] = jnp.where(is_first, for_first, for_second)

    def finish_half(b, which, states):
        run(lambda j: finish_tile(half_tile(b, which, j), states[b, :, tile_columns(j)]), 0, half_tiles)

    def fresh_half(b, which):
        run(lambda j: fresh_tile(half_tile(b, which, j)), 0, half_tiles)

    cuts = sorted({0, batch, *(sum(outs[: k + 1]) for k in range(len(outs)))})
    stores = []
    for n, (start, stop) in enumerate(zip(cuts, cuts[1:])):
        k = sum(sum(outs[: i + 1]) <= start for i in range(len(outs)))
        at = start - sum(outs[:k])
        stores.append(
            pltpu.make_async_copy(
                out_ref.at[:, start:stop], out_refs[k].at[:, at : at + stop - start], out_sems.at[n]
            )
        )

    fresh_half(0, 1 - core)
    pl.semaphore_wait(barrier, CHIPS + 2)
    pair_copy(0).start()
    pass_on(0)
    closing_pair_copy.start()
    fresh_half(0, core)
    fresh_half(1, 1 - core)
    pair_copy(1).start()
    closing_pair_copy.wait()
    closing0 = jnp.where(is_first, closing[...], peer_closing[...])
    closing1 = jnp.where(is_first, peer_closing[...], closing[...])
    pair_heads[:, :16] = jnp.exp(jnp.concatenate([closing0, closing1], axis=0)).T
    total_closing[...] = closing0 + closing1
    got_closing[chip] = total_closing[...]
    pair_copy(0).wait()
    combine(0)
    send_states(0)
    fresh_half(1, core)
    pair_copy(1).wait()
    combine(1)
    send_states(1)
    if hops == 3:
        pass_on(1)
    scores[...] = jnp.where(row >= column, dot(maps_ref[:, STATE:], write_flat[...]), 0.0)
    run(within_tile, 0, batch_tiles)
    scan_states(0)
    send_back(0)
    if hops == 2:
        pass_on(1)
    run(within_tile, batch_tiles, batch_tiles + half_tiles)
    scan_states(1)
    send_back(1)
    if hops == 3:
        pass_on(2)
    run(within_tile, batch_tiles + half_tiles, 2 * batch_tiles)
    take_back(0)
    finish_half(0, core, mine)
    back_pair_copy(0).wait()
    finish_half(0, 1 - core, landed)
    stores[0].start()
    take_back(1)
    finish_half(1, core, mine)
    back_pair_copy(1).wait()
    finish_half(1, 1 - core, landed)
    for store in stores[1:]:
        store.start()
    all_of(got_closing, send2, recv2).wait_send()
    for b in range(BATCHES):
        all_of(got.at[b], send1.at[b], recv1.at[b]).wait_send()
        all_of(before.at[b], send3.at[b], recv3.at[b]).wait_send()
    hop(hops - 1).wait_recv()
    last = pltpu.make_async_copy(relay_slots.at[hops - 1], relay_out, out_sems.at[len(outs) + 1])
    last.start()
    for k in range(hops):
        hop(k).wait_send()
    for store in stores + [last]:
        store.wait()


def group(pieces, xs, halo, vec, maps, step, relay, hops, outs, collective_id):
    features = sum(pieces)
    heads = features // HEAD
    half, quarter = features // BATCHES // 2, features // BATCHES // 4
    corner = lambda i: (0, 0)
    dma = pltpu.SemaphoreType.DMA
    vmem = pltpu.VMEM
    return pl.pallas_call(
        functools.partial(group_kernel, pieces, hops, outs),
        out_shape=[jax.ShapeDtypeStruct((ROWS, columns), BF16) for columns in outs]
        + [jax.ShapeDtypeStruct(array.shape, array.dtype) for array in (relay,)],
        grid=(1,),
        in_specs=[pl.BlockSpec(memory_space=pl.ANY)] * len(pieces)
        + [
            pl.BlockSpec((HALO, features), corner),
            pl.BlockSpec((vec.shape[0], features), corner),
            pl.BlockSpec((ROWS, 2 * STATE), corner),
            pl.BlockSpec((heads + 8, ROWS), corner),
        ]
        + [pl.BlockSpec(memory_space=pl.ANY)] ,
        out_specs=[pl.BlockSpec(memory_space=pl.ANY)] * (len(outs) + 1),
        scratch_shapes=[
            vmem((hops,) + relay.shape, BF16),
            dma((hops,)),
            dma((hops,)),
            vmem((ROWS, features), BF16),
            dma((len(outs) + 2,)),
            vmem((ROWS, features), BF16),
            dma((len(pieces),)),
            vmem((heads, ROWS), F32),
            vmem((heads, ROWS), F32),
            vmem((heads, ROWS), F32),
            vmem((heads, 128), F32),
            vmem((HEADS, 128), F32),
            vmem((HEADS, 128), F32),
            vmem((8, HEADS), F32),
            vmem((ROWS, 128), F32),
            vmem((ROWS, ROWS), F32),
            vmem((STATE, ROWS), BF16),
            vmem((ROWS, features), BF16),
            vmem((ROWS, features), F32),
            vmem((STATE, features), BF16),
            vmem((BATCHES, STATE, half), BF16),
            vmem((8, HEADS), F32),
            vmem((BATCHES, STATE, half), BF16),
            vmem((8, HEADS), F32),
            vmem((BATCHES, CHIPS, 16, quarter), BF16),
            vmem((CHIPS, 8, HEADS), F32),
            vmem((BATCHES, CHIPS, 16, quarter), BF16),
            vmem((BATCHES, STATE, half), BF16),
            vmem((BATCHES, STATE, half), BF16),
            vmem((BATCHES, STATE, half), BF16),
            vmem((BATCHES, STATE, half), BF16),
            dma((2 * BATCHES + 1,)),
            dma((2 * BATCHES + 1,)),
            dma((BATCHES,)),
            dma((BATCHES,)),
            dma,
            dma,
            dma((BATCHES,)),
            dma((BATCHES,)),
        ],
        compiler_params=pltpu.CompilerParams(
            collective_id=collective_id, has_side_effects=True, vmem_limit_bytes=VMEM_LIMIT
        ),
        cost_estimate=pl.CostEstimate(
            flops=ROWS * features, bytes_accessed=ROWS * features, transcendentals=0
        ),
        name="group",
    )(*xs, halo, vec, maps, step, relay)


def widen_kernel(blocks, *refs):
    parts, out, held, loads, stores = refs[:-4], refs[-4], refs[-3], refs[-2], refs[-1]
    start = out.shape[1] - sum(width for _, _, width in blocks)
    pairs = []
    at = 0
    for k, (part, begin, width) in enumerate(blocks):
        here = held.at[:, at : at + width]
        load = pltpu.make_async_copy(parts[part].at[:, begin : begin + width], here, loads.at[k])
        store = pltpu.make_async_copy(here, out.at[:, start + at : start + at + width], stores.at[k])
        pairs.append((load, store))
        at += width
    for load, _ in pairs:
        load.start()
    for load, store in pairs:
        load.wait()
        store.start()
    for _, store in pairs:
        store.wait()


def widen(parts, width):
    blocks = []
    for k, part in enumerate(parts):
        begin = 0
        while begin < part.shape[1]:
            size = min(1024, part.shape[1] - begin)
            blocks.append((k, begin, size))
            begin += size
    dma = pltpu.SemaphoreType.DMA((len(blocks),))
    return pl.pallas_call(
        functools.partial(widen_kernel, blocks),
        in_specs=[pl.BlockSpec(memory_space=pl.ANY)] * len(parts),
        out_specs=pl.BlockSpec(memory_space=pl.ANY),
        out_shape=jax.ShapeDtypeStruct((ROWS, width), BF16),
        scratch_shapes=[pltpu.VMEM((ROWS, sum(part.shape[1] for part in parts)), BF16), dma, dma],
        compiler_params=pltpu.CompilerParams(vmem_limit_bytes=VMEM_LIMIT),
        cost_estimate=pl.CostEstimate(flops=1, bytes_accessed=ROWS * width * 2, transcendentals=0),
        name="widen",
    )(*parts)


def moved(array, by):
    peers = lax.axis_size("pipe")
    return lax.ppermute(array, "pipe", [(i, (i + by) % peers) for i in range(peers)])


def shards(
    incoming, norm_gain, proj_state, proj_step, conv_weight, decay_rate, step_bias, skip_gain, out_gain
):
    x = incoming[0]
    features = x.shape[1]
    home, back, away = HEADS_HOME * HEAD, HEADS_BACK * HEAD, HEADS_AWAY * HEAD
    early, late, round_ = HEADS_EARLY * HEAD, HEADS_LATE * HEAD, HEADS_ROUND * HEAD

    maps, step, step_away, vec, halo, halo_away, vec_away, x_early, x_late, x_round = project(
        x, proj_state[0], proj_step[0], norm_gain, conv_weight[0], out_gain, step_bias, decay_rate, skip_gain,
        (early, late, round_), 2,
    )
    x_late, halo_away, step_away, maps_away = (moved(a, 1) for a in (x_late, halo_away, step_away, maps))

    rows, rows_back, x_round = group(
        (home,), (x,), halo, vec, maps, step, x_round, 2, (home - back, back), 0
    )
    rows, x_late, halo_away, step_away, maps_away = lax.optimization_barrier(
        (rows, x_late, halo_away, step_away, maps_away)
    )
    rows_in = moved(rows, 1)

    rows_away, rows_back = group(
        (early, late, round_), (x_early, x_late, x_round), halo_away, vec_away, maps_away, step_away,
        rows_back, 3, (away,), 1,
    )
    passed = widen((rows_back, rows_away), features)
    return lax.dynamic_update_slice(passed, rows_in, (0, 0))[None]


def solution(mesh):
    return jax.shard_map(
        shards,
        mesh=mesh,
        in_specs=(
            P("pipe", "ctx", None),
            P("pipe", None),
            P("pipe", None, None),
            P("pipe", None, None),
            P("pipe", None, None),
            P("pipe", None),
            P("pipe", None),
            P("pipe", None),
            P("pipe", None),
        ),
        out_specs=P("pipe", "ctx", None),
        check_vma=False,
    )
```

time: 104 us -> 98.4 us (0.946)
  Pallas kernels: 97.2 us -> 89.3 us
  waiting for transfers between devices: 0.02 us -> 2.58 us
  starting transfers between devices: 5.26 us -> 3.9 us
    pallas_call x4, Pallas kernels: 97.2 us -> 89.3 us  [the longest x2 71.7 us: group(): pl.pallas_call(functools.partial(group_kernel, pieces, hops, outs), out_s...]
    ppermute x6 -> x5, waiting for transfers between devices: 0.02 us -> 2.58 us  [moved(): lax.ppermute(array, 'pipe', [(i, (i + by) % peers) for i in range(peers)])]
    ppermute x6 -> x5, starting transfers between devices: 5.26 us -> 3.9 us  [moved(): lax.ppermute(array, 'pipe', [(i, (i + by) % peers) for i in range(peers)])]
  transfers between devices with their start and end apart: 6 -> 5, of which waited for: 0 -> 1; matrix products, arithmetic and copies ran while one was open for 0% -> 0% of each run, Pallas kernels for 80% -> 76%
where the time goes in v4:
time: 98.4 us; the launch traced here: 98 us
  Pallas kernels  89.3 us (91%)
  starting transfers between devices  3.9 us (4%)
  waiting for transfers between devices  2.58 us (3%)
  local copies, waits for them, and re-layouts  2.07 us (2%)
    pallas_call x2, Pallas kernels, group(): pl.pallas_call(functools.partial(group_kernel, pieces, hops, outs), out_s...  71.7 us
    pallas_call x1, Pallas kernels, project(): pl.pallas_call(functools.partial(project_kernel, features - away), in_spe...  15 us
    ppermute x5, starting transfers between devices, moved(): lax.ppermute(array, 'pipe', [(i, (i + by) % peers) for i in range(peers)])  3.9 us
    ppermute x5, waiting for transfers between devices, moved(): lax.ppermute(array, 'pipe', [(i, (i + by) % peers) for i in range(peers)])  2.58 us
    pallas_call x1, Pallas kernels, widen(): pl.pallas_call(functools.partial(widen_kernel, blocks), in_specs=[pl.Bloc...  2.56 us
  transfers between devices with their start and end apart: 5, of which 1 were waited for; matrix products, arithmetic and copies ran while one was open for 0% of the time, Pallas kernels for 76%

profile of v4, /device:TPU:1, one launch (start us, length us, event | category | flops | bytes accessed | tf_op | source)
XLA Modules:
  0.0 98.0 jit_solution(10838283149616229835)
XLA Ops:
  0.0 15.0 %project.1 = (bf16[256,256]{1,0:T(8,128)(2,1)}, f32[72,256]{1,0:T(8,128)}, f32[72,256]{1,0:T(8,128)}, f32[8,8192]{1,0:T(8,128)}, bf16[8,8192]{1,0:T(8,128)(2,1)}...) custom-call(bf16[256,8192]{1,0:T(8,128)(2,1)} %bitcast.7, ...), custom_call_target="tpu_custom_call" | custom-call | flops 1610612736 | bytes 37748736 | tf_op jit(solution)/shard_map/project/pallas_call | solution.py:200
  15.0 0.3 collective-permute-start
  15.3 0.1 collective-permute-start.3
  15.4 1.1 %collective-permute-start.2 = (f32[72,256]{1,0:T(8,128)}, f32[72,256]{1,0:T(8,128)S(1)}, u32[]{:S(2)}, u32[]{:S(2)}) collective-permute-start(f32[72,256]{1,0:T(8,128)} %get-tuple-element.34), channel_id=1, source_target_pairs={{0,32},{32,64},{64,96},{96,0},{1,33},{33,65},{65,97},{97,1},{2,34}... | collective-permute-start | bytes 221192 | tf_op jit(solution)/shard_map/ppermute | solution.py:735
  16.5 2.1 %collective-permute-start.1 = (bf16[8,4096]{1,0:T(8,128)(2,1)}, bf16[8,4096]{1,0:T(8,128)(2,1)S(1)}, u32[]{:S(2)}, u32[]{:S(2)}) collective-permute-start(bf16[8,4096]{1,0:T(8,128)(2,1)} %get-tuple-element.33), channel_id=1, source_target_pairs={{0,32},{32,64},{64,96},{96,0},{1,33},{33,65},{65,97},{97,1},{2,34}... | collective-permute-start | bytes 196616 | tf_op jit(solution)/shard_map/ppermute | solution.py:735
  18.6 37.8 %group.2 = (bf16[256,3328]{1,0:T(8,128)(2,1)}, bf16[256,768]{1,0:T(8,128)(2,1)}, bf16[256,768]{1,0:T(8,128)(2,1)}) custom-call(bf16[256,8192]{1,0:T(8,128)(2,1)} %bitcast.8, bf16[8,8192]{1,0:T(8,128)(2,1)} %get-tuple-element.26.refs_1_, f32[8,8192]{1,0:T(8,128)} %get-tuple-element.27.refs_2_, bf16[256,256]{1,0:T(8,128)(2,1)} %get-tuple-element.28.refs_3_, ...), custom_call_target="tpu_custom_call" | custom-call | flops 1048576 | bytes 1048576 | tf_op jit(solution)/shard_map/group/pallas_call | solution.py:627
  56.4 0.0 collective-permute-done.1.refs_3_
  56.4 0.0 copy-start.3
  56.4 0.0 collective-permute-done.2.refs_6_
  56.5 0.0 copy-start.2
  56.5 0.0 collective-permute-done.3.refs_5_
  56.5 0.0 copy-start.1
  56.5 0.0 collective-permute-done.refs_1_
  56.5 0.0 copy-start
  56.5 0.3 collective-permute-start.4
  56.8 0.2 copy-done.3
  57.1 0.1 copy-done.2
  57.1 0.1 copy-done.1
  57.2 0.4 copy-done
  57.6 33.9 %group.3 = (bf16[256,4096]{1,0:T(8,128)(2,1)}, bf16[256,768]{1,0:T(8,128)(2,1)}) custom-call(bf16[256,768]{1,0:T(8,128)(2,1)} %get-tuple-element.25.refs_0_, bf16[256,2560]{1,0:T(8,128)(2,1)} %copy-done, bf16[256,768]{1,0:T(8,128)(2,1)} %get-tuple-element.36.refs_2_, bf16[8,4096]{1,0:T(8,128)(2,1)} %copy-done.3, f32[8,4096]{1,0:T(8,128)} %get-tuple-element.38.refs_4_, ...), custom_call_target="tpu_custom_call" | custom-call | flops 1048576 | bytes 1048576 | tf_op jit(solution)/shard_map/group/pallas_call | solution.py:627
  91.5 2.6 %widen.1 = bf16[256,8192]{1,0:T(8,128)(2,1)} custom-call(bf16[256,768]{1,0:T(8,128)(2,1)} %get-tuple-element.42.refs_0_, bf16[256,4096]{1,0:T(8,128)(2,1)} %get-tuple-element.43.refs_1_), custom_call_target="tpu_custom_call" | custom-call | flops 1 | bytes 4194304 | tf_op jit(solution)/shard_map/widen/pallas_call | solution.py:721
  94.1 2.6 %collective-permute-done.4 = bf16[256,3328]{1,0:T(8,128)(2,1)S(1)} collective-permute-done((bf16[256,3328]{1,0:T(8,128)(2,1)}, bf16[256,3328]{1,0:T(8,128)(2,1)S(1)}, u32[]{:S(2)}, u32[]{:S(2)}) %collective-permute-start.4) | collective-permute-done | bytes 1703968 | tf_op jit(solution)/shard_map/ppermute | solution.py:735
  96.7 1.3 %bitcast_dynamic-update-slice_fusion = bf16[1,256,8192]{2,1,0:T(8,128)(2,1)} fusion(bf16[1,256,8192]{2,1,0:T(8,128)(2,1)} %bitcast.10, bf16[256,3328]{1,0:T(8,128)(2,1)S(1)} %collective-permute-done.4), kind=kLoop, calls=%fused_computation | loop fusion | bytes 3407872 | tf_op jit(solution)/shard_map/dynamic_update_slice | solution.py:765
Async XLA Ops:
  15.0 41.5 %collective-permute-start = (bf16[256,2560]{1,0:T(8,128)(2,1)}, bf16[256,2560]{1,0:T(8,128)(2,1)S(1)}, u32[]{:S(2)}, u32[]{:S(2)}) collective-permute-start(bf16[256,2560]{1,0:T(8,128)(2,1)} %get-tuple-element.32), channel_id=1, source_target_pairs={{0,32},{32,64},{64,96},{96,0},{1,33},{33,65},{65,97},{97,1},{2,34}... | collective-permute-start | bytes 3932168 | tf_op jit(solution)/shard_map/ppermute | solution.py:735
  15.3 41.2 %collective-permute-start.3 = (bf16[256,256]{1,0:T(8,128)(2,1)}, bf16[256,256]{1,0:T(8,128)(2,1)S(1)}, u32[]{:S(2)}, u32[]{:S(2)}) collective-permute-start(bf16[256,256]{1,0:T(8,128)(2,1)} %get-tuple-element.28.refs_3_), channel_id=1, source_target_pairs={{0,32},{32,64},{64,96},{96,0},{1,33},{33,65},{65,97},{97,1},{2,34}... | collective-permute-start | bytes 393224 | tf_op jit(solution)/shard_map/ppermute | solution.py:735
  15.4 41.1 %collective-permute-start.2 = (f32[72,256]{1,0:T(8,128)}, f32[72,256]{1,0:T(8,128)S(1)}, u32[]{:S(2)}, u32[]{:S(2)}) collective-permute-start(f32[72,256]{1,0:T(8,128)} %get-tuple-element.34), channel_id=1, source_target_pairs={{0,32},{32,64},{64,96},{96,0},{1,33},{33,65},{65,97},{97,1},{2,34}... | collective-permute-start | bytes 221192 | tf_op jit(solution)/shard_map/ppermute | solution.py:735
  16.5 39.9 %collective-permute-start.1 = (bf16[8,4096]{1,0:T(8,128)(2,1)}, bf16[8,4096]{1,0:T(8,128)(2,1)S(1)}, u32[]{:S(2)}, u32[]{:S(2)}) collective-permute-start(bf16[8,4096]{1,0:T(8,128)(2,1)} %get-tuple-element.33), channel_id=1, source_target_pairs={{0,32},{32,64},{64,96},{96,0},{1,33},{33,65},{65,97},{97,1},{2,34}... | collective-permute-start | bytes 196616 | tf_op jit(solution)/shard_map/ppermute | solution.py:735
  56.4 0.6 copy-start.3
  56.5 0.7 copy-start.2
  56.5 0.7 copy-start.1
  56.5 1.1 %copy-start = (bf16[256,2560]{1,0:T(8,128)(2,1)}, bf16[256,2560]{1,0:T(8,128)(2,1)S(1)}, u32[]{:S(2)}) copy-start(bf16[256,2560]{1,0:T(8,128)(2,1)S(1)} %collective-permute-done.refs_1_) | copy-start | bytes 3932164
  56.5 40.1 %collective-permute-start.4 = (bf16[256,3328]{1,0:T(8,128)(2,1)}, bf16[256,3328]{1,0:T(8,128)(2,1)S(1)}, u32[]{:S(2)}, u32[]{:S(2)}) collective-permute-start(bf16[256,3328]{1,0:T(8,128)(2,1)} %get-tuple-element.44), channel_id=1, source_target_pairs={{0,32},{32,64},{64,96},{96,0},{1,33},{33,65},{65,97},{97,1},{2,34}... | collective-permute-start | bytes 5111816 | tf_op jit(solution)/shard_map/ppermute | solution.py:735

commit v5 on v4

--- a/solution.py
+++ b/solution.py
@@ -28,7 +28,7 @@
 HEADS_HOME = 64
 HEADS_BACK = 12
 HEADS_EARLY = 12
-HEADS_ROUND = 12
+HEADS_ROUND = 14
 HEADS_AWAY = HEADS - HEADS_HOME
 HEADS_LATE = HEADS_AWAY - HEADS_EARLY - HEADS_ROUND
 
@@ -70,11 +70,10 @@
     rate_ref,
     skip_ref,
     maps_ref,
+    maps_away_ref,
     step_ref,
     step_away_ref,
     vec_ref,
-    halo_ref,
-    halo_away_ref,
     vec_away_ref,
     early_ref,
     late_ref,
@@ -127,26 +126,41 @@
     edge_copy = pltpu.make_async_remote_copy(
         x_ref.at[ROWS - 16 :, :], edge, send.at[2], recv.at[2], {"ctx": after}, MESH
     )
+    core = lax.rem(me, 2)
+    half = away // 2
+    mine = pl.ds(pl.multiple_of(core * half, 128), half)
     vec_copy = pltpu.make_async_remote_copy(
-        vec_ref.at[:, first:], vec_away_ref, send.at[3], recv.at[3], {"pipe": beyond}, MESH
+        vec_ref.at[:, pl.ds(pl.multiple_of(first + core * half, 128), half)],
+        vec_away_ref.at[:, mine],
+        send.at[3],
+        recv.at[3],
+        {"pipe": beyond},
+        MESH,
+    )
+    vec_pair_copy = pltpu.make_async_remote_copy(
+        vec_away_ref.at[:, mine],
+        vec_away_ref.at[:, mine],
+        send.at[4],
+        recv.at[4],
+        {"ctx": me + 1 - 2 * core},
+        MESH,
     )
     late_copy = pltpu.make_async_copy(x.at[:, second:third], late_ref, late_sem)
 
+    vec_ref[:4, :] = conv_ref[...]
+    vec_ref[4:5, :] = gain_ref[...]
+    vec_ref[5:6, :] = out_gain_ref[...]
+    vec_ref[6:8, :] = jnp.zeros((2, features), F32)
     for load in x_loads:
         load.start()
     for pair in w_loads:
         for load in pair:
             load.start()
     pl.semaphore_wait(barrier, 4)
+    vec_copy.start()
     early_copy.start()
     round_copy.start()
     edge_copy.start()
-
-    vec_ref[:4, :] = conv_ref[...]
-    vec_ref[4:5, :] = gain_ref[...]
-    vec_ref[5:6, :] = out_gain_ref[...]
-    vec_ref[6:8, :] = jnp.zeros((2, features), F32)
-    vec_copy.start()
 
     total = jnp.zeros((ROWS, 128), F32)
     for k in range(chunks):
@@ -158,6 +172,9 @@
     late_copy.start()
     scale = lax.rsqrt(jnp.sum(total, axis=-1, keepdims=True) * (1.0 / features) + epsilon)
 
+    vec_copy.wait()
+    vec_pair_copy.start()
+
     maps = jnp.zeros((ROWS, 2 * STATE), F32)
     step = jnp.zeros((ROWS, HEADS), F32)
     for k in range(chunks):
@@ -166,7 +183,8 @@
         normed = (x[:, part(k)].astype(F32) * scale * gain_ref[:, part(k)]).astype(BF16)
         maps = maps + dot(normed, ws[part(k), :])
         step = step + dot(normed, wt[part(k), :])
-    maps_ref[...] = maps.astype(BF16)
+    for ref in (maps_ref, maps_away_ref):
+        ref[:, : 2 * STATE] = maps.astype(BF16)
     step = jax.nn.softplus(step + bias_ref[...]).T
     flat = jnp.broadcast_to(scale, (ROWS, 128)).T[:1, :]
     home = step_ref.shape[0] - 8
@@ -181,11 +199,13 @@
     rows = edge[...].astype(F32)[16 - HALO :, :]
     meansq = jnp.sum(rows * rows, axis=-1, keepdims=True) * (1.0 / features)
     rows = rows * lax.rsqrt(meansq + epsilon) * gain_ref[...]
-    rows = jnp.where(me == 0, jnp.zeros_like(rows), rows).astype(BF16)
-    halo_ref[...] = rows
-    halo_away_ref[...] = rows[:, features - away :]
+    rows = jnp.where(me == 0, jnp.zeros_like(rows), rows)
+    for ref, start in ((maps_ref, 0), (maps_away_ref, features - away)):
+        ref[:, 2 * STATE :] = jnp.concatenate(
+            [rows[:, start + i * 128 : start + (i + 1) * 128] for i in range(ROWS // HALO)], axis=0
+        ).astype(BF16)
     late_copy.wait()
-    vec_copy.wait()
+    vec_pair_copy.wait()
     early_copy.wait()
     round_copy.wait()
 
@@ -200,14 +220,13 @@
     return pl.pallas_call(
         functools.partial(project_kernel, features - away),
         in_specs=[any_] * 3 + [vmem] * 6,
-        out_specs=[vmem] * 6 + [any_] * 4,
+        out_specs=[vmem] * 5 + [any_] * 4,
         out_shape=[
-            jax.ShapeDtypeStruct((ROWS, 2 * STATE), BF16),
+            jax.ShapeDtypeStruct((ROWS, 2 * STATE + 128), BF16),
+            jax.ShapeDtypeStruct((ROWS, 2 * STATE + 128), BF16),
             jax.ShapeDtypeStruct((HEADS - away // HEAD + 8, ROWS), F32),
             jax.ShapeDtypeStruct((away // HEAD + 8, ROWS), F32),
             jax.ShapeDtypeStruct((8, features), F32),
-            jax.ShapeDtypeStruct((HALO, features), BF16),
-            jax.ShapeDtypeStruct((HALO, away), BF16),
             jax.ShapeDtypeStruct((8, away), F32),
         ]
         + [jax.ShapeDtypeStruct((ROWS, columns), BF16) for columns in widths],
@@ -218,8 +237,8 @@
             pltpu.VMEM((16, features), BF16),
             dma((chunks,)),
             dma((2 * chunks,)),
-            dma((4,)),
-            dma((4,)),
+            dma((5,)),
+            dma((5,)),
             dma,
         ],
         compiler_params=pltpu.CompilerParams(
@@ -241,7 +260,7 @@
         return taken
 
     x_refs = take(len(pieces))
-    shared = take(4)
+    shared = take(3)
     relay_in = take(1)[0]
     out_refs = take(len(outs))
     relay_out = take(1)[0]
@@ -253,7 +272,6 @@
     hops,
     outs,
     x_refs,
-    halo_ref,
     vec_ref,
     maps_ref,
     step_ref,
@@ -382,7 +400,10 @@
     def fresh_tile(i):
         columns = tile_columns(i)
         normed = (x_ref[:, columns].astype(F32) * scale[:, :1] * vec_ref[4:5, columns]).astype(BF16)
-        normed = jnp.concatenate([halo_ref[:, columns].astype(F32), normed.astype(F32)], axis=0)
+        parts = TILE // 128
+        halo = maps_ref[pl.ds(pl.multiple_of(i * HALO * parts, HALO * parts), HALO * parts), 2 * STATE :].astype(F32)
+        halo = jnp.concatenate([halo[k * HALO : (k + 1) * HALO] for k in range(parts)], axis=1)
+        normed = jnp.concatenate([halo, normed.astype(F32)], axis=0)
         shifted = pltpu.roll(normed, 1, 0)
         early = vec_ref[1:2, columns] * normed + vec_ref[0:1, columns] * shifted
         conv = vec_ref[3:4, columns] * normed[HALO:] + vec_ref[2:3, columns] * shifted[HALO:]
@@ -422,7 +443,7 @@
     def finish_tile(i, state):
         columns = tile_columns(i)
         inner = inner_ref[:, columns].astype(F32)
-        carried = dot(maps_ref[:, STATE:], state) * spread_heads(enter_heads[tile_heads(i), :], TILE)
+        carried = dot(maps_ref[:, STATE : 2 * STATE], state) * spread_heads(enter_heads[tile_heads(i), :], TILE)
         skip = spread_heads(skip_heads[tile_heads(i), :8], TILE)[0:1, :]
         output = within_ref[:, columns] + carried + skip * inner
         square = (output * output).astype(BF16)
@@ -507,7 +528,8 @@
                 closing_copy(to).start()
             state_copy(b, to).start()
 
-        run(one, 1, CHIPS)
+        for d in range(1, CHIPS):
+            one(d)
         rows, columns = place(chip)
         got[b, chip] = total[b, rows, columns]
 
@@ -529,7 +551,8 @@
                 state = decays[k : k + 1, :] * state + got[b, k].astype(F32)
 
     def send_back(b):
-        run(lambda d: back_copy(b, lax.rem(chip + d, CHIPS)).start(), 1, CHIPS)
+        for d in range(1, CHIPS):
+            back_copy(b, lax.rem(chip + d, CHIPS)).start()
         rows, columns = place(chip)
         entering[b, rows, columns] = before[b, chip]
 
@@ -581,7 +604,7 @@
     send_states(1)
     if hops == 3:
         pass_on(1)
-    scores[...] = jnp.where(row >= column, dot(maps_ref[:, STATE:], write_flat[...]), 0.0)
+    scores[...] = jnp.where(row >= column, dot(maps_ref[:, STATE : 2 * STATE], write_flat[...]), 0.0)
     run(within_tile, 0, batch_tiles)
     scan_states(0)
     send_back(0)
@@ -617,7 +640,7 @@
         store.wait()
 
 
-def group(pieces, xs, halo, vec, maps, step, relay, hops, outs, collective_id):
+def group(pieces, xs, vec, maps, step, relay, hops, outs, collective_id):
     features = sum(pieces)
     heads = features // HEAD
     half, quarter = features // BATCHES // 2, features // BATCHES // 4
@@ -631,9 +654,8 @@
         grid=(1,),
         in_specs=[pl.BlockSpec(memory_space=pl.ANY)] * len(pieces)
         + [
-            pl.BlockSpec((HALO, features), corner),
             pl.BlockSpec((vec.shape[0], features), corner),
-            pl.BlockSpec((ROWS, 2 * STATE), corner),
+            pl.BlockSpec(maps.shape, corner),
             pl.BlockSpec((heads + 8, ROWS), corner),
         ]
         + [pl.BlockSpec(memory_space=pl.ANY)] ,
@@ -686,7 +708,7 @@
             flops=ROWS * features, bytes_accessed=ROWS * features, transcendentals=0
         ),
         name="group",
-    )(*xs, halo, vec, maps, step, relay)
+    )(*xs, vec, maps, step, relay)
 
 
 def widen_kernel(blocks, *refs):
@@ -743,22 +765,20 @@
     home, back, away = HEADS_HOME * HEAD, HEADS_BACK * HEAD, HEADS_AWAY * HEAD
     early, late, round_ = HEADS_EARLY * HEAD, HEADS_LATE * HEAD, HEADS_ROUND * HEAD
 
-    maps, step, step_away, vec, halo, halo_away, vec_away, x_early, x_late, x_round = project(
+    maps, maps_away, step, step_away, vec, vec_away, x_early, x_late, x_round = project(
         x, proj_state[0], proj_step[0], norm_gain, conv_weight[0], out_gain, step_bias, decay_rate, skip_gain,
         (early, late, round_), 2,
     )
-    x_late, halo_away, step_away, maps_away = (moved(a, 1) for a in (x_late, halo_away, step_away, maps))
+    x_late, step_away, maps_away = (moved(a, 1) for a in (x_late, step_away, maps_away))
 
     rows, rows_back, x_round = group(
-        (home,), (x,), halo, vec, maps, step, x_round, 2, (home - back, back), 0
-    )
-    rows, x_late, halo_away, step_away, maps_away = lax.optimization_barrier(
-        (rows, x_late, halo_away, step_away, maps_away)
-    )
+        (home,), (x,), vec, maps, step, x_round, 2, (home - back, back), 0
+    )
+    rows, x_late, step_away, maps_away = lax.optimization_barrier((rows, x_late, step_away, maps_away))
     rows_in = moved(rows, 1)
 
     rows_away, rows_back = group(
-        (early, late, round_), (x_early, x_late, x_round), halo_away, vec_away, maps_away, step_away,
+        (early, late, round_), (x_early, x_late, x_round), vec_away, maps_away, step_away,
         rows_back, 3, (away,), 1,
     )
     passed = widen((rows_back, rows_away), features)

time: 98.4 us -> 95.4 us (0.970)
  Pallas kernels: 89.3 us -> 87.6 us
    pallas_call x2, Pallas kernels: 71.7 us -> 69.4 us  [group(): pl.pallas_call(functools.partial(group_kernel, pieces, hops, outs), out_s...]
    ppermute x5 -> x4, waiting for transfers between devices: 2.58 us -> 1.63 us  [moved(): lax.ppermute(array, 'pipe', [(i, (i + by) % peers) for i in range(peers)])]
    ppermute x5 -> x4, starting transfers between devices: 3.9 us -> 3.59 us  [moved(): lax.ppermute(array, 'pipe', [(i, (i + by) % peers) for i in range(peers)])]
  transfers between devices with their start and end apart: 5 -> 4, of which waited for: 1 -> 1; matrix products, arithmetic and copies ran while one was open for 0% -> 0% of each run, Pallas kernels for 76% -> 76%
where the time goes in v5:
time: 95.4 us; the launch traced here: 94.2 us
  Pallas kernels  87.6 us (92%)
  starting transfers between devices  3.59 us (4%)
  waiting for transfers between devices  1.63 us (2%)
  local copies, waits for them, and re-layouts  1.31 us (1%)
    pallas_call x2, Pallas kernels, group(): pl.pallas_call(functools.partial(group_kernel, pieces, hops, outs), out_s...  69.4 us
    pallas_call x1, Pallas kernels, project(): pl.pallas_call(functools.partial(project_kernel, features - away), in_spe...  15.6 us
    ppermute x4, starting transfers between devices, moved(): lax.ppermute(array, 'pipe', [(i, (i + by) % peers) for i in range(peers)])  3.59 us
    pallas_call x1, Pallas kernels, widen(): pl.pallas_call(functools.partial(widen_kernel, blocks), in_specs=[pl.Bloc...  2.56 us
  transfers between devices with their start and end apart: 4, of which 1 were waited for; matrix products, arithmetic and copies ran while one was open for 0% of the time, Pallas kernels for 76%

profile of v5, /device:TPU:1, one launch (start us, length us, event | category | flops | bytes accessed | tf_op | source)
XLA Modules:
  0.0 94.2 jit_solution(12051270158181294722)
XLA Ops:
  0.0 15.6 %project.1 = (bf16[256,384]{1,0:T(8,128)(2,1)}, bf16[256,384]{1,0:T(8,128)(2,1)}, f32[72,256]{1,0:T(8,128)}, f32[72,256]{1,0:T(8,128)}, f32[8,8192]{1,0:T(8,128)...) custom-call(bf16[256,8192]{1,0:T(8,128)(2,1)} %bitcast.7, ...), custom_call_target="tpu_custom_call" | custom-call | flops 1610612736 | bytes 37748736 | tf_op jit(solution)/shard_map/project/pallas_call | solution.py:220
  15.7 0.1 collective-permute-start
  15.7 0.2 collective-permute-start.2
  15.9 1.2 %collective-permute-start.1 = (f32[72,256]{1,0:T(8,128)}, f32[72,256]{1,0:T(8,128)S(1)}, u32[]{:S(2)}, u32[]{:S(2)}) collective-permute-start(f32[72,256]{1,0:T(8,128)} %get-tuple-element.30), channel_id=1, source_target_pairs={{0,32},{32,64},{64,96},{96,0},{1,33},{33,65},{65,97},{97,1},{2,34}... | collective-permute-start | bytes 221192 | tf_op jit(solution)/shard_map/ppermute | solution.py:757
  17.1 35.6 %group.2 = (bf16[256,3328]{1,0:T(8,128)(2,1)}, bf16[256,768]{1,0:T(8,128)(2,1)}, bf16[256,896]{1,0:T(8,128)(2,1)}) custom-call(bf16[256,8192]{1,0:T(8,128)(2,1)} %bitcast.8, f32[8,8192]{1,0:T(8,128)} %get-tuple-element.24.refs_1_, bf16[256,384]{1,0:T(8,128)(2,1)} %get-tuple-element.25.refs_2_, f32[72,256]{1,0:T(8,128)} %get-tuple-element.26.refs_3_, ...), custom_call_target="tpu_custom_call" | custom-call | flops 1048576 | bytes 1048576 | tf_op jit(solution)/shard_map/group/pallas_call | solution.py:650
  52.7 0.0 collective-permute-done.1.refs_5_
  52.7 0.0 copy-start.2
  52.8 0.0 collective-permute-done.2.refs_4_
  52.8 0.0 copy-start.1
  52.8 0.0 collective-permute-done.refs_1_
  52.8 0.0 copy-start
  52.8 2.1 %collective-permute-start.3 = (bf16[256,3328]{1,0:T(8,128)(2,1)}, bf16[256,3328]{1,0:T(8,128)(2,1)S(1)}, u32[]{:S(2)}, u32[]{:S(2)}) collective-permute-start(bf16[256,3328]{1,0:T(8,128)(2,1)} %get-tuple-element.40), channel_id=1, source_target_pairs={{0,32},{32,64},{64,96},{96,0},{1,33},{33,65},{65,97},{97,1},{2,34}... | collective-permute-start | bytes 5111816 | tf_op jit(solution)/shard_map/ppermute | solution.py:757
  54.9 0.0 copy-done.2
  54.9 0.0 copy-done.1
  54.9 0.0 copy-done
  54.9 33.8 %group.3 = (bf16[256,4096]{1,0:T(8,128)(2,1)}, bf16[256,768]{1,0:T(8,128)(2,1)}) custom-call(bf16[256,768]{1,0:T(8,128)(2,1)} %get-tuple-element.23.refs_0_, bf16[256,2432]{1,0:T(8,128)(2,1)} %copy-done, bf16[256,896]{1,0:T(8,128)(2,1)} %get-tuple-element.33.refs_2_, f32[8,4096]{1,0:T(8,128)} %get-tuple-element.34.refs_3_, bf16[256,384]{1,0:T(8,128)(2,1)} %copy-done.1, ...), custom_call_target="tpu_custom_call" | custom-call | flops 1048576 | bytes 1048576 | tf_op jit(solution)/shard_map/group/pallas_call | solution.py:650
  88.7 2.6 %widen.1 = bf16[256,8192]{1,0:T(8,128)(2,1)} custom-call(bf16[256,768]{1,0:T(8,128)(2,1)} %get-tuple-element.38.refs_0_, bf16[256,4096]{1,0:T(8,128)(2,1)} %get-tuple-element.39.refs_1_), custom_call_target="tpu_custom_call" | custom-call | flops 1 | bytes 4194304 | tf_op jit(solution)/shard_map/widen/pallas_call | solution.py:743
  91.3 1.6 %collective-permute-done.3 = bf16[256,3328]{1,0:T(8,128)(2,1)S(1)} collective-permute-done((bf16[256,3328]{1,0:T(8,128)(2,1)}, bf16[256,3328]{1,0:T(8,128)(2,1)S(1)}, u32[]{:S(2)}, u32[]{:S(2)}) %collective-permute-start.3) | collective-permute-done | bytes 1703968 | tf_op jit(solution)/shard_map/ppermute | solution.py:757
  92.9 1.3 %bitcast_dynamic-update-slice_fusion = bf16[1,256,8192]{2,1,0:T(8,128)(2,1)} fusion(bf16[1,256,8192]{2,1,0:T(8,128)(2,1)} %bitcast.10, bf16[256,3328]{1,0:T(8,128)(2,1)S(1)} %collective-permute-done.3), kind=kLoop, calls=%fused_computation | loop fusion | bytes 3407872 | tf_op jit(solution)/shard_map/dynamic_update_slice | solution.py:785
Async XLA Ops:
  15.7 37.1 %collective-permute-start = (bf16[256,2432]{1,0:T(8,128)(2,1)}, bf16[256,2432]{1,0:T(8,128)(2,1)S(1)}, u32[]{:S(2)}, u32[]{:S(2)}) collective-permute-start(bf16[256,2432]{1,0:T(8,128)(2,1)} %get-tuple-element.29), channel_id=1, source_target_pairs={{0,32},{32,64},{64,96},{96,0},{1,33},{33,65},{65,97},{97,1},{2,34}... | collective-permute-start | bytes 3735560 | tf_op jit(solution)/shard_map/ppermute | solution.py:757
  15.7 37.0 %collective-permute-start.2 = (bf16[256,384]{1,0:T(8,128)(2,1)}, bf16[256,384]{1,0:T(8,128)(2,1)S(1)}, u32[]{:S(2)}, u32[]{:S(2)}) collective-permute-start(bf16[256,384]{1,0:T(8,128)(2,1)} %get-tuple-element.31), channel_id=1, source_target_pairs={{0,32},{32,64},{64,96},{96,0},{1,33},{33,65},{65,97},{97,1},{2,34}... | collective-permute-start | bytes 589832 | tf_op jit(solution)/shard_map/ppermute | solution.py:757
  15.9 36.8 %collective-permute-start.1 = (f32[72,256]{1,0:T(8,128)}, f32[72,256]{1,0:T(8,128)S(1)}, u32[]{:S(2)}, u32[]{:S(2)}) collective-permute-start(f32[72,256]{1,0:T(8,128)} %get-tuple-element.30), channel_id=1, source_target_pairs={{0,32},{32,64},{64,96},{96,0},{1,33},{33,65},{65,97},{97,1},{2,34}... | collective-permute-start | bytes 221192 | tf_op jit(solution)/shard_map/ppermute | solution.py:757
  52.7 2.2 %copy-start.2 = (f32[72,256]{1,0:T(8,128)}, f32[72,256]{1,0:T(8,128)S(1)}, u32[]{:S(2)}) copy-start(f32[72,256]{1,0:T(8,128)S(1)} %collective-permute-done.1.refs_5_) | copy-start | bytes 221188
  52.8 2.2 %copy-start.1 = (bf16[256,384]{1,0:T(8,128)(2,1)}, bf16[256,384]{1,0:T(8,128)(2,1)S(1)}, u32[]{:S(2)}) copy-start(bf16[256,384]{1,0:T(8,128)(2,1)S(1)} %collective-permute-done.2.refs_4_) | copy-start | bytes 589828
  52.8 2.1 %copy-start = (bf16[256,2432]{1,0:T(8,128)(2,1)}, bf16[256,2432]{1,0:T(8,128)(2,1)S(1)}, u32[]{:S(2)}) copy-start(bf16[256,2432]{1,0:T(8,128)(2,1)S(1)} %collective-permute-done.refs_1_) | copy-start | bytes 3735556
  52.8 40.1 %collective-permute-start.3 = (bf16[256,3328]{1,0:T(8,128)(2,1)}, bf16[256,3328]{1,0:T(8,128)(2,1)S(1)}, u32[]{:S(2)}, u32[]{:S(2)}) collective-permute-start(bf16[256,3328]{1,0:T(8,128)(2,1)} %get-tuple-element.40), channel_id=1, source_target_pairs={{0,32},{32,64},{64,96},{96,0},{1,33},{33,65},{65,97},{97,1},{2,34}... | collective-permute-start | bytes 5111816 | tf_op jit(solution)/shard_map/ppermute | solution.py:757

commit v6 on v5

--- a/solution.py
+++ b/solution.py
@@ -27,10 +27,9 @@
 
 HEADS_HOME = 64
 HEADS_BACK = 12
-HEADS_EARLY = 12
-HEADS_ROUND = 14
+HEADS_ROUND = 16
 HEADS_AWAY = HEADS - HEADS_HOME
-HEADS_LATE = HEADS_AWAY - HEADS_EARLY - HEADS_ROUND
+HEADS_AHEAD = HEADS_AWAY - HEADS_ROUND
 
 
 def dot(a, b):
@@ -59,7 +58,6 @@
 
 
 def project_kernel(
-    first,
     x_ref,
     ws_ref,
     wt_ref,
@@ -75,18 +73,14 @@
     step_away_ref,
     vec_ref,
     vec_away_ref,
-    early_ref,
-    late_ref,
-    round_ref,
     x,
     ws,
     wt,
     edge,
     x_sems,
     w_sems,
-    send,
-    recv,
-    late_sem,
+    edge_send,
+    edge_recv,
 ):
     features = x.shape[1]
     away = vec_away_ref.shape[1]
@@ -94,15 +88,10 @@
     me = lax.axis_index("ctx")
     peers = lax.axis_size("ctx")
     after, ahead = lax.rem(me + 1, peers), lax.rem(me + peers - 1, peers)
-    section = lax.axis_index("pipe")
-    sections = lax.axis_size("pipe")
-    behind, beyond = lax.rem(section + sections - 1, sections), lax.rem(section + 1, sections)
 
     barrier = pltpu.get_barrier_semaphore()
     for other in (after, ahead):
         pl.semaphore_signal(barrier, inc=1, device_id={"ctx": other}, device_id_type=MESH)
-    for other in (behind, beyond):
-        pl.semaphore_signal(barrier, inc=1, device_id={"pipe": other}, device_id_type=MESH)
 
     def part(k):
         return slice(k * CHUNK, (k + 1) * CHUNK)
@@ -115,51 +104,21 @@
         )
         for k in range(chunks)
     ]
-    second = first + early_ref.shape[1]
-    third = second + late_ref.shape[1]
-    early_copy = pltpu.make_async_remote_copy(
-        x_ref.at[:, first:second], early_ref, send.at[0], recv.at[0], {"pipe": beyond}, MESH
+    edge_copy = pltpu.make_async_remote_copy(
+        x_ref.at[ROWS - 16 :, :], edge, edge_send, edge_recv, {"ctx": after}, MESH
     )
-    round_copy = pltpu.make_async_remote_copy(
-        x_ref.at[:, third:], round_ref, send.at[1], recv.at[1], {"pipe": behind}, MESH
-    )
-    edge_copy = pltpu.make_async_remote_copy(
-        x_ref.at[ROWS - 16 :, :], edge, send.at[2], recv.at[2], {"ctx": after}, MESH
-    )
-    core = lax.rem(me, 2)
-    half = away // 2
-    mine = pl.ds(pl.multiple_of(core * half, 128), half)
-    vec_copy = pltpu.make_async_remote_copy(
-        vec_ref.at[:, pl.ds(pl.multiple_of(first + core * half, 128), half)],
-        vec_away_ref.at[:, mine],
-        send.at[3],
-        recv.at[3],
-        {"pipe": beyond},
-        MESH,
-    )
-    vec_pair_copy = pltpu.make_async_remote_copy(
-        vec_away_ref.at[:, mine],
-        vec_away_ref.at[:, mine],
-        send.at[4],
-        recv.at[4],
-        {"ctx": me + 1 - 2 * core},
-        MESH,
-    )
-    late_copy = pltpu.make_async_copy(x.at[:, second:third], late_ref, late_sem)
 
     vec_ref[:4, :] = conv_ref[...]
     vec_ref[4:5, :] = gain_ref[...]
     vec_ref[5:6, :] = out_gain_ref[...]
     vec_ref[6:8, :] = jnp.zeros((2, features), F32)
+    vec_away_ref[...] = vec_ref[:, features - away :]
     for load in x_loads:
         load.start()
     for pair in w_loads:
         for load in pair:
             load.start()
-    pl.semaphore_wait(barrier, 4)
-    vec_copy.start()
-    early_copy.start()
-    round_copy.start()
+    pl.semaphore_wait(barrier, 2)
     edge_copy.start()
 
     total = jnp.zeros((ROWS, 128), F32)
@@ -169,11 +128,7 @@
             square = x[:, i : i + 512].astype(F32)
             square = square * square
             total = total + (square[:, :128] + square[:, 128:256]) + (square[:, 256:384] + square[:, 384:])
-    late_copy.start()
     scale = lax.rsqrt(jnp.sum(total, axis=-1, keepdims=True) * (1.0 / features) + epsilon)
-
-    vec_copy.wait()
-    vec_pair_copy.start()
 
     maps = jnp.zeros((ROWS, 2 * STATE), F32)
     step = jnp.zeros((ROWS, HEADS), F32)
@@ -204,23 +159,18 @@
         ref[:, 2 * STATE :] = jnp.concatenate(
             [rows[:, start + i * 128 : start + (i + 1) * 128] for i in range(ROWS // HALO)], axis=0
         ).astype(BF16)
-    late_copy.wait()
-    vec_pair_copy.wait()
-    early_copy.wait()
-    round_copy.wait()
-
-
-def project(x, proj_state, proj_step, gain, conv, out_gain, bias, rate, skip, widths, collective_id):
+
+
+def project(x, proj_state, proj_step, gain, conv, out_gain, bias, rate, skip, away, collective_id):
     features = x.shape[1]
-    away = sum(widths)
     chunks = features // CHUNK
     any_ = pl.BlockSpec(memory_space=pl.ANY)
     vmem = pl.BlockSpec(memory_space=pltpu.VMEM)
     dma = pltpu.SemaphoreType.DMA
     return pl.pallas_call(
-        functools.partial(project_kernel, features - away),
+        project_kernel,
         in_specs=[any_] * 3 + [vmem] * 6,
-        out_specs=[vmem] * 5 + [any_] * 4,
+        out_specs=[vmem] * 6,
         out_shape=[
             jax.ShapeDtypeStruct((ROWS, 2 * STATE + 128), BF16),
             jax.ShapeDtypeStruct((ROWS, 2 * STATE + 128), BF16),
@@ -228,8 +178,7 @@
             jax.ShapeDtypeStruct((away // HEAD + 8, ROWS), F32),
             jax.ShapeDtypeStruct((8, features), F32),
             jax.ShapeDtypeStruct((8, away), F32),
-        ]
-        + [jax.ShapeDtypeStruct((ROWS, columns), BF16) for columns in widths],
+        ],
         scratch_shapes=[
             pltpu.VMEM(x.shape, BF16),
             pltpu.VMEM(proj_state.shape, BF16),
@@ -237,8 +186,7 @@
             pltpu.VMEM((16, features), BF16),
             dma((chunks,)),
             dma((2 * chunks,)),
-            dma((5,)),
-            dma((5,)),
+            dma,
             dma,
         ],
         compiler_params=pltpu.CompilerParams(
@@ -613,9 +561,9 @@
     run(within_tile, batch_tiles, batch_tiles + half_tiles)
     scan_states(1)
     send_back(1)
+    run(within_tile, batch_tiles + half_tiles, 2 * batch_tiles)
     if hops == 3:
         pass_on(2)
-    run(within_tile, batch_tiles + half_tiles, 2 * batch_tiles)
     take_back(0)
     finish_half(0, core, mine)
     back_pair_copy(0).wait()
@@ -763,22 +711,26 @@
     x = incoming[0]
     features = x.shape[1]
     home, back, away = HEADS_HOME * HEAD, HEADS_BACK * HEAD, HEADS_AWAY * HEAD
-    early, late, round_ = HEADS_EARLY * HEAD, HEADS_LATE * HEAD, HEADS_ROUND * HEAD
-
-    maps, maps_away, step, step_away, vec, vec_away, x_early, x_late, x_round = project(
+    ahead, round_ = HEADS_AHEAD * HEAD, HEADS_ROUND * HEAD
+
+    x_ahead = moved(x[:, home : home + ahead], 1)
+    x_round = moved(x[:, features - round_ :], -1)
+    maps, maps_away, step, step_away, vec, vec_away = project(
         x, proj_state[0], proj_step[0], norm_gain, conv_weight[0], out_gain, step_bias, decay_rate, skip_gain,
-        (early, late, round_), 2,
+        away, 2,
     )
-    x_late, step_away, maps_away = (moved(a, 1) for a in (x_late, step_away, maps_away))
+    step_away, maps_away, vec_away = moved(step_away, 1), moved(maps_away, 1), moved(vec_away, 1)
 
     rows, rows_back, x_round = group(
         (home,), (x,), vec, maps, step, x_round, 2, (home - back, back), 0
     )
-    rows, x_late, step_away, maps_away = lax.optimization_barrier((rows, x_late, step_away, maps_away))
+    rows, x_ahead, step_away, maps_away, vec_away = lax.optimization_barrier(
+        (rows, x_ahead, step_away, maps_away, vec_away)
+    )
     rows_in = moved(rows, 1)
 
     rows_away, rows_back = group(
-        (early, late, round_), (x_early, x_late, x_round), vec_away, maps_away, step_away,
+        (ahead, round_), (x_ahead, x_round), vec_away, maps_away, step_away,
         rows_back, 3, (away,), 1,
     )
     passed = widen((rows_back, rows_away), features)

time: 95.4 us -> 94.7 us (level)
  Pallas kernels: 87.6 us -> 78.7 us
  local copies, waits for them, and re-layouts: 1.31 us -> 4.86 us
  starting transfers between devices: 3.59 us -> 6.67 us
  waiting for transfers between devices: 1.63 us -> 4.02 us
    pallas_call x1, Pallas kernels: 15.6 us -> 10 us  [project(): pl.pallas_call(project_kernel, in_specs=[any_] * 3 + [vmem] * 6, out_spec...]
    pallas_call x2, Pallas kernels: 69.4 us -> 66.1 us  [group(): pl.pallas_call(functools.partial(group_kernel, pieces, hops, outs), out_s...]
    ppermute x4 -> x6, starting transfers between devices: 3.59 us -> 6.67 us  [moved(): lax.ppermute(array, 'pipe', [(i, (i + by) % peers) for i in range(peers)])]
    slice x0 -> x2, local copies, waits for them, and re-layouts: none -> 2.58 us  [the longest x1 1.51 us: shards(): x_ahead = moved(x[:, home:home + ahead], 1)]
    ppermute x4 -> x6, waiting for transfers between devices: 1.63 us -> 4.02 us  [moved(): lax.ppermute(array, 'pipe', [(i, (i + by) % peers) for i in range(peers)])]
    unnamed x6 -> x10, local copies, waits for them, and re-layouts: 0.01 us -> 0.98 us
  transfers between devices with their start and end apart: 4 -> 6, of which waited for: 1 -> 1; matrix products, arithmetic and copies ran while one was open for 0% -> 1% of each run, Pallas kernels for 76% -> 83%
where the time goes in v6:
time: 94.7 us; the launch traced here: 94.4 us
  Pallas kernels  78.7 us (83%)
  starting transfers between devices  6.67 us (7%)
  local copies, waits for them, and re-layouts  4.86 us (5%)
  waiting for transfers between devices  4.02 us (4%)
    pallas_call x2, Pallas kernels, group(): pl.pallas_call(functools.partial(group_kernel, pieces, hops, outs), out_s...  66.1 us
    pallas_call x1, Pallas kernels, project(): pl.pallas_call(project_kernel, in_specs=[any_] * 3 + [vmem] * 6, out_spec...  10 us
    ppermute x6, starting transfers between devices, moved(): lax.ppermute(array, 'pipe', [(i, (i + by) % peers) for i in range(peers)])  6.67 us
    ppermute x6, waiting for transfers between devices, moved(): lax.ppermute(array, 'pipe', [(i, (i + by) % peers) for i in range(peers)])  4.02 us
    pallas_call x1, Pallas kernels, widen(): pl.pallas_call(functools.partial(widen_kernel, blocks), in_specs=[pl.Bloc...  2.56 us
  transfers between devices with their start and end apart: 6, of which 1 were waited for; matrix products, arithmetic and copies ran while one was open for 1% of the time, Pallas kernels for 83%

profile of v6, /device:TPU:1, one launch (start us, length us, event | category | flops | bytes accessed | tf_op | source)
XLA Modules:
  0.0 94.4 jit_solution(11321302367655110626)
XLA Ops:
  0.0 1.5 %slice.9 = bf16[256,3072]{1,0:T(8,128)(2,1)S(1)} slice(bf16[256,8192]{1,0:T(8,128)(2,1)} %bitcast.7), slice={[0:256], [4096:7168]} | slice | bytes 3145728 | tf_op jit(solution)/shard_map/slice | solution.py:716
  1.5 2.1 %collective-permute-start.1 = (bf16[256,3072]{1,0:T(8,128)(2,1)S(1)}, bf16[256,3072]{1,0:T(8,128)(2,1)S(1)}, u32[]{:S(2)}, u32[]{:S(2)}) collective-permute-start(bf16[256,3072]{1,0:T(8,128)(2,1)S(1)} %slice.9), channel_id=1, source_target_pairs={{0,32},{32,64},{64,96},{96,0},{1,33},{33,65},{65,97},{97,1},{2,34}... | collective-permute-start | bytes 4718600 | tf_op jit(solution)/shard_map/ppermute | solution.py:705
  3.6 1.1 %slice.8 = bf16[256,1024]{1,0:T(8,128)(2,1)S(1)} slice(bf16[256,8192]{1,0:T(8,128)(2,1)} %bitcast.8), slice={[0:256], [7168:8192]} | slice | bytes 1048576 | tf_op jit(solution)/shard_map/slice | solution.py:717
  4.7 1.4 %collective-permute-start = (bf16[256,1024]{1,0:T(8,128)(2,1)S(1)}, bf16[256,1024]{1,0:T(8,128)(2,1)S(1)}, u32[]{:S(2)}, u32[]{:S(2)}) collective-permute-start(bf16[256,1024]{1,0:T(8,128)(2,1)S(1)} %slice.8), channel_id=1, source_target_pairs={{0,96},{32,0},{64,32},{96,64},{1,97},{33,1},{65,33},{97,65},{2,98}... | collective-permute-start | bytes 1572872 | tf_op jit(solution)/shard_map/ppermute | solution.py:705
  6.1 10.0 %project.1 = (bf16[256,384]{1,0:T(8,128)(2,1)}, bf16[256,384]{1,0:T(8,128)(2,1)}, f32[72,256]{1,0:T(8,128)}, f32[72,256]{1,0:T(8,128)}, f32[8,8192]{1,0:T(8,128)}, /*index=5*/f32[8,4096]{1,0:T(8,128)}) custom-call(bf16[256,8192]{1,0:T(8,128)(2,1)} %bitcast.9, bf16[8192,256]{1,0:T(8,128)(2,1)} %bitcast.11, bf16[8192,128]{1,0:T(8,128)(2,1)} %bitcast.13, ...), custom_call_target="tpu_custom_call" | custom-call | flops 1610612736 | bytes 37748736 | tf_op jit(solution)/shard_map/project/pallas_call | solution.py:170
  16.1 0.1 collective-permute-start.3
  16.2 1.2 %collective-permute-start.4 = (f32[8,4096]{1,0:T(8,128)}, f32[8,4096]{1,0:T(8,128)S(1)}, u32[]{:S(2)}, u32[]{:S(2)}) collective-permute-start(f32[8,4096]{1,0:T(8,128)} %get-tuple-element.27), channel_id=1, source_target_pairs={{0,32},{32,64},{64,96},{96,0},{1,33},{33,65},{65,97},{97,1},{2,34}... | collective-permute-start | bytes 393224 | tf_op jit(solution)/shard_map/ppermute | solution.py:705
  17.4 0.9 collective-permute-start.2
  18.3 0.0 collective-permute-done.refs_4_
  18.3 0.0 copy-start.1
  18.3 0.8 copy-done.1
  19.1 33.8 %group.2 = (bf16[256,3328]{1,0:T(8,128)(2,1)}, bf16[256,768]{1,0:T(8,128)(2,1)}, bf16[256,1024]{1,0:T(8,128)(2,1)}) custom-call(bf16[256,8192]{1,0:T(8,128)(2,1)} %bitcast.10, f32[8,8192]{1,0:T(8,128)} %get-tuple-element.21.refs_1_, bf16[256,384]{1,0:T(8,128)(2,1)} %get-tuple-element.22.refs_2_, f32[72,256]{1,0:T(8,128)} %get-tuple-element.23.refs_3_, ...), custom_call_target="tpu_custom_call" | custom-call | flops 1048576 | bytes 1048576 | tf_op jit(solution)/shard_map/group/pallas_call | solution.py:598
  52.8 0.0 collective-permute-done.2.refs_4_
  52.9 0.0 copy-start.4
  52.9 0.0 collective-permute-done.4.refs_2_
  52.9 0.0 copy-start.3
  52.9 0.0 collective-permute-done.3.refs_3_
  52.9 0.0 copy-start.2
  52.9 0.0 collective-permute-done.1.refs_0_
  52.9 0.0 copy-start
  52.9 1.0 %collective-permute-start.5 = (bf16[256,3328]{1,0:T(8,128)(2,1)}, bf16[256,3328]{1,0:T(8,128)(2,1)S(1)}, u32[]{:S(2)}, u32[]{:S(2)}) collective-permute-start(bf16[256,3328]{1,0:T(8,128)(2,1)} %get-tuple-element.36), channel_id=1, source_target_pairs={{0,32},{32,64},{64,96},{96,0},{1,33},{33,65},{65,97},{97,1},{2,34}... | collective-permute-start | bytes 5111816 | tf_op jit(solution)/shard_map/ppermute | solution.py:705
  54.0 0.0 copy-done.4
  54.0 0.0 copy-done.3
  54.0 0.0 copy-done.2
  54.0 0.2 copy-done
  54.1 32.4 %group.3 = (bf16[256,4096]{1,0:T(8,128)(2,1)}, bf16[256,768]{1,0:T(8,128)(2,1)}) custom-call(bf16[256,3072]{1,0:T(8,128)(2,1)} %copy-done, bf16[256,1024]{1,0:T(8,128)(2,1)} %get-tuple-element.29.refs_1_, f32[8,4096]{1,0:T(8,128)} %copy-done.3, bf16[256,384]{1,0:T(8,128)(2,1)} %copy-done.2, f32[72,256]{1,0:T(8,128)} %copy-done.4, ...), custom_call_target="tpu_custom_call" | custom-call | flops 1048576 | bytes 1048576 | tf_op jit(solution)/shard_map/group/pallas_call | solution.py:598
  86.5 2.6 %widen.1 = bf16[256,8192]{1,0:T(8,128)(2,1)} custom-call(bf16[256,768]{1,0:T(8,128)(2,1)} %get-tuple-element.34.refs_0_, bf16[256,4096]{1,0:T(8,128)(2,1)} %get-tuple-element.35.refs_1_), custom_call_target="tpu_custom_call" | custom-call | flops 1 | bytes 4194304 | tf_op jit(solution)/shard_map/widen/pallas_call | solution.py:691
  89.1 4.0 %collective-permute-done.5 = bf16[256,3328]{1,0:T(8,128)(2,1)S(1)} collective-permute-done((bf16[256,3328]{1,0:T(8,128)(2,1)}, bf16[256,3328]{1,0:T(8,128)(2,1)S(1)}, u32[]{:S(2)}, u32[]{:S(2)}) %collective-permute-start.5) | collective-permute-done | bytes 1703968 | tf_op jit(solution)/shard_map/ppermute | solution.py:705
  93.1 1.3 %bitcast_dynamic-update-slice_fusion = bf16[1,256,8192]{2,1,0:T(8,128)(2,1)} fusion(bf16[1,256,8192]{2,1,0:T(8,128)(2,1)} %bitcast.12, bf16[256,3328]{1,0:T(8,128)(2,1)S(1)} %collective-permute-done.5), kind=kLoop, calls=%fused_computation | loop fusion | bytes 3407872 | tf_op jit(solution)/shard_map/dynamic_update_slice | solution.py:737
Async XLA Ops:
  1.5 51.4 %collective-permute-start.1 = (bf16[256,3072]{1,0:T(8,128)(2,1)S(1)}, bf16[256,3072]{1,0:T(8,128)(2,1)S(1)}, u32[]{:S(2)}, u32[]{:S(2)}) collective-permute-start(bf16[256,3072]{1,0:T(8,128)(2,1)S(1)} %slice.9), channel_id=1, source_target_pairs={{0,32},{32,64},{64,96},{96,0},{1,33},{33,65},{65,97},{97,1},{2,34}... | collective-permute-start | bytes 4718600 | tf_op jit(solution)/shard_map/ppermute | solution.py:705
  4.7 13.6 %collective-permute-start = (bf16[256,1024]{1,0:T(8,128)(2,1)S(1)}, bf16[256,1024]{1,0:T(8,128)(2,1)S(1)}, u32[]{:S(2)}, u32[]{:S(2)}) collective-permute-start(bf16[256,1024]{1,0:T(8,128)(2,1)S(1)} %slice.8), channel_id=1, source_target_pairs={{0,96},{32,0},{64,32},{96,64},{1,97},{33,1},{65,33},{97,65},{2,98}... | collective-permute-start | bytes 1572872 | tf_op jit(solution)/shard_map/ppermute | solution.py:705
  16.1 36.8 %collective-permute-start.3 = (bf16[256,384]{1,0:T(8,128)(2,1)}, bf16[256,384]{1,0:T(8,128)(2,1)S(1)}, u32[]{:S(2)}, u32[]{:S(2)}) collective-permute-start(bf16[256,384]{1,0:T(8,128)(2,1)} %get-tuple-element.26), channel_id=1, source_target_pairs={{0,32},{32,64},{64,96},{96,0},{1,33},{33,65},{65,97},{97,1},{2,34}... | collective-permute-start | bytes 589832 | tf_op jit(solution)/shard_map/ppermute | solution.py:705
  16.2 36.7 %collective-permute-start.4 = (f32[8,4096]{1,0:T(8,128)}, f32[8,4096]{1,0:T(8,128)S(1)}, u32[]{:S(2)}, u32[]{:S(2)}) collective-permute-start(f32[8,4096]{1,0:T(8,128)} %get-tuple-element.27), channel_id=1, source_target_pairs={{0,32},{32,64},{64,96},{96,0},{1,33},{33,65},{65,97},{97,1},{2,34}... | collective-permute-start | bytes 393224 | tf_op jit(solution)/shard_map/ppermute | solution.py:705
  17.4 35.5 %collective-permute-start.2 = (f32[72,256]{1,0:T(8,128)}, f32[72,256]{1,0:T(8,128)S(1)}, u32[]{:S(2)}, u32[]{:S(2)}) collective-permute-start(f32[72,256]{1,0:T(8,128)} %get-tuple-element.25), channel_id=1, source_target_pairs={{0,32},{32,64},{64,96},{96,0},{1,33},{33,65},{65,97},{97,1},{2,34}... | collective-permute-start | bytes 221192 | tf_op jit(solution)/shard_map/ppermute | solution.py:705
  18.3 0.8 copy-start.1
  52.9 1.1 %copy-start.4 = (f32[72,256]{1,0:T(8,128)}, f32[72,256]{1,0:T(8,128)S(1)}, u32[]{:S(2)}) copy-start(f32[72,256]{1,0:T(8,128)S(1)} %collective-permute-done.2.refs_4_) | copy-start | bytes 221188
  52.9 1.1 %copy-start.3 = (f32[8,4096]{1,0:T(8,128)}, f32[8,4096]{1,0:T(8,128)S(1)}, u32[]{:S(2)}) copy-start(f32[8,4096]{1,0:T(8,128)S(1)} %collective-permute-done.4.refs_2_) | copy-start | bytes 393220
  52.9 1.1 %copy-start.2 = (bf16[256,384]{1,0:T(8,128)(2,1)}, bf16[256,384]{1,0:T(8,128)(2,1)S(1)}, u32[]{:S(2)}) copy-start(bf16[256,384]{1,0:T(8,128)(2,1)S(1)} %collective-permute-done.3.refs_3_) | copy-start | bytes 589828
  52.9 1.2 %copy-start = (bf16[256,3072]{1,0:T(8,128)(2,1)}, bf16[256,3072]{1,0:T(8,128)(2,1)S(1)}, u32[]{:S(2)}) copy-start(bf16[256,3072]{1,0:T(8,128)(2,1)S(1)} %collective-permute-done.1.refs_0_) | copy-start | bytes 4718596
  52.9 40.1 %collective-permute-start.5 = (bf16[256,3328]{1,0:T(8,128)(2,1)}, bf16[256,3328]{1,0:T(8,128)(2,1)S(1)}, u32[]{:S(2)}, u32[]{:S(2)}) collective-permute-start(bf16[256,3328]{1,0:T(8,128)(2,1)} %get-tuple-element.36), channel_id=1, source_target_pairs={{0,32},{32,64},{64,96},{96,0},{1,33},{33,65},{65,97},{97,1},{2,34}... | collective-permute-start | bytes 5111816 | tf_op jit(solution)/shard_map/ppermute | solution.py:705

commit v7 on v6

--- a/solution.py
+++ b/solution.py
@@ -600,13 +600,15 @@
         out_shape=[jax.ShapeDtypeStruct((ROWS, columns), BF16) for columns in outs]
         + [jax.ShapeDtypeStruct(array.shape, array.dtype) for array in (relay,)],
         grid=(1,),
-        in_specs=[pl.BlockSpec(memory_space=pl.ANY)] * len(pieces)
+        in_specs=[
+            pl.BlockSpec(memory_space=vmem if x.shape[1] == columns else pl.ANY) for x, columns in zip(xs, pieces)
+        ]
         + [
             pl.BlockSpec((vec.shape[0], features), corner),
             pl.BlockSpec(maps.shape, corner),
             pl.BlockSpec((heads + 8, ROWS), corner),
         ]
-        + [pl.BlockSpec(memory_space=pl.ANY)] ,
+        + [pl.BlockSpec(memory_space=vmem if hops == 2 else pl.ANY)] ,
         out_specs=[pl.BlockSpec(memory_space=pl.ANY)] * (len(outs) + 1),
         scratch_shapes=[
             vmem((hops,) + relay.shape, BF16),

time: 94.7 us -> 94.7 us (level)
  transfers between devices with their start and end apart: 6 -> 6, of which waited for: 1 -> 1; matrix products, arithmetic and copies ran while one was open for 1% -> 1% of each run, Pallas kernels for 83% -> 84%
where the time goes in v7:
time: 94.7 us; the launch traced here: 94.4 us
  Pallas kernels  79.5 us (84%)
  starting transfers between devices  6.87 us (7%)
  local copies, waits for them, and re-layouts  4.69 us (5%)
  waiting for transfers between devices  3.18 us (3%)
    pallas_call x2, Pallas kernels, group(): pl.pallas_call(functools.partial(group_kernel, pieces, hops, outs), out_s...  66.9 us
    pallas_call x1, Pallas kernels, project(): pl.pallas_call(project_kernel, in_specs=[any_] * 3 + [vmem] * 6, out_spec...  10 us
    ppermute x6, starting transfers between devices, moved(): lax.ppermute(array, 'pipe', [(i, (i + by) % peers) for i in range(peers)])  6.87 us
    ppermute x6, waiting for transfers between devices, moved(): lax.ppermute(array, 'pipe', [(i, (i + by) % peers) for i in range(peers)])  3.18 us
    pallas_call x1, Pallas kernels, widen(): pl.pallas_call(functools.partial(widen_kernel, blocks), in_specs=[pl.Bloc...  2.56 us
  transfers between devices with their start and end apart: 6, of which 1 were waited for; matrix products, arithmetic and copies ran while one was open for 1% of the time, Pallas kernels for 84%

profile of v7, /device:TPU:1, one launch (start us, length us, event | category | flops | bytes accessed | tf_op | source)
XLA Modules:
  0.0 94.4 jit_solution(13440718518033473389)
XLA Ops:
  0.0 1.5 %slice.9 = bf16[256,3072]{1,0:T(8,128)(2,1)S(1)} slice(bf16[256,8192]{1,0:T(8,128)(2,1)} %bitcast.7), slice={[0:256], [4096:7168]} | slice | bytes 3145728 | tf_op jit(solution)/shard_map/slice | solution.py:718
  1.5 2.1 %collective-permute-start.1 = (bf16[256,3072]{1,0:T(8,128)(2,1)S(1)}, bf16[256,3072]{1,0:T(8,128)(2,1)S(1)}, u32[]{:S(2)}, u32[]{:S(2)}) collective-permute-start(bf16[256,3072]{1,0:T(8,128)(2,1)S(1)} %slice.9), channel_id=1, source_target_pairs={{0,32},{32,64},{64,96},{96,0},{1,33},{33,65},{65,97},{97,1},{2,34}... | collective-permute-start | bytes 4718600 | tf_op jit(solution)/shard_map/ppermute | solution.py:707
  3.6 1.1 %slice.8 = bf16[256,1024]{1,0:T(8,128)(2,1)S(1)} slice(bf16[256,8192]{1,0:T(8,128)(2,1)} %bitcast.8), slice={[0:256], [7168:8192]} | slice | bytes 1048576 | tf_op jit(solution)/shard_map/slice | solution.py:719
  4.7 1.4 %collective-permute-start = (bf16[256,1024]{1,0:T(8,128)(2,1)S(1)}, bf16[256,1024]{1,0:T(8,128)(2,1)S(1)}, u32[]{:S(2)}, u32[]{:S(2)}) collective-permute-start(bf16[256,1024]{1,0:T(8,128)(2,1)S(1)} %slice.8), channel_id=1, source_target_pairs={{0,96},{32,0},{64,32},{96,64},{1,97},{33,1},{65,33},{97,65},{2,98}... | collective-permute-start | bytes 1572872 | tf_op jit(solution)/shard_map/ppermute | solution.py:707
  6.1 10.0 %project.1 = (bf16[256,384]{1,0:T(8,128)(2,1)}, bf16[256,384]{1,0:T(8,128)(2,1)}, f32[72,256]{1,0:T(8,128)}, f32[72,256]{1,0:T(8,128)}, f32[8,8192]{1,0:T(8,128)}, /*index=5*/f32[8,4096]{1,0:T(8,128)}) custom-call(bf16[256,8192]{1,0:T(8,128)(2,1)} %bitcast.9, bf16[8192,256]{1,0:T(8,128)(2,1)} %bitcast.11, bf16[8192,128]{1,0:T(8,128)(2,1)} %bitcast.13, ...), custom_call_target="tpu_custom_call" | custom-call | flops 1610612736 | bytes 37748736 | tf_op jit(solution)/shard_map/project/pallas_call | solution.py:170
  16.1 0.1 collective-permute-start.3
  16.2 1.2 %collective-permute-start.4 = (f32[8,4096]{1,0:T(8,128)}, f32[8,4096]{1,0:T(8,128)S(1)}, u32[]{:S(2)}, u32[]{:S(2)}) collective-permute-start(f32[8,4096]{1,0:T(8,128)} %get-tuple-element.27), channel_id=1, source_target_pairs={{0,32},{32,64},{64,96},{96,0},{1,33},{33,65},{65,97},{97,1},{2,34}... | collective-permute-start | bytes 393224 | tf_op jit(solution)/shard_map/ppermute | solution.py:707
  17.4 0.9 collective-permute-start.2
  18.3 0.0 collective-permute-done.refs_4_
  18.3 0.0 copy-start.1
  18.3 0.8 copy-done.1
  19.1 33.8 %group.2 = (bf16[256,3328]{1,0:T(8,128)(2,1)}, bf16[256,768]{1,0:T(8,128)(2,1)}, bf16[256,1024]{1,0:T(8,128)(2,1)}) custom-call(bf16[256,8192]{1,0:T(8,128)(2,1)} %bitcast.10, f32[8,8192]{1,0:T(8,128)} %get-tuple-element.21.refs_1_, bf16[256,384]{1,0:T(8,128)(2,1)} %get-tuple-element.22.refs_2_, f32[72,256]{1,0:T(8,128)} %get-tuple-element.23.refs_3_, ...), custom_call_target="tpu_custom_call" | custom-call | flops 1048576 | bytes 1048576 | tf_op jit(solution)/shard_map/group/pallas_call | solution.py:598
  52.8 0.0 collective-permute-done.2.refs_4_
  52.9 0.0 copy-start.4
  52.9 0.0 collective-permute-done.4.refs_2_
  52.9 0.0 copy-start.3
  52.9 0.0 collective-permute-done.3.refs_3_
  52.9 0.0 copy-start.2
  52.9 0.0 collective-permute-done.1.refs_0_
  52.9 0.0 copy-start
  52.9 1.2 %collective-permute-start.5 = (bf16[256,3328]{1,0:T(8,128)(2,1)}, bf16[256,3328]{1,0:T(8,128)(2,1)S(1)}, u32[]{:S(2)}, u32[]{:S(2)}) collective-permute-start(bf16[256,3328]{1,0:T(8,128)(2,1)} %get-tuple-element.36), channel_id=1, source_target_pairs={{0,32},{32,64},{64,96},{96,0},{1,33},{33,65},{65,97},{97,1},{2,34}... | collective-permute-start | bytes 5111816 | tf_op jit(solution)/shard_map/ppermute | solution.py:707
  54.2 0.0 copy-done.4
  54.2 0.0 copy-done.3
  54.2 0.0 copy-done.2
  54.2 0.0 copy-done
  54.2 33.2 %group.3 = (bf16[256,4096]{1,0:T(8,128)(2,1)}, bf16[256,768]{1,0:T(8,128)(2,1)}) custom-call(bf16[256,3072]{1,0:T(8,128)(2,1)} %copy-done, bf16[256,1024]{1,0:T(8,128)(2,1)} %get-tuple-element.29.refs_1_, f32[8,4096]{1,0:T(8,128)} %copy-done.3, bf16[256,384]{1,0:T(8,128)(2,1)} %copy-done.2, f32[72,256]{1,0:T(8,128)} %copy-done.4, ...), custom_call_target="tpu_custom_call" | custom-call | flops 1048576 | bytes 1048576 | tf_op jit(solution)/shard_map/group/pallas_call | solution.py:598
  87.3 2.6 %widen.1 = bf16[256,8192]{1,0:T(8,128)(2,1)} custom-call(bf16[256,768]{1,0:T(8,128)(2,1)} %get-tuple-element.34.refs_0_, bf16[256,4096]{1,0:T(8,128)(2,1)} %get-tuple-element.35.refs_1_), custom_call_target="tpu_custom_call" | custom-call | flops 1 | bytes 4194304 | tf_op jit(solution)/shard_map/widen/pallas_call | solution.py:693
  89.9 3.2 %collective-permute-done.5 = bf16[256,3328]{1,0:T(8,128)(2,1)S(1)} collective-permute-done((bf16[256,3328]{1,0:T(8,128)(2,1)}, bf16[256,3328]{1,0:T(8,128)(2,1)S(1)}, u32[]{:S(2)}, u32[]{:S(2)}) %collective-permute-start.5) | collective-permute-done | bytes 1703968 | tf_op jit(solution)/shard_map/ppermute | solution.py:707
  93.1 1.3 %bitcast_dynamic-update-slice_fusion = bf16[1,256,8192]{2,1,0:T(8,128)(2,1)} fusion(bf16[1,256,8192]{2,1,0:T(8,128)(2,1)} %bitcast.12, bf16[256,3328]{1,0:T(8,128)(2,1)S(1)} %collective-permute-done.5), kind=kLoop, calls=%fused_computation | loop fusion | bytes 3407872 | tf_op jit(solution)/shard_map/dynamic_update_slice | solution.py:739
Async XLA Ops:
  1.5 51.4 %collective-permute-start.1 = (bf16[256,3072]{1,0:T(8,128)(2,1)S(1)}, bf16[256,3072]{1,0:T(8,128)(2,1)S(1)}, u32[]{:S(2)}, u32[]{:S(2)}) collective-permute-start(bf16[256,3072]{1,0:T(8,128)(2,1)S(1)} %slice.9), channel_id=1, source_target_pairs={{0,32},{32,64},{64,96},{96,0},{1,33},{33,65},{65,97},{97,1},{2,34}... | collective-permute-start | bytes 4718600 | tf_op jit(solution)/shard_map/ppermute | solution.py:707
  4.7 13.6 %collective-permute-start = (bf16[256,1024]{1,0:T(8,128)(2,1)S(1)}, bf16[256,1024]{1,0:T(8,128)(2,1)S(1)}, u32[]{:S(2)}, u32[]{:S(2)}) collective-permute-start(bf16[256,1024]{1,0:T(8,128)(2,1)S(1)} %slice.8), channel_id=1, source_target_pairs={{0,96},{32,0},{64,32},{96,64},{1,97},{33,1},{65,33},{97,65},{2,98}... | collective-permute-start | bytes 1572872 | tf_op jit(solution)/shard_map/ppermute | solution.py:707
  16.1 36.8 %collective-permute-start.3 = (bf16[256,384]{1,0:T(8,128)(2,1)}, bf16[256,384]{1,0:T(8,128)(2,1)S(1)}, u32[]{:S(2)}, u32[]{:S(2)}) collective-permute-start(bf16[256,384]{1,0:T(8,128)(2,1)} %get-tuple-element.26), channel_id=1, source_target_pairs={{0,32},{32,64},{64,96},{96,0},{1,33},{33,65},{65,97},{97,1},{2,34}... | collective-permute-start | bytes 589832 | tf_op jit(solution)/shard_map/ppermute | solution.py:707
  16.2 36.7 %collective-permute-start.4 = (f32[8,4096]{1,0:T(8,128)}, f32[8,4096]{1,0:T(8,128)S(1)}, u32[]{:S(2)}, u32[]{:S(2)}) collective-permute-start(f32[8,4096]{1,0:T(8,128)} %get-tuple-element.27), channel_id=1, source_target_pairs={{0,32},{32,64},{64,96},{96,0},{1,33},{33,65},{65,97},{97,1},{2,34}... | collective-permute-start | bytes 393224 | tf_op jit(solution)/shard_map/ppermute | solution.py:707
  17.4 35.5 %collective-permute-start.2 = (f32[72,256]{1,0:T(8,128)}, f32[72,256]{1,0:T(8,128)S(1)}, u32[]{:S(2)}, u32[]{:S(2)}) collective-permute-start(f32[72,256]{1,0:T(8,128)} %get-tuple-element.25), channel_id=1, source_target_pairs={{0,32},{32,64},{64,96},{96,0},{1,33},{33,65},{65,97},{97,1},{2,34}... | collective-permute-start | bytes 221192 | tf_op jit(solution)/shard_map/ppermute | solution.py:707
  18.3 0.8 copy-start.1
  52.9 1.3 %copy-start.4 = (f32[72,256]{1,0:T(8,128)}, f32[72,256]{1,0:T(8,128)S(1)}, u32[]{:S(2)}) copy-start(f32[72,256]{1,0:T(8,128)S(1)} %collective-permute-done.2.refs_4_) | copy-start | bytes 221188
  52.9 1.3 %copy-start.3 = (f32[8,4096]{1,0:T(8,128)}, f32[8,4096]{1,0:T(8,128)S(1)}, u32[]{:S(2)}) copy-start(f32[8,4096]{1,0:T(8,128)S(1)} %collective-permute-done.4.refs_2_) | copy-start | bytes 393220
  52.9 1.3 %copy-start.2 = (bf16[256,384]{1,0:T(8,128)(2,1)}, bf16[256,384]{1,0:T(8,128)(2,1)S(1)}, u32[]{:S(2)}) copy-start(bf16[256,384]{1,0:T(8,128)(2,1)S(1)} %collective-permute-done.3.refs_3_) | copy-start | bytes 589828
  52.9 1.2 %copy-start = (bf16[256,3072]{1,0:T(8,128)(2,1)}, bf16[256,3072]{1,0:T(8,128)(2,1)S(1)}, u32[]{:S(2)}) copy-start(bf16[256,3072]{1,0:T(8,128)(2,1)S(1)} %collective-permute-done.1.refs_0_) | copy-start | bytes 4718596
  52.9 40.1 %collective-permute-start.5 = (bf16[256,3328]{1,0:T(8,128)(2,1)}, bf16[256,3328]{1,0:T(8,128)(2,1)S(1)}, u32[]{:S(2)}, u32[]{:S(2)}) collective-permute-start(bf16[256,3328]{1,0:T(8,128)(2,1)} %get-tuple-element.36), channel_id=1, source_target_pairs={{0,32},{32,64},{64,96},{96,0},{1,33},{33,65},{65,97},{97,1},{2,34}... | collective-permute-start | bytes 5111816 | tf_op jit(solution)/shard_map/ppermute | solution.py:707
